TPU v7x, 32 devices: a whole 2x2x4 slice. The times are simulated.
32 devices in a mesh: seq: 16 (over z, y, x), head: 2 (over core).
Axes of the slice: x: 2, y: 2, z: 4, core: 2. Of those that a mesh axis runs over, the one named last changes fastest.
Arguments:
- query_rows: bfloat16 [16384, 2048], P('seq', 'head'), may hold values from -6 to 6
- key_rows: bfloat16 [16384, 2048], P('seq', 'head'), may hold values from -6 to 6
- value_rows: bfloat16 [16384, 2048], P('seq', 'head'), may hold values from -6 to 6
- head_scale: float32 [16], P('head'), may hold values from 0.25 to 4
- out_gain: float32 [2048], P('head'), may hold values from 0.5 to 1.5
Outputs:
- attended: bfloat16 [16384, 2048], P('seq', 'head')
All inputs are finite; a program needn't handle non-finite values.
Results may differ from a plain program's by a relative error of at most 0.001.
Values sent between devices are 32-bit elements; how exact they have to be, the bound alone decides.
No kernel may reach another device: no remote copies, remote signals or barrier semaphores. Data moves between devices by JAX's collectives and lax.ppermute only.
A program may use at most 320 MiB of HBM per device.

v0:
```python
import jax
import jax.numpy as jnp
from jax import lax
from jax.sharding import PartitionSpec as P

BLK = 128


epsilon = 1e-06
highest = lax.Precision.HIGHEST


def prefix(part, axis, combine, identity):
    place = lax.axis_index(axis)
    gathered = jax.tree.map(lambda a: lax.all_gather(a, axis), part)
    state = jax.tree.map(lambda a, e: jnp.zeros_like(a) + jnp.asarray(e, a.dtype), part, identity)

    def one(lap, state):
        return combine(
            state, jax.tree.map(lambda a: lax.dynamic_index_in_dim(a, lap, 0, False), gathered)
        )

    return lax.fori_loop(0, place, one, state)


def matmul_heads(left, right):
    return jnp.einsum("hde,hef->hdf", left, right, precision=highest)


def merge_triple(earlier, later):
    return (
        earlier[0] + later[0],
        earlier[1] + later[1],
        earlier[2] + later[2] + matmul_heads(later[0], earlier[1]),
    )


def walk_blocks(carry, item):
    new_carry = (
        carry[0] + item[0],
        carry[1] + item[1],
        carry[2] + item[2] + matmul_heads(item[0], carry[1]),
    )
    return (new_carry, carry)


def per_device(query_rows, key_rows, value_rows, head_scale, out_gain):
    tok_rows = query_rows.shape[0]
    heads = head_scale.shape[0]
    head_size = query_rows.shape[1] // heads
    block_count = tok_rows // BLK
    query_blk = query_rows.reshape(block_count, BLK, heads, head_size)
    key_blk = key_rows.reshape(block_count, BLK, heads, head_size)
    value_blk = value_rows.reshape(block_count, BLK, heads, head_size)
    query_f32 = query_blk.astype(jnp.float32)
    value_f32 = value_blk.astype(jnp.float32)
    positions = jnp.arange(BLK)
    lower_mask = (positions[:, None] >= positions[None, :]).astype(jnp.float32)
    upper_mask = (positions[:, None] <= positions[None, :]).astype(jnp.float32)
    strict_lower = (positions[:, None] > positions[None, :]).astype(jnp.float32)
    scores = jnp.einsum("nthd,nahd->nhta", query_blk, key_blk, preferred_element_type=jnp.float32)
    back_scores = jnp.einsum(
        "nahd,nbhd->nhab", key_blk, query_blk, preferred_element_type=jnp.float32
    )
    weights = (
        jnp.einsum(
            "nhta,nhab->nhtb", scores * lower_mask, back_scores * upper_mask, precision=highest
        )
        * lower_mask
    )
    inside = jnp.einsum("nhtb,nbhd->nhtd", weights, value_f32, precision=highest)
    blk_k = jnp.einsum("nahd,nahe->nhde", key_blk, key_blk, preferred_element_type=jnp.float32)
    blk_qv = jnp.einsum("nahd,nahe->nhde", query_blk, value_blk, preferred_element_type=jnp.float32)
    earlier = jnp.einsum(
        "nhab,nbhd->nhad", back_scores * strict_lower, value_f32, precision=highest
    )
    blk_cross = jnp.einsum(
        "nahd,nhae->nhde", key_blk.astype(jnp.float32), earlier, precision=highest
    )
    zeros = jnp.zeros((heads, head_size, head_size), jnp.float32)
    totals, before = lax.scan(walk_blocks, (zeros, zeros, zeros), (blk_k, blk_qv, blk_cross))
    seg_k, seg_qv, seg_cross = prefix(
        (totals[0], totals[1], totals[2]), "seq", merge_triple, (zeros, zeros, zeros)
    )
    sums_k = seg_k[None] + before[0]
    sums_qv = seg_qv[None] + before[1]
    cross = (
        seg_cross[None]
        + before[2]
        + jnp.einsum("nhde,hef->nhdf", before[0], seg_qv, precision=highest)
    )
    prior = jnp.einsum("nhde,nhef->nhdf", sums_k, sums_qv, precision=highest) - cross
    query_state = jnp.einsum("nthd,nhde->nhte", query_f32, sums_k, precision=highest)
    carried = jnp.einsum("nhte,nbhe->nhtb", query_state, query_f32, precision=highest) * lower_mask
    numer = inside + jnp.einsum("nhtb,nbhd->nhtd", carried, value_f32, precision=highest)
    numer = numer + jnp.einsum("nthd,nhde->nhte", query_f32, prior, precision=highest)
    numer = numer.transpose(0, 2, 1, 3).reshape(tok_rows, heads, head_size)
    scaled = numer * head_scale[None, :, None]
    local_sq = jnp.sum(scaled * scaled, axis=(1, 2))
    total_sq = lax.psum(local_sq, "head")
    mean_sq = total_sq / (heads * lax.axis_size("head") * head_size)
    normed = scaled * lax.rsqrt(mean_sq + epsilon)[:, None, None]
    return (normed.reshape(tok_rows, heads * head_size) * out_gain[None, :]).astype(jnp.bfloat16)


def solution(mesh):
    return jax.shard_map(
        per_device,
        mesh=mesh,
        in_specs=(P("seq", "head"), P("seq", "head"), P("seq", "head"), P("head"), P("head")),
        out_specs=P("seq", "head"),
        check_vma=False,
    )
```

profile of v0, /device:TPU:31, one launch (start us, length us, event | category | flops | bytes accessed | tf_op | source)
XLA Modules:
  0.0 583.2 jit_solution(1458295555518064925)
XLA Ops:
  14.7 3.3 fusion.42
  18.0 4.4 fusion.21
  22.4 3.7 convolution_bitcast_fusion
  26.1 88.7 %while.36 = (s32[]{:T(128)}, f32[8,128,128]{2,1,0:T(8,128)S(1)}, f32[8,128,128]{2,1,0:T(8,128)S(1)}, f32[8,128,128]{2,1,0:T(8,128)}, f32[8,8,128,128]{3,2,1,0:T(...) while((s32[]{:T(128)}, f32[8,128,128]{2,1,0:T(8,128)S(1)}, ...), condition=%wide.region_1.2_spmd.clone, body=%wide.region_0.1_spmd.clone.sunk | while | flops 202768384 | bytes 11011737 | solution.py:81
  43.0 2.8 convolution_add_fusion.5
  65.5 2.8 convolution_add_fusion.5
  87.9 2.8 convolution_add_fusion.5
  110.5 2.8 convolution_add_fusion.5
  117.2 4.1 copy.35
  121.4 3.3 fusion.48
  124.7 5.9 %fusion.25 = f32[8,8,128,128]{3,2,1,0:T(8,128)} fusion(f32[8,8,128,128]{3,2,1,0:T(8,128)S(1)} %copy-done.4, f32[8,8,128,128]{3,2,1,0:T(8,128)S(1)} %fusion.48, f32[128,128]{1,0:T(8,128)S(1)} %get-tuple-element.224, f32[128,128]{1,0:T(8,128)S(1)} %get-tuple-element.223), kind=kOutput, calls=%fused_computation.40 | convolution fusion | flops 1612709888 | bytes 12713984 | tf_op jit(solution)/shard_map/nhta,nhab->nhtb/dot_general | solution.py:66
  130.6 96.3 %all-gather.7.cloned.1.call-done = f32[128,128,128]{2,1,0:T(8,128)} async-done(((f32[8,128,128]{2,1,0:T(8,128)}), f32[128,128,128]{2,1,0:T(8,128)}) %all-gather.7.cloned.1.call-update) | async-done | bytes 8388624 | tf_op jit(solution)/shard_map/all_gather | solution.py:15
  226.9 113.8 %all-gather.9.cloned.1.call-done = f32[128,128,128]{2,1,0:T(8,128)} async-done(((f32[8,128,128]{2,1,0:T(8,128)}), f32[128,128,128]{2,1,0:T(8,128)}) %all-gather.9.cloned.1.call-update) | async-done | bytes 8388624 | tf_op jit(solution)/shard_map/all_gather | solution.py:15
  340.8 113.8 %all-gather.11.cloned.1.call-done = f32[128,128,128]{2,1,0:T(8,128)} async-done(((f32[8,128,128]{2,1,0:T(8,128)}), f32[128,128,128]{2,1,0:T(8,128)}) %all-gather.11.cloned.1.call-update) | async-done | bytes 8388624 | tf_op jit(solution)/shard_map/all_gather | solution.py:15
  455.5 64.7 %while.35 = (s32[]{:T(128)}, f32[8,128,128]{2,1,0:T(8,128)S(1)}, f32[8,128,128]{2,1,0:T(8,128)S(1)}, f32[8,128,128]{2,1,0:T(8,128)}, s32[]{:T(128)}, /*index=5*/...) while((s32[]{:T(128)}, f32[8,128,128]{2,1,0:T(8,128)S(1)}, ...), condition=%wide.region_3.4_spmd, body=%wide.region_2.3_spmd.sunk | while | flops 201850880 | bytes 5768347 | solution.py:23
  520.2 5.6 fusion.59
  525.9 2.9 fusion.29
  528.8 5.1 fusion.17
  533.9 4.5 fusion.54
  538.4 6.2 %fusion.19 = f32[8,8,128,128]{2,3,1,0:T(8,128)} fusion(bf16[8,128,8,128]{1,3,2,0:T(8,128)(2,1)S(1)} %copy-done.8, f32[8,8,128,128]{3,2,1,0:T(8,128)S(1)} %fusion.54, f32[128,128]{1,0:T(8,128)S(1)} %get-tuple-element.223), kind=kOutput, calls=%fused_computation.34 | convolution fusion | flops 1611661312 | bytes 10551296 | tf_op jit(solution)/shard_map/nhtb,nbhd->nhtd/dot_general | solution.py:95
  544.7 8.0 %fusion.14 = f32[8,8,128,128]{3,2,1,0:T(8,128)} fusion(f32[8,8,128,128]{3,2,1,0:T(8,128)S(1)} %fusion.17, f32[8,128,8,128]{1,3,0,2:T(8,128)S(1)} %fusion.59, f32[8,8,128,128]{3,2,1,0:T(8,128)} %get-tuple-element.115, f32[8,128,128]{2,1,0:T(8,128)S(1)} %copy-done.7, bf16[8,128,8,128]{3,2,1,0:T(8,128)(2,1)S(1)} %bitcast.94), kind=kOutput, calls=%fused_computation.29 | convolution fusion | flops 1613758464 | bytes 19398656 | tf_op jit(solution)/shard_map/nthd,nhde->nhte/dot_general | solution.py:96
  552.7 11.3 %multiply_reduce_fusion = (f32[8,128]{1,0:T(8,128)S(1)}, f32[8,128,8,128]{1,3,2,0:T(8,128)}) fusion(f32[8]{0:T(128)S(1)} %copy-done.13, f32[8,8,128,128]{3,2,1,0:T(8,128)} %fusion.14, f32[8,8,128,128]{2,3,1,0:T(8,128)} %fusion.19, bf16[8,128,8,128]{1,3,2,0:T(8,128)(2,1)S(1)} %copy-done.8, f32[8,8,128,128]{3,2,1,0:T(8,128)} %fusion.25, ...), kind=kOutput, calls=%fused_computation.30 | convolution fusion | flops 1616903168 | bytes 18944032 | tf_op jit(solution)/shard_map/nhtb,nbhd->nhtd/dot_general | solution.py:71
  566.7 5.4 copy.53
  572.0 4.2 fusion.12
  (127 shorter events, 155.6 us)
Async XLA Ops:
  6.5 220.4 %all-gather.7.cloned.1.call-start = ((), (), s32[]{:S(2)}) async-start(), calls=%async_computation | async-start | bytes 8912896 | tf_op jit(solution)/shard_map/all_gather | solution.py:15
  6.6 2.4 copy-start.10
  6.6 3.0 copy-start.11
  9.6 12.7 %copy-start.2 = (bf16[128,8,8,128]{3,2,1,0:T(8,128)(2,1)}, bf16[128,8,8,128]{3,2,1,0:T(8,128)(2,1)S(1)}, u32[]{:S(2)}) copy-start(bf16[128,8,8,128]{3,2,1,0:T(8,128)(2,1)S(1)} %copy.63) | copy-start | bytes 6291460
  10.3 7.7 %copy-start.6 = (bf16[128,8,8,128]{3,2,1,0:T(8,128)(2,1)}, bf16[128,8,8,128]{3,2,1,0:T(8,128)(2,1)S(1)}, u32[]{:S(2)}) copy-start(bf16[128,8,8,128]{3,2,1,0:T(8,128)(2,1)S(1)} %copy.64) | copy-start | bytes 6291460
  14.7 3.3 copy-start.3
  114.8 0.8 copy-start.1
  114.9 1.0 copy-start
  114.9 6.5 %copy-start.13 = (f32[8]{0:T(128)S(1)}, f32[8]{0:T(128)}, u32[]{:S(2)}) copy-start(f32[8]{0:T(128)} %param.12) | copy-start | bytes 100
  115.7 225.1 %all-gather.9.cloned.1.call-start = ((), (), s32[]{:S(2)}) async-start(), calls=%async_computation.1 | async-start | bytes 8912896 | tf_op jit(solution)/shard_map/all_gather | solution.py:15
  116.4 338.2 %all-gather.11.cloned.1.call-start = ((), (), s32[]{:S(2)}) async-start(), calls=%async_computation.2 | async-start | bytes 8912896 | tf_op jit(solution)/shard_map/all_gather | solution.py:15
  121.4 3.3 copy-start.4
  520.2 5.6 copy-start.5
  525.9 3.0 copy-start.9
  533.9 4.5 copy-start.8
  538.4 6.2 %copy-start.7 = (f32[8,128,128]{2,1,0:T(8,128)S(1)}, f32[8,128,128]{2,1,0:T(8,128)}, u32[]{:S(2)}) copy-start(f32[8,128,128]{2,1,0:T(8,128)} %get-tuple-element.114) | copy-start | bytes 1572868
  566.7 5.4 copy-start.12
Sparse Core Ops, SparseCore 0:
  115.8 111.1 all-gather.6
  229.7 111.0 all-gather.8
  343.5 111.0 all-gather.10
where the time goes:
time: 593 us; the launch traced here: 583 us
  waiting for transfers between devices  325 us (55%)
  matrix products  133 us (22%)
  other arithmetic  61.2 us (10%)
  local copies, waits for them, and re-layouts  46.4 us (8%)
  between operations  13.8 us (2%)
    all_gather x3, waiting for transfers between devices, prefix(): gathered = jax.tree.map(lambda a: lax.all_gather(a, axis), part)  324 us
    dot_general x23, matrix products, matmul_heads(): return jnp.einsum('hde,hef->hdf', left, right, precision=highest)  64.6 us
    dynamic_slice x16, local copies, waits for them, and re-layouts, per_device(): lax.scan(walk_blocks, (zeros, zeros, zeros), (blk_k, blk_qv, blk_cross))  31.3 us
    dynamic_update_slice x16, other arithmetic, per_device(): lax.scan(walk_blocks, (zeros, zeros, zeros), (blk_k, blk_qv, blk_cross))  22.4 us
    add x15, other arithmetic, merge_triple(): earlier[1] + later[1]  22.1 us
    add x8, other arithmetic, walk_blocks(): carry[1] + item[1]  12.4 us
  transfers between devices with their start and end apart: 3, of which 3 were waited for; matrix products, arithmetic and copies ran while one was open for 2% of the time, Pallas kernels for 0%

commit v1 on v0

v1 whole, which is shorter than its diff:
```python
import functools

import jax
import jax.numpy as jnp
from jax import lax
from jax.experimental import pallas as pl
from jax.experimental.pallas import tpu as pltpu
from jax.sharding import PartitionSpec as P

BLK = 128
VMEM_LIMIT = 48 * 1024 * 1024

epsilon = 1e-06
f32, bf16 = jnp.float32, jnp.bfloat16

NN = (((1,), (0,)), ((), ()))
NT = (((1,), (1,)), ((), ()))
TN = (((0,), (0,)), ((), ()))


def dot(a, b, dims=NN):
    return lax.dot_general(a, b, dims, preferred_element_type=f32)


def split(a):
    high = a.astype(bf16)
    return high, (a - high.astype(f32)).astype(bf16)


def lanes(*parts):
    return jnp.concatenate(parts, axis=1)


def rows(*parts):
    return jnp.concatenate(parts, axis=0)


def dot_f32(a, b):
    a_high, a_low = split(a)
    b_high, b_low = split(b)
    return dot(lanes(a_high, a_low), rows(b_high, b_high)) + dot(a_high, b_low)


def lower():
    shape = (BLK, BLK)
    return lax.broadcasted_iota(jnp.int32, shape, 0) >= lax.broadcasted_iota(jnp.int32, shape, 1)


def moments_kernel(q_ref, k_ref, v_ref, out_ref):
    k = k_ref[...]
    out_ref[0, :BLK] = dot(k, k, TN)
    out_ref[0, BLK:] = dot(q_ref[...], v_ref[...], TN)


def first_stage_kernel(q_ref, k_ref, v_ref, r_ref, d_ref):
    blocks = q_ref.shape[0] // BLK
    mask = lower()
    state = jnp.zeros((BLK, BLK), f32)
    total = jnp.zeros((BLK, BLK), f32)
    for i in range(blocks):
        at = pl.ds(i * BLK, BLK)
        q, k, v = q_ref[at], k_ref[at], v_ref[at]
        a_high, a_low = split(jnp.where(mask, dot(q, k, NT), 0.0))
        r = dot(lanes(a_high, a_low), rows(k, k))
        if i > 0:
            s_high, s_low = split(state)
            r = r + dot(lanes(q, q), rows(s_high, s_low))
        state = state + dot(k, k, TN)
        r_ref[at] = r
        r_high, r_low = split(r)
        total = total + dot(rows(r_high, r_low), rows(v, v), TN)
    d_ref[0] = total


def second_stage_kernel(q_ref, v_ref, r_ref, s_ref, num_ref):
    blocks = q_ref.shape[0] // BLK
    mask = lower()
    s_high, s_low = split(s_ref[0])
    s_both = rows(s_high, s_low)
    state = jnp.zeros((BLK, BLK), f32)
    for i in range(blocks):
        at = pl.ds(i * BLK, BLK)
        q, v = q_ref[at], v_ref[at]
        qq, vv = lanes(q, q), rows(v, v)
        r_high, r_low = split(r_ref[at] + dot(qq, s_both))
        a_high, a_low = split(jnp.where(mask, dot(qq, lanes(r_high, r_low), NT), 0.0))
        num = dot(lanes(a_high, a_low), vv)
        if i > 0:
            d_high, d_low = split(state)
            num = num + dot(qq, rows(d_high, d_low))
        num_ref[at] = num
        if i + 1 < blocks:
            state = state + dot(rows(r_high, r_low), vv, TN)


def owner_local_kernel(moments_ref, s_ref, c_ref, f_ref):
    members = moments_ref.shape[0]
    s = jnp.zeros((BLK, BLK), f32)
    c = jnp.zeros((BLK, BLK), f32)
    f = jnp.zeros((BLK, BLK), f32)
    for m in range(members):
        s_ref[m], c_ref[m], f_ref[m] = s, c, f
        c_own = moments_ref[m, BLK:]
        if m > 0:
            f = f + dot_f32(s, c_own)
        s = s + moments_ref[m, :BLK]
        c = c + c_own
    s_ref[members], c_ref[members], f_ref[members] = s, c, f


def owner_shift_kernel(s_ref, c_ref, f_ref, before_ref, back_ref, out_ref):
    members = back_ref.shape[0]
    before = before_ref[...]
    for m in range(members):
        back_ref[m] = s_ref[m] + before
    out_ref[0] = f_ref[0]
    for m in range(1, members + 1):
        out_ref[m] = f_ref[m] + dot_f32(before, c_ref[m])


def owner_sum_kernel(d_ref, h_ref, base_ref, total_ref):
    members = d_ref.shape[0]
    d = jnp.zeros((BLK, BLK), f32)
    for m in range(members):
        base_ref[m] = h_ref[m] + d
        d = d + d_ref[m]
    total_ref[...] = h_ref[members] + d


def add_kernel(base_ref, before_ref, out_ref):
    for m in range(out_ref.shape[0]):
        out_ref[m] = base_ref[m] + before_ref[...]


def scale_kernel(q_ref, num_ref, d_ref, scale_ref, y_ref, part_ref):
    heads = d_ref.shape[0]
    part = jnp.zeros(part_ref.shape, f32)
    for h in range(heads):
        at = slice(h * BLK, (h + 1) * BLK)
        q = q_ref[:, at]
        d_high, d_low = split(d_ref[h])
        y = (num_ref[:, at] + dot(lanes(q, q), rows(d_high, d_low))) * scale_ref[:, at]
        y_ref[:, at] = y
        part = part + y * y
    part_ref[...] = part


def norm_kernel(features, y_ref, mine_ref, other_ref, gain_ref, out_ref):
    total = jnp.sum(mine_ref[...] + other_ref[...], axis=1, keepdims=True)
    inv = lax.rsqrt(total * (1.0 / features) + epsilon)
    out_ref[...] = (y_ref[...] * inv * gain_ref[...]).astype(bf16)


def params(*semantics):
    return pltpu.CompilerParams(dimension_semantics=semantics, vmem_limit_bytes=VMEM_LIMIT)


def cost(us, moved):
    return pl.CostEstimate(flops=int(us * 4e8), bytes_accessed=int(moved), transcendentals=0)


def per_device(query_rows, key_rows, value_rows, head_scale, out_gain):
    tokens, width = query_rows.shape
    heads = head_scale.shape[0]
    seq = lax.axis_size("seq")
    members = heads
    groups = seq // members
    index_groups = [[g * members + m for m in range(members)] for g in range(groups)]
    onward = [(i, i + members) for i in range(seq - members)]

    def swap(a):
        return lax.all_to_all(a, "seq", 0, 0, axis_index_groups=index_groups)

    head_col = pl.BlockSpec((tokens, BLK), lambda h: (0, h))
    head_mat = pl.BlockSpec((1, BLK, BLK), lambda h: (h, 0, 0))
    mats = lambda n: jax.ShapeDtypeStruct((n, BLK, BLK), f32)
    mat = jax.ShapeDtypeStruct((BLK, BLK), f32)

    moments = pl.pallas_call(
        moments_kernel,
        grid=(heads,),
        in_specs=[head_col] * 3,
        out_specs=pl.BlockSpec((1, 2 * BLK, BLK), lambda h: (h, 0, 0)),
        out_shape=jax.ShapeDtypeStruct((heads, 2 * BLK, BLK), f32),
        compiler_params=params("arbitrary"),
        name="moments",
    )(query_rows, key_rows, value_rows)
    moments_in = swap(moments)

    r_local, d_local = pl.pallas_call(
        first_stage_kernel,
        grid=(heads,),
        in_specs=[head_col] * 3,
        out_specs=[head_col, head_mat],
        out_shape=[jax.ShapeDtypeStruct((tokens, width), f32), mats(heads)],
        compiler_params=params("arbitrary"),
        cost_estimate=cost(10, 10 * tokens * width),
        name="first_stage",
    )(query_rows, key_rows, value_rows)
    d_in = swap(d_local)

    s_part, c_part, f_part = pl.pallas_call(
        owner_local_kernel,
        out_shape=[mats(members + 1)] * 3,
        compiler_params=params(),
        name="owner_local",
    )(moments_in)
    s_before = jnp.zeros((BLK, BLK), f32)
    for _ in range(groups - 1):
        s_before = lax.ppermute(s_before + s_part[members], "seq", onward)
    s_back, h_part = pl.pallas_call(
        owner_shift_kernel,
        out_shape=[mats(members), mats(members + 1)],
        compiler_params=params(),
        name="owner_shift",
    )(s_part, c_part, f_part, s_before)
    s_pre = swap(s_back)

    d_base, d_total = pl.pallas_call(
        owner_sum_kernel,
        out_shape=[mats(members), mat],
        compiler_params=params(),
        name="owner_sum",
    )(d_in, h_part)
    d_before = jnp.zeros((BLK, BLK), f32)
    for _ in range(groups - 1):
        d_before = lax.ppermute(d_before + d_total, "seq", onward)
    d_back = pl.pallas_call(
        add_kernel, out_shape=mats(members), compiler_params=params(), name="owner_add"
    )(d_base, d_before)
    d_pre = swap(d_back)

    num = pl.pallas_call(
        second_stage_kernel,
        grid=(heads,),
        in_specs=[head_col, head_col, head_col, head_mat],
        out_specs=head_col,
        out_shape=jax.ShapeDtypeStruct((tokens, width), f32),
        compiler_params=params("arbitrary"),
        cost_estimate=cost(10, 12 * tokens * width),
        name="second_stage",
    )(query_rows, value_rows, r_local, s_pre)

    step = 256
    row_blk = pl.BlockSpec((step, width), lambda i: (i, 0))
    row_part = pl.BlockSpec((step, BLK), lambda i: (i, 0))
    one_row = pl.BlockSpec((1, width), lambda i: (0, 0))
    scale_row = jnp.repeat(head_scale, BLK)[None, :]
    y, part = pl.pallas_call(
        scale_kernel,
        grid=(tokens // step,),
        in_specs=[row_blk, row_blk, pl.BlockSpec((heads, BLK, BLK), lambda i: (0, 0, 0)), one_row],
        out_specs=[row_blk, row_part],
        out_shape=[jax.ShapeDtypeStruct((tokens, width), f32), jax.ShapeDtypeStruct((tokens, BLK), f32)],
        compiler_params=params("arbitrary"),
        name="scale_squares",
    )(query_rows, num, d_pre, scale_row)
    shards = lax.axis_size("head")
    other = jnp.zeros_like(part)
    for turn in range(1, shards):
        other = other + lax.ppermute(part, "head", [(i, (i + turn) % shards) for i in range(shards)])
    return pl.pallas_call(
        functools.partial(norm_kernel, width * shards),
        grid=(tokens // step,),
        in_specs=[row_blk, row_part, row_part, one_row],
        out_specs=row_blk,
        out_shape=jax.ShapeDtypeStruct((tokens, width), bf16),
        compiler_params=params("arbitrary"),
        name="norm",
    )(y, part, other, out_gain[None, :])


def solution(mesh):
    return jax.shard_map(
        per_device,
        mesh=mesh,
        in_specs=(P("seq", "head"), P("seq", "head"), P("seq", "head"), P("head"), P("head")),
        out_specs=P("seq", "head"),
        check_vma=False,
    )
```

time: 593 us -> 112 us (0.19)
  the two profiles are of different devices: /device:TPU:31 before, /device:TPU:0 now
where the time goes in v1:
time: 112 us; the launch traced here: 111 us
  Pallas kernels  62.4 us (56%)
  starting transfers between devices  31.8 us (28%)
  local copies, waits for them, and re-layouts  10.2 us (9%)
  waiting for transfers between devices  6.34 us (6%)
    pallas_call x1, Pallas kernels, per_device(): pl.pallas_call(second_stage_kernel, grid=(heads,), in_specs=[head_col, he...  24.1 us
    all_to_all x4, starting transfers between devices, swap(): return lax.all_to_all(a, 'seq', 0, 0, axis_index_groups=index_groups)  22 us
    pallas_call x1, Pallas kernels, per_device(): pl.pallas_call(first_stage_kernel, grid=(heads,), in_specs=[head_col] * 3...  20.6 us
    unnamed x20, local copies, waits for them, and re-layouts  10.1 us
    pallas_call x1, Pallas kernels, per_device(): pl.pallas_call(moments_kernel, grid=(heads,), in_specs=[head_col] * 3, ou...  7.22 us
    pallas_call x1, Pallas kernels, per_device(): pl.pallas_call(scale_kernel, grid=(tokens // step,), in_specs=[row_blk, r...  5.51 us
    ppermute x1, starting transfers between devices, per_device(): d_before = lax.ppermute(d_before + d_total, 'seq', onward)  5.29 us
    ppermute x1, starting transfers between devices, per_device(): s_before = lax.ppermute(s_before + s_part[members], 'seq', onward)  4.5 us
  transfers between devices with their start and end apart: 7, of which 4 were waited for; matrix products, arithmetic and copies ran while one was open for 0% of the time, Pallas kernels for 43%

profile of v1, /device:TPU:0, one launch (start us, length us, event | category | flops | bytes accessed | tf_op | source)
XLA Modules:
  0.0 110.8 jit_solution(11179428119980126488)
XLA Ops:
  0.0 1.6 %copy-done = bf16[1024,1024]{1,0:T(8,128)(2,1)S(1)} copy-done((bf16[1024,1024]{1,0:T(8,128)(2,1)S(1)}, bf16[1024,1024]{1,0:T(8,128)(2,1)}, u32[]{:S(2)}) %copy-start) | copy-done | bytes 2097176
  1.6 1.6 %copy-done.3 = bf16[1024,1024]{1,0:T(8,128)(2,1)S(1)} copy-done((bf16[1024,1024]{1,0:T(8,128)(2,1)S(1)}, bf16[1024,1024]{1,0:T(8,128)(2,1)}, u32[]{:S(2)}) %copy-start.3) | copy-done | bytes 2097176
  3.2 7.2 %moments.1 = f32[8,256,128]{2,1,0:T(8,128)} custom-call(bf16[1024,1024]{1,0:T(8,128)(2,1)S(1)} %copy-done, bf16[1024,1024]{1,0:T(8,128)(2,1)S(1)} %copy-done.3, bf16[1024,1024]{1,0:T(8,128)(2,1)} %v_ref.5), custom_call_target="tpu_custom_call" | custom-call | tf_op jit(solution)/shard_map/moments/pallas_call | solution.py:179
  10.4 6.2 %all-to-all-start = ((f32[8,256,128]{2,1,0:T(8,128)}), f32[8,256,128]{2,1,0:T(8,128)S(1)}, u32[]{:S(2)}, u32[]{:S(2)}) async-start(f32[8,256,128]{2,1,0:T(8,128)} %moments.1), calls=%async_computation | async-start | bytes 2097152 | tf_op jit(solution)/shard_map/all_to_all | solution.py:172
  16.6 1.6 %copy-done.4 = bf16[1024,1024]{1,0:T(8,128)(2,1)S(1)} copy-done((bf16[1024,1024]{1,0:T(8,128)(2,1)S(1)}, bf16[1024,1024]{1,0:T(8,128)(2,1)}, u32[]{:S(2)}) %copy-start.4) | copy-done | bytes 2097176
  18.2 20.6 %first_stage.1 = (f32[1024,1024]{1,0:T(8,128)}, f32[8,128,128]{2,1,0:T(8,128)S(1)}) custom-call(bf16[1024,1024]{1,0:T(8,128)(2,1)S(1)} %copy-done.1, bf16[1024,1024]{1,0:T(8,128)(2,1)S(1)} %copy-done.4, bf16[1024,1024]{1,0:T(8,128)(2,1)} %v_ref.5), custom_call_target="tpu_custom_call" | custom-call | flops 4000000000 | bytes 10485760 | tf_op jit(solution)/shard_map/first_stage/pallas_call | solution.py:190
  38.8 0.8 copy-done.6
  39.6 5.1 %all-to-all-start.2 = ((f32[8,128,128]{2,1,0:T(8,128)}), f32[8,128,128]{2,1,0:T(8,128)}, u32[]{:S(2)}, u32[]{:S(2)}) async-start(f32[8,128,128]{2,1,0:T(8,128)} %copy-done.6), calls=%async_computation.2 | async-start | bytes 1048576 | tf_op jit(solution)/shard_map/all_to_all | solution.py:172
  45.1 4.5 %collective-permute-start = (f32[128,128]{1,0:T(8,128)S(1)}, f32[128,128]{1,0:T(8,128)S(1)}, u32[]{:S(2)}, u32[]{:S(2)}) collective-permute-start(f32[128,128]{1,0:T(8,128)S(1)} %slice_bitcast_fusion), channel_id=1, source_target_pairs={{0,16},{2,18},{4,20},{6,22},{8,24},{10,26},{12,28},{14,30},{1,17},... | collective-permute-start | bytes 196616 | tf_op jit(solution)/shard_map/ppermute | solution.py:210
  49.6 1.9 %collective-permute-done.before_ref = f32[128,128]{1,0:T(8,128)S(1)} collective-permute-done((f32[128,128]{1,0:T(8,128)S(1)}, f32[128,128]{1,0:T(8,128)S(1)}, u32[]{:S(2)}, u32[]{:S(2)}) %collective-permute-start) | collective-permute-done | bytes 65568 | tf_op jit(solution)/shard_map/ppermute | solution.py:210
  51.9 0.8 copy-done.7
  52.7 0.7 all-to-all-done.2.d_ref
  53.3 5.0 %all-to-all-start.1 = ((f32[8,128,128]{2,1,0:T(8,128)}), f32[8,128,128]{2,1,0:T(8,128)S(1)}, u32[]{:S(2)}, u32[]{:S(2)}) async-start(f32[8,128,128]{2,1,0:T(8,128)} %copy-done.7), calls=%async_computation.1 | async-start | bytes 1048576 | tf_op jit(solution)/shard_map/all_to_all | solution.py:172
  58.4 1.1 owner_sum.1
  59.5 5.3 %collective-permute-start.1 = (f32[128,128]{1,0:T(8,128)S(1)}, f32[128,128]{1,0:T(8,128)S(1)}, u32[]{:S(2)}, u32[]{:S(2)}) collective-permute-start(f32[128,128]{1,0:T(8,128)S(1)} %get-tuple-element.24), channel_id=1, source_target_pairs={{0,16},{2,18},{4,20},{6,22},{8,24},{10,26},{12,28},{14,30},{1,17},... | collective-permute-start | bytes 196616 | tf_op jit(solution)/shard_map/ppermute | solution.py:227
  64.8 1.9 %collective-permute-done.1.before_ref = f32[128,128]{1,0:T(8,128)S(1)} collective-permute-done((f32[128,128]{1,0:T(8,128)S(1)}, f32[128,128]{1,0:T(8,128)S(1)}, u32[]{:S(2)}, u32[]{:S(2)}) %collective-permute-start.1) | collective-permute-done | bytes 65568 | tf_op jit(solution)/shard_map/ppermute | solution.py:227
  66.6 0.9 owner_add.1
  67.6 5.7 %all-to-all-start.3 = ((f32[8,128,128]{2,1,0:T(8,128)}), f32[8,128,128]{2,1,0:T(8,128)S(1)}, u32[]{:S(2)}, u32[]{:S(2)}) async-start(f32[8,128,128]{2,1,0:T(8,128)} %owner_add.1), calls=%async_computation.3 | async-start | bytes 1048576 | tf_op jit(solution)/shard_map/all_to_all | solution.py:172
  73.2 1.6 %copy-done.5 = bf16[1024,1024]{1,0:T(8,128)(2,1)S(1)} copy-done((bf16[1024,1024]{1,0:T(8,128)(2,1)S(1)}, bf16[1024,1024]{1,0:T(8,128)(2,1)}, u32[]{:S(2)}) %copy-start.5) | copy-done | bytes 2097176
  74.8 24.1 %second_stage.1.num_ref = f32[1024,1024]{1,0:T(8,128)} custom-call(bf16[1024,1024]{1,0:T(8,128)(2,1)S(1)} %copy-done.1, bf16[1024,1024]{1,0:T(8,128)(2,1)S(1)} %copy-done.5, f32[1024,1024]{1,0:T(8,128)} %get-tuple-element.16.r_ref, f32[8,128,128]{2,1,0:T(8,128)S(1)} %all-to-all-done.1.s_ref), custom_call_target="tpu_custom_call" | custom-call | flops 4000000000 | bytes 12582912 | tf_op jit(solution)/shard_map/second_stage/pallas_call | solution.py:233
  99.0 5.5 %scale_squares.1 = (f32[1024,1024]{1,0:T(8,128)}, f32[1024,128]{1,0:T(8,128)S(1)}) custom-call(bf16[1024,1024]{1,0:T(8,128)(2,1)S(1)} %copy-done.1, f32[1024,1024]{1,0:T(8,128)} %second_stage.1.num_ref, f32[8,128,128]{2,1,0:T(8,128)S(1)} %all-to-all-done.3.d_ref, f32[1,1024]{1,0:T(1,128)S(1)} %bitcast.4), custom_call_target="tpu_custom_call" | custom-call | tf_op jit(solution)/shard_map/scale_squares/pallas_call | solution.py:249
  104.5 1.9 %collective-permute-done.2.other_ref = f32[1024,128]{1,0:T(8,128)S(1)} collective-permute-done((f32[1024,128]{1,0:T(8,128)S(1)}, f32[1024,128]{1,0:T(8,128)S(1)}, u32[]{:S(2)}, u32[]{:S(2)}) %collective-permute-start.2) | collective-permute-done | bytes 524320 | tf_op jit(solution)/shard_map/ppermute | solution.py:261
  106.4 2.2 %copy-done.2 = f32[1024,1024]{1,0:T(8,128)S(1)} copy-done((f32[1024,1024]{1,0:T(8,128)S(1)}, f32[1024,1024]{1,0:T(8,128)}, u32[]{:S(2)}) %copy-start.2) | copy-done | bytes 4194328
  108.6 2.1 %norm.1 = bf16[1024,1024]{1,0:T(8,128)(2,1)} custom-call(f32[1024,1024]{1,0:T(8,128)S(1)} %copy-done.2, f32[1024,128]{1,0:T(8,128)S(1)} %get-tuple-element.26.mine_ref, f32[1024,128]{1,0:T(8,128)S(1)} %collective-permute-done.2.other_ref, f32[1,1024]{1,0:T(1,128)S(1)} %bitcast.5), custom_call_target="tpu_custom_call" | custom-call | tf_op jit(solution)/shard_map/norm/pallas_call | solution.py:262
  (21 shorter events, 0.9 us)
Async XLA Ops:
  0.0 1.6 %copy-start = (bf16[1024,1024]{1,0:T(8,128)(2,1)S(1)}, bf16[1024,1024]{1,0:T(8,128)(2,1)}, u32[]{:S(2)}) copy-start(bf16[1024,1024]{1,0:T(8,128)(2,1)} %q_ref.7) | copy-start | bytes 6291460
  1.6 1.6 %copy-start.3 = (bf16[1024,1024]{1,0:T(8,128)(2,1)S(1)}, bf16[1024,1024]{1,0:T(8,128)(2,1)}, u32[]{:S(2)}) copy-start(bf16[1024,1024]{1,0:T(8,128)(2,1)} %k_ref.3) | copy-start | bytes 6291460
  3.2 13.4 %copy-start.1 = (bf16[1024,1024]{1,0:T(8,128)(2,1)S(1)}, bf16[1024,1024]{1,0:T(8,128)(2,1)}, u32[]{:S(2)}) copy-start(bf16[1024,1024]{1,0:T(8,128)(2,1)} %q_ref.7) | copy-start | bytes 6291460
  10.4 29.2 %all-to-all-start = ((f32[8,256,128]{2,1,0:T(8,128)}), f32[8,256,128]{2,1,0:T(8,128)S(1)}, u32[]{:S(2)}, u32[]{:S(2)}) async-start(f32[8,256,128]{2,1,0:T(8,128)} %moments.1), calls=%async_computation | async-start | bytes 2097152 | tf_op jit(solution)/shard_map/all_to_all | solution.py:172
  16.6 1.6 %copy-start.4 = (bf16[1024,1024]{1,0:T(8,128)(2,1)S(1)}, bf16[1024,1024]{1,0:T(8,128)(2,1)}, u32[]{:S(2)}) copy-start(bf16[1024,1024]{1,0:T(8,128)(2,1)} %k_ref.3) | copy-start | bytes 6291460
  38.8 0.8 copy-start.6
  39.6 13.7 %all-to-all-start.2 = ((f32[8,128,128]{2,1,0:T(8,128)}), f32[8,128,128]{2,1,0:T(8,128)}, u32[]{:S(2)}, u32[]{:S(2)}) async-start(f32[8,128,128]{2,1,0:T(8,128)} %copy-done.6), calls=%async_computation.2 | async-start | bytes 1048576 | tf_op jit(solution)/shard_map/all_to_all | solution.py:172
  45.1 6.4 %collective-permute-start = (f32[128,128]{1,0:T(8,128)S(1)}, f32[128,128]{1,0:T(8,128)S(1)}, u32[]{:S(2)}, u32[]{:S(2)}) collective-permute-start(f32[128,128]{1,0:T(8,128)S(1)} %slice_bitcast_fusion), channel_id=1, source_target_pairs={{0,16},{2,18},{4,20},{6,22},{8,24},{10,26},{12,28},{14,30},{1,17},... | collective-permute-start | bytes 196616 | tf_op jit(solution)/shard_map/ppermute | solution.py:210
  51.9 0.8 copy-start.7
  53.3 14.2 %all-to-all-start.1 = ((f32[8,128,128]{2,1,0:T(8,128)}), f32[8,128,128]{2,1,0:T(8,128)S(1)}, u32[]{:S(2)}, u32[]{:S(2)}) async-start(f32[8,128,128]{2,1,0:T(8,128)} %copy-done.7), calls=%async_computation.1 | async-start | bytes 1048576 | tf_op jit(solution)/shard_map/all_to_all | solution.py:172
  59.5 7.2 %collective-permute-start.1 = (f32[128,128]{1,0:T(8,128)S(1)}, f32[128,128]{1,0:T(8,128)S(1)}, u32[]{:S(2)}, u32[]{:S(2)}) collective-permute-start(f32[128,128]{1,0:T(8,128)S(1)} %get-tuple-element.24), channel_id=1, source_target_pairs={{0,16},{2,18},{4,20},{6,22},{8,24},{10,26},{12,28},{14,30},{1,17},... | collective-permute-start | bytes 196616 | tf_op jit(solution)/shard_map/ppermute | solution.py:227
  67.6 31.4 %all-to-all-start.3 = ((f32[8,128,128]{2,1,0:T(8,128)}), f32[8,128,128]{2,1,0:T(8,128)S(1)}, u32[]{:S(2)}, u32[]{:S(2)}) async-start(f32[8,128,128]{2,1,0:T(8,128)} %owner_add.1), calls=%async_computation.3 | async-start | bytes 1048576 | tf_op jit(solution)/shard_map/all_to_all | solution.py:172
  73.2 1.6 %copy-start.5 = (bf16[1024,1024]{1,0:T(8,128)(2,1)S(1)}, bf16[1024,1024]{1,0:T(8,128)(2,1)}, u32[]{:S(2)}) copy-start(bf16[1024,1024]{1,0:T(8,128)(2,1)} %v_ref.5) | copy-start | bytes 6291460
  74.8 24.1 %copy-start.9 = (f32[8]{0:T(128)S(1)}, f32[8]{0:T(128)}, u32[]{:S(2)}) copy-start(f32[8]{0:T(128)} %param.8) | copy-start | bytes 100
  99.0 7.4 %copy-start.8 = (f32[1024]{0:T(1024)S(1)}, f32[1024]{0:T(1024)}, u32[]{:S(2)}) copy-start(f32[1024]{0:T(1024)} %param.9) | copy-start | bytes 12292
  104.5 1.9 %collective-permute-start.2 = (f32[1024,128]{1,0:T(8,128)S(1)}, f32[1024,128]{1,0:T(8,128)S(1)}, u32[]{:S(2)}, u32[]{:S(2)}) collective-permute-start(f32[1024,128]{1,0:T(8,128)S(1)} %get-tuple-element.26.mine_ref), channel_id=1, source_target_pairs={{0,1},{1,0},{2,3},{3,2},{4,5},{5,4},{6,7},{7,6},{8,9},{9,8},{10,11... | collective-permute-start | bytes 1572872 | tf_op jit(solution)/shard_map/ppermute | solution.py:261
  106.4 2.2 %copy-start.2 = (f32[1024,1024]{1,0:T(8,128)S(1)}, f32[1024,1024]{1,0:T(8,128)}, u32[]{:S(2)}) copy-start(f32[1024,1024]{1,0:T(8,128)} %get-tuple-element.25.y_ref) | copy-start | bytes 12582916

commit v2 on v1

v2 whole, which is shorter than its diff:
```python
import functools

import jax
import jax.numpy as jnp
from jax import lax
from jax.experimental import pallas as pl
from jax.experimental.pallas import tpu as pltpu
from jax.sharding import PartitionSpec as P

BLK = 128
CHUNK = 256
PAIR = 2
VMEM_LIMIT = 60 * 1024 * 1024

epsilon = 1e-06
f32, bf16 = jnp.float32, jnp.bfloat16

NN = (((1,), (0,)), ((), ()))
NT = (((1,), (1,)), ((), ()))
TN = (((0,), (0,)), ((), ()))


def dot(a, b, dims=NN):
    return lax.dot_general(a, b, dims, preferred_element_type=f32)


def split(a):
    high = a.astype(bf16)
    return high, (a - high.astype(f32)).astype(bf16)


def lanes(*parts):
    return jnp.concatenate(parts, axis=1)


def rows(*parts):
    return jnp.concatenate(parts, axis=0)


def dot_f32(a, b):
    a_high, a_low = split(a)
    b_high, b_low = split(b)
    return dot(lanes(a_high, a_low), rows(b_high, b_high)) + dot(a_high, b_low)


def ordered(size):
    shape = (size, size)
    return lax.broadcasted_iota(jnp.int32, shape, 0) - lax.broadcasted_iota(jnp.int32, shape, 1)


def span(j, size=BLK):
    return slice(j * size, (j + 1) * size)


def moments_kernel(q_ref, k_ref, v_ref, out_ref, kt_ref, vt_ref):
    for j in range(out_ref.shape[0]):
        at = span(j)
        k = k_ref[:, at]
        kt, vt = k.T, v_ref[:, at].T
        kt_ref[at, :], vt_ref[at, :] = kt, vt
        out_ref[j, :BLK] = dot(kt, k)
        out_ref[j, BLK:] = dot(vt, q_ref[:, at])


def first_stage_kernel(q_ref, k_ref, kt_ref, vt_ref, r_ref, d_ref, qt_ref):
    heads = d_ref.shape[0]
    mask = ordered(CHUNK) >= 0
    steps = q_ref.shape[0] // CHUNK
    states = [jnp.zeros((BLK, BLK), f32)] * heads
    for i in range(steps):
        at = span(i, CHUNK)
        for j in range(heads):
            cols = span(j)
            q, k, kt = q_ref[at, cols], k_ref[at, cols], kt_ref[cols, at]
            qt_ref[cols, at] = q.T
            r = dot(lanes(*split(jnp.where(mask, dot(q, kt), 0.0))), rows(k, k))
            if i > 0:
                r = r + dot(lanes(q, q), rows(*split(states[j])))
            if i + 1 < steps:
                states[j] = states[j] + dot(kt, k)
            r_ref[at, span(j, 2 * BLK)] = lanes(*split(r))
    for j in range(heads):
        d = dot(vt_ref[span(j), :], r_ref[:, span(j, 2 * BLK)])
        d_ref[j] = d[:, :BLK] + d[:, BLK:]


def second_stage_kernel(q_ref, qt_ref, vt_ref, r_ref, s_ref, num_ref):
    heads = s_ref.shape[0]
    mask = ordered(CHUNK) <= 0
    steps = q_ref.shape[0] // CHUNK
    states = [jnp.zeros((BLK, BLK), f32)] * heads
    s_both = [rows(*split(s_ref[j])) for j in range(heads)]
    for i in range(steps):
        at = span(i, CHUNK)
        for j in range(heads):
            cols = span(j)
            q, qt, vt = q_ref[at, cols], qt_ref[cols, at], vt_ref[cols, at]
            qt2 = rows(qt, qt)
            pair = r_ref[at, span(j, 2 * BLK)].astype(f32)
            r = lanes(*split(pair[:, :BLK] + pair[:, BLK:] + dot(lanes(q, q), s_both[j])))
            num = dot(lanes(vt, vt), rows(*split(jnp.where(mask, dot(r, qt2), 0.0))))
            if i > 0:
                num = num + dot(lanes(*split(states[j])), qt2)
            num_ref[cols, at] = num
            if i + 1 < steps:
                d = dot(vt, r)
                states[j] = states[j] + d[:, :BLK] + d[:, BLK:]


def owner_local_kernel(moments_ref, s_ref, c_ref, f_ref):
    members = moments_ref.shape[0]
    s = jnp.zeros((BLK, BLK), f32)
    c = jnp.zeros((BLK, BLK), f32)
    f = jnp.zeros((BLK, BLK), f32)
    for m in range(members):
        s_ref[m], c_ref[m], f_ref[m] = s, c, f
        c_own = moments_ref[m, BLK:]
        if m > 0:
            f = f + dot_f32(c_own, s)
        s = s + moments_ref[m, :BLK]
        c = c + c_own
    s_ref[members], c_ref[members], f_ref[members] = s, c, f


def owner_shift_kernel(s_ref, c_ref, f_ref, before_ref, back_ref, out_ref):
    members = back_ref.shape[0]
    before = before_ref[...]
    for m in range(members):
        back_ref[m] = s_ref[m] + before
    out_ref[0] = f_ref[0]
    for m in range(1, members + 1):
        out_ref[m] = f_ref[m] + dot_f32(c_ref[m], before)


def owner_sum_kernel(d_ref, h_ref, base_ref, total_ref):
    members = d_ref.shape[0]
    d = jnp.zeros((BLK, BLK), f32)
    for m in range(members):
        base_ref[m] = h_ref[m] + d
        d = d + d_ref[m]
    total_ref[...] = h_ref[members] + d


def add_kernel(base_ref, before_ref, out_ref):
    for m in range(out_ref.shape[0]):
        out_ref[m] = base_ref[m] + before_ref[...]


def scale_kernel(qt_ref, num_ref, d_ref, gain_ref, scale_ref, y_ref, part_ref):
    first = pl.program_id(0) * d_ref.shape[0]
    part = jnp.zeros((8, qt_ref.shape[1]), f32)
    for j in range(d_ref.shape[0]):
        qt = qt_ref[span(j), :]
        y = num_ref[span(j), :] + dot(lanes(*split(d_ref[j])), rows(qt, qt))
        y = y * scale_ref[first + j]
        part = part + jnp.sum((y * y).reshape(BLK // 8, 8, y.shape[1]), axis=0)
        gain = jnp.broadcast_to(gain_ref[j], (BLK, BLK)).T
        for i in range(y.shape[1] // BLK):
            y_ref[span(j), span(i)] = y[:, span(i)] * gain
    @pl.when(pl.program_id(0) == 0)
    def _():
        part_ref[...] = part
    @pl.when(pl.program_id(0) > 0)
    def _():
        part_ref[...] += part


def norm_kernel(features, y_ref, mine_ref, other_ref, out_ref):
    total = jnp.sum(mine_ref[...] + other_ref[...], axis=0, keepdims=True)
    inv = lax.rsqrt(total * (1.0 / features) + epsilon)
    out_ref[...] = (y_ref[...] * inv).astype(bf16).T


def params(*semantics):
    return pltpu.CompilerParams(dimension_semantics=semantics, vmem_limit_bytes=VMEM_LIMIT)


def cost(us, moved):
    return pl.CostEstimate(flops=int(us * 4e8), bytes_accessed=int(moved), transcendentals=0)


def per_device(query_rows, key_rows, value_rows, head_scale, out_gain):
    tokens, width = query_rows.shape
    heads = head_scale.shape[0]
    seq = lax.axis_size("seq")
    members = heads
    groups = seq // members
    index_groups = [[g * members + m for m in range(members)] for g in range(groups)]
    onward = [(i, i + members) for i in range(seq - members)]

    def swap(a):
        return lax.all_to_all(a, "seq", 0, 0, axis_index_groups=index_groups)

    head_col = pl.BlockSpec((tokens, PAIR * BLK), lambda h: (0, h))
    head_col2 = pl.BlockSpec((tokens, 2 * PAIR * BLK), lambda h: (0, h))
    head_row = pl.BlockSpec((PAIR * BLK, tokens), lambda h: (h, 0))
    head_mat = pl.BlockSpec((PAIR, BLK, BLK), lambda h: (h, 0, 0))
    mats = lambda n: jax.ShapeDtypeStruct((n, BLK, BLK), f32)
    mat = jax.ShapeDtypeStruct((BLK, BLK), f32)
    turned = jax.ShapeDtypeStruct((width, tokens), bf16)
    turned_f32 = jax.ShapeDtypeStruct((width, tokens), f32)

    moments, k_t, v_t = pl.pallas_call(
        moments_kernel,
        grid=(heads // PAIR,),
        in_specs=[head_col] * 3,
        out_specs=[pl.BlockSpec((PAIR, 2 * BLK, BLK), lambda h: (h, 0, 0)), head_row, head_row],
        out_shape=[jax.ShapeDtypeStruct((heads, 2 * BLK, BLK), f32), turned, turned],
        compiler_params=params("arbitrary"),
        name="moments",
    )(query_rows, key_rows, value_rows)
    moments_in = swap(moments)

    r_local, d_local, q_t = pl.pallas_call(
        first_stage_kernel,
        grid=(heads // PAIR,),
        in_specs=[head_col, head_col, head_row, head_row],
        out_specs=[head_col2, head_mat, head_row],
        out_shape=[jax.ShapeDtypeStruct((tokens, 2 * width), bf16), mats(heads), turned],
        compiler_params=params("arbitrary"),
        cost_estimate=cost(10, 10 * tokens * width),
        name="first_stage",
    )(query_rows, key_rows, k_t, v_t)
    d_in = swap(d_local)

    s_part, c_part, f_part = pl.pallas_call(
        owner_local_kernel,
        out_shape=[mats(members + 1)] * 3,
        compiler_params=params(),
        name="owner_local",
    )(moments_in)
    s_before = jnp.zeros((BLK, BLK), f32)
    for _ in range(groups - 1):
        s_before = lax.ppermute(s_before + s_part[members], "seq", onward)
    s_back, h_part = pl.pallas_call(
        owner_shift_kernel,
        out_shape=[mats(members), mats(members + 1)],
        compiler_params=params(),
        name="owner_shift",
    )(s_part, c_part, f_part, s_before)
    s_pre = swap(s_back)

    d_base, d_total = pl.pallas_call(
        owner_sum_kernel,
        out_shape=[mats(members), mat],
        compiler_params=params(),
        name="owner_sum",
    )(d_in, h_part)
    d_before = jnp.zeros((BLK, BLK), f32)
    for _ in range(groups - 1):
        d_before = lax.ppermute(d_before + d_total, "seq", onward)
    d_back = pl.pallas_call(
        add_kernel, out_shape=mats(members), compiler_params=params(), name="owner_add"
    )(d_base, d_before)
    d_pre = swap(d_back)

    num = pl.pallas_call(
        second_stage_kernel,
        grid=(heads // PAIR,),
        in_specs=[head_col, head_row, head_row, head_col2, head_mat],
        out_specs=head_row,
        out_shape=turned_f32,
        compiler_params=params("arbitrary"),
        cost_estimate=cost(10, 12 * tokens * width),
        name="second_stage",
    )(query_rows, q_t, v_t, r_local, s_pre)

    part_blk = pl.BlockSpec((8, tokens), lambda h: (0, 0))
    y, part = pl.pallas_call(
        scale_kernel,
        grid=(heads // PAIR,),
        in_specs=[
            head_row,
            head_row,
            head_mat,
            pl.BlockSpec((PAIR, 1, BLK), lambda h: (h, 0, 0)),
            pl.BlockSpec(memory_space=pltpu.SMEM),
        ],
        out_specs=[head_row, part_blk],
        out_shape=[turned_f32, jax.ShapeDtypeStruct((8, tokens), f32)],
        compiler_params=params("arbitrary"),
        name="scale_squares",
    )(q_t, num, d_pre, out_gain.reshape(heads, 1, BLK), head_scale)
    shards = lax.axis_size("head")
    other = jnp.zeros_like(part)
    for turn in range(1, shards):
        other = other + lax.ppermute(part, "head", [(i, (i + turn) % shards) for i in range(shards)])
    step = 256
    col_blk = pl.BlockSpec((width, step), lambda i: (0, i))
    col_part = pl.BlockSpec((8, step), lambda i: (0, i))
    return pl.pallas_call(
        functools.partial(norm_kernel, width * shards),
        grid=(tokens // step,),
        in_specs=[col_blk, col_part, col_part],
        out_specs=pl.BlockSpec((step, width), lambda i: (i, 0)),
        out_shape=jax.ShapeDtypeStruct((tokens, width), bf16),
        compiler_params=params("arbitrary"),
        name="norm",
    )(y, part, other)


def solution(mesh):
    return jax.shard_map(
        per_device,
        mesh=mesh,
        in_specs=(P("seq", "head"), P("seq", "head"), P("seq", "head"), P("head"), P("head")),
        out_specs=P("seq", "head"),
        check_vma=False,
    )
```

time: 112 us -> 92.8 us (0.83)
  Pallas kernels: 62.4 us -> 48.5 us
  local copies, waits for them, and re-layouts: 10.2 us -> 3.49 us
  waiting for transfers between devices: 6.34 us -> 9.19 us
    pallas_call x4, Pallas kernels: 57.5 us -> 34.5 us  [the longest x1 11.9 us: per_device(): pl.pallas_call(second_stage_kernel, grid=(heads // PAIR,), in_specs=[head...]
    unnamed x20 -> x14, local copies, waits for them, and re-layouts: 10.1 us -> 2.65 us
    all_to_all x4, waiting for transfers between devices: 0.67 us -> 3.7 us  [swap(): return lax.all_to_all(a, 'seq', 0, 0, axis_index_groups=index_groups)]
    pallas_call x1, Pallas kernels: 2.15 us -> 4.58 us  [per_device(): pl.pallas_call(functools.partial(norm_kernel, width * shards), grid=(toke...]
    pallas_call x1, Pallas kernels: 0.36 us -> 2.73 us  [per_device(): pl.pallas_call(owner_local_kernel, out_shape=[mats(members + 1)] * 3, com...]
    pallas_call x1, Pallas kernels: 0.38 us -> 2.63 us  [per_device(): pl.pallas_call(owner_shift_kernel, out_shape=[mats(members), mats(members...]
  transfers between devices with their start and end apart: 7 -> 7, of which waited for: 4 -> 4; matrix products, arithmetic and copies ran while one was open for 0% -> 1% of each run, Pallas kernels for 43% -> 35%
where the time goes in v2:
time: 92.8 us; the launch traced here: 91.9 us
  Pallas kernels  48.5 us (52%)
  starting transfers between devices  30.7 us (33%)
  waiting for transfers between devices  9.19 us (10%)
  local copies, waits for them, and re-layouts  3.49 us (4%)
    all_to_all x4, starting transfers between devices, swap(): return lax.all_to_all(a, 'seq', 0, 0, axis_index_groups=index_groups)  20.9 us
    pallas_call x1, Pallas kernels, per_device(): pl.pallas_call(second_stage_kernel, grid=(heads // PAIR,), in_specs=[head...  11.9 us
    pallas_call x1, Pallas kernels, per_device(): pl.pallas_call(first_stage_kernel, grid=(heads // PAIR,), in_specs=[head_...  11 us
    pallas_call x1, Pallas kernels, per_device(): pl.pallas_call(moments_kernel, grid=(heads // PAIR,), in_specs=[head_col]...  5.84 us
    pallas_call x1, Pallas kernels, per_device(): pl.pallas_call(scale_kernel, grid=(heads // PAIR,), in_specs=[head_row, h...  5.83 us
    ppermute x1, starting transfers between devices, per_device(): d_before = lax.ppermute(d_before + d_total, 'seq', onward)  5.28 us
    pallas_call x1, Pallas kernels, per_device(): pl.pallas_call(functools.partial(norm_kernel, width * shards), grid=(toke...  4.58 us
    ppermute x1, starting transfers between devices, per_device(): s_before = lax.ppermute(s_before + s_part[members], 'seq', onward)  4.49 us
  transfers between devices with their start and end apart: 7, of which 4 were waited for; matrix products, arithmetic and copies ran while one was open for 1% of the time, Pallas kernels for 35%

profile of v2, /device:TPU:0, one launch (start us, length us, event | category | flops | bytes accessed | tf_op | source)
XLA Modules:
  0.0 91.9 jit_solution(6262417490820337328)
XLA Ops:
  0.0 5.8 %moments.1 = (f32[8,256,128]{2,1,0:T(8,128)}, bf16[1024,1024]{1,0:T(8,128)(2,1)}, bf16[1024,1024]{1,0:T(8,128)(2,1)}) custom-call(bf16[1024,1024]{1,0:T(8,128)(2,1)} %q_ref.5, bf16[1024,1024]{1,0:T(8,128)(2,1)} %k_ref.3, bf16[1024,1024]{1,0:T(8,128)(2,1)} %v_ref.1), custom_call_target="tpu_custom_call" | custom-call | tf_op jit(solution)/shard_map/moments/pallas_call | solution.py:203
  5.8 6.2 %all-to-all-start = ((f32[8,256,128]{2,1,0:T(8,128)}), f32[8,256,128]{2,1,0:T(8,128)S(1)}, u32[]{:S(2)}, u32[]{:S(2)}) async-start(f32[8,256,128]{2,1,0:T(8,128)} %get-tuple-element.24), calls=%async_computation | async-start | bytes 2097152 | tf_op jit(solution)/shard_map/all_to_all | solution.py:192
  12.0 11.0 %first_stage.1 = (bf16[1024,2048]{1,0:T(8,128)(2,1)}, f32[8,128,128]{2,1,0:T(8,128)}, bf16[1024,1024]{1,0:T(8,128)(2,1)}) custom-call(bf16[1024,1024]{1,0:T(8,128)(2,1)} %q_ref.5, bf16[1024,1024]{1,0:T(8,128)(2,1)} %k_ref.3, bf16[1024,1024]{1,0:T(8,128)(2,1)} %get-tuple-element.20.kt_ref, bf16[1024,1024]{1,0:T(8,128)(2,1)} %get-tuple-element.21.vt_ref), custom_call_target="tpu_custom_call" | custom-call | flops 4000000000 | bytes 10485760 | tf_op jit(solution)/shard_map/first_stage/pallas_call | solution.py:214
  23.0 3.7 %all-to-all-done.moments_ref = f32[8,256,128]{2,1,0:T(8,128)S(1)} async-done(((f32[8,256,128]{2,1,0:T(8,128)}), f32[8,256,128]{2,1,0:T(8,128)S(1)}, u32[]{:S(2)}, u32[]{:S(2)}) %all-to-all-start) | async-done | bytes 1048608 | tf_op jit(solution)/shard_map/all_to_all | solution.py:192
  26.7 3.5 %all-to-all-start.2 = ((f32[8,128,128]{2,1,0:T(8,128)}), f32[8,128,128]{2,1,0:T(8,128)S(1)}, u32[]{:S(2)}, u32[]{:S(2)}) async-start(f32[8,128,128]{2,1,0:T(8,128)} %get-tuple-element.29), calls=%async_computation.2 | async-start | bytes 1048576 | tf_op jit(solution)/shard_map/all_to_all | solution.py:192
  30.2 2.7 %owner_local.1 = (f32[9,128,128]{2,1,0:T(8,128)}, f32[9,128,128]{2,1,0:T(8,128)}, f32[9,128,128]{2,1,0:T(8,128)}) custom-call(f32[8,256,128]{2,1,0:T(8,128)} %copy-done), custom_call_target="tpu_custom_call" | custom-call | tf_op jit(solution)/shard_map/owner_local/pallas_call | solution.py:226
  33.0 0.8 slice_bitcast_fusion
  33.8 4.5 %collective-permute-start = (f32[128,128]{1,0:T(8,128)S(1)}, f32[128,128]{1,0:T(8,128)S(1)}, u32[]{:S(2)}, u32[]{:S(2)}) collective-permute-start(f32[128,128]{1,0:T(8,128)S(1)} %slice_bitcast_fusion), channel_id=1, source_target_pairs={{0,16},{2,18},{4,20},{6,22},{8,24},{10,26},{12,28},{14,30},{1,17},... | collective-permute-start | bytes 196616 | tf_op jit(solution)/shard_map/ppermute | solution.py:234
  38.3 1.9 %collective-permute-done.before_ref = f32[128,128]{1,0:T(8,128)S(1)} collective-permute-done((f32[128,128]{1,0:T(8,128)S(1)}, f32[128,128]{1,0:T(8,128)S(1)}, u32[]{:S(2)}, u32[]{:S(2)}) %collective-permute-start) | collective-permute-done | bytes 65568 | tf_op jit(solution)/shard_map/ppermute | solution.py:234
  40.2 0.6 copy-done.4
  40.8 2.6 %owner_shift.1 = (f32[8,128,128]{2,1,0:T(8,128)}, f32[9,128,128]{2,1,0:T(8,128)}) custom-call(f32[9,128,128]{2,1,0:T(8,128)} %get-tuple-element.25.s_ref, f32[9,128,128]{2,1,0:T(8,128)} %get-tuple-element.26.c_ref, f32[9,128,128]{2,1,0:T(8,128)} %get-tuple-element.27.f_ref, f32[128,128]{1,0:T(8,128)} %copy-done.4), custom_call_target="tpu_custom_call" | custom-call | tf_op jit(solution)/shard_map/owner_shift/pallas_call | solution.py:235
  43.4 5.6 %all-to-all-start.1 = ((f32[8,128,128]{2,1,0:T(8,128)}), f32[8,128,128]{2,1,0:T(8,128)S(1)}, u32[]{:S(2)}, u32[]{:S(2)}) async-start(f32[8,128,128]{2,1,0:T(8,128)} %get-tuple-element.28), calls=%async_computation.1 | async-start | bytes 1048576 | tf_op jit(solution)/shard_map/all_to_all | solution.py:192
  49.0 2.1 %owner_sum.1 = (f32[8,128,128]{2,1,0:T(8,128)}, f32[128,128]{1,0:T(8,128)}) custom-call(f32[8,128,128]{2,1,0:T(8,128)} %copy-done.2, f32[9,128,128]{2,1,0:T(8,128)} %get-tuple-element.30.h_ref), custom_call_target="tpu_custom_call" | custom-call | tf_op jit(solution)/shard_map/owner_sum/pallas_call | solution.py:243
  51.1 5.3 %collective-permute-start.1 = (f32[128,128]{1,0:T(8,128)}, f32[128,128]{1,0:T(8,128)S(1)}, u32[]{:S(2)}, u32[]{:S(2)}) collective-permute-start(f32[128,128]{1,0:T(8,128)} %get-tuple-element.32), channel_id=1, source_target_pairs={{0,16},{2,18},{4,20},{6,22},{8,24},{10,26},{12,28},{14,30},{1,17},... | collective-permute-start | bytes 196616 | tf_op jit(solution)/shard_map/ppermute | solution.py:251
  56.4 2.2 %collective-permute-done.1.before_ref = f32[128,128]{1,0:T(8,128)S(1)} collective-permute-done((f32[128,128]{1,0:T(8,128)}, f32[128,128]{1,0:T(8,128)S(1)}, u32[]{:S(2)}, u32[]{:S(2)}) %collective-permute-start.1) | collective-permute-done | bytes 65568 | tf_op jit(solution)/shard_map/ppermute | solution.py:251
  58.6 0.6 copy-done.5
  59.2 1.9 %owner_add.1 = f32[8,128,128]{2,1,0:T(8,128)} custom-call(f32[8,128,128]{2,1,0:T(8,128)} %get-tuple-element.31.base_ref, f32[128,128]{1,0:T(8,128)} %copy-done.5), custom_call_target="tpu_custom_call" | custom-call | tf_op jit(solution)/shard_map/owner_add/pallas_call | solution.py:252
  61.2 5.7 %all-to-all-start.3 = ((f32[8,128,128]{2,1,0:T(8,128)}), f32[8,128,128]{2,1,0:T(8,128)S(1)}, u32[]{:S(2)}, u32[]{:S(2)}) async-start(f32[8,128,128]{2,1,0:T(8,128)} %owner_add.1), calls=%async_computation.3 | async-start | bytes 1048576 | tf_op jit(solution)/shard_map/all_to_all | solution.py:192
  66.8 11.9 %second_stage.1.num_ref = f32[1024,1024]{1,0:T(8,128)} custom-call(bf16[1024,1024]{1,0:T(8,128)(2,1)} %q_ref.5, bf16[1024,1024]{1,0:T(8,128)(2,1)} %get-tuple-element.22.qt_ref, bf16[1024,1024]{1,0:T(8,128)(2,1)} %get-tuple-element.21.vt_ref, bf16[1024,2048]{1,0:T(8,128)(2,1)} %get-tuple-element.23.r_ref, f32[8,128,128]{2,1,0:T(8,128)} %copy-done.3), custom_call_target="tpu_custom_call" | custom-call | flops 4000000000 | bytes 12582912 | tf_op jit(solution)/shard_map/second_stage/pallas_call | solution.py:257
  78.7 0.8 copy-done.1
  79.5 5.8 %scale_squares.1 = (f32[1024,1024]{1,0:T(8,128)}, f32[8,1024]{1,0:T(8,128)}) custom-call(bf16[1024,1024]{1,0:T(8,128)(2,1)} %get-tuple-element.22.qt_ref, f32[1024,1024]{1,0:T(8,128)} %second_stage.1.num_ref, f32[8,128,128]{2,1,0:T(8,128)} %copy-done.1, f32[8,1,128]{2,1,0:T(1,128)} %bitcast.3, f32[8]{0:T(128)} %scale_ref.1), custom_call_target="tpu_custom_call" | custom-call | tf_op jit(solution)/shard_map/scale_squares/pallas_call | solution.py:269
  85.3 1.4 %collective-permute-done.2.other_ref = f32[8,1024]{1,0:T(8,128)S(1)} collective-permute-done((f32[8,1024]{1,0:T(8,128)}, f32[8,1024]{1,0:T(8,128)S(1)}, u32[]{:S(2)}, u32[]{:S(2)}) %collective-permute-start.2) | collective-permute-done | bytes 32800 | tf_op jit(solution)/shard_map/ppermute | solution.py:287
  86.7 0.6 copy-done.6
  87.3 4.6 %norm.1 = bf16[1024,1024]{1,0:T(8,128)(2,1)} custom-call(f32[1024,1024]{1,0:T(8,128)} %get-tuple-element.33.y_ref, f32[8,1024]{1,0:T(8,128)} %get-tuple-element.34.mine_ref, f32[8,1024]{1,0:T(8,128)} %copy-done.6), custom_call_target="tpu_custom_call" | custom-call | tf_op jit(solution)/shard_map/norm/pallas_call | solution.py:291
  (14 shorter events, 0.0 us)
Async XLA Ops:
  5.8 20.9 %all-to-all-start = ((f32[8,256,128]{2,1,0:T(8,128)}), f32[8,256,128]{2,1,0:T(8,128)S(1)}, u32[]{:S(2)}, u32[]{:S(2)}) async-start(f32[8,256,128]{2,1,0:T(8,128)} %get-tuple-element.24), calls=%async_computation | async-start | bytes 2097152 | tf_op jit(solution)/shard_map/all_to_all | solution.py:192
  26.7 3.5 %copy-start = (f32[8,256,128]{2,1,0:T(8,128)}, f32[8,256,128]{2,1,0:T(8,128)S(1)}, u32[]{:S(2)}) copy-start(f32[8,256,128]{2,1,0:T(8,128)S(1)} %all-to-all-done.moments_ref) | copy-start | bytes 3145732
  26.7 16.7 %all-to-all-start.2 = ((f32[8,128,128]{2,1,0:T(8,128)}), f32[8,128,128]{2,1,0:T(8,128)S(1)}, u32[]{:S(2)}, u32[]{:S(2)}) async-start(f32[8,128,128]{2,1,0:T(8,128)} %get-tuple-element.29), calls=%async_computation.2 | async-start | bytes 1048576 | tf_op jit(solution)/shard_map/all_to_all | solution.py:192
  33.8 6.4 %collective-permute-start = (f32[128,128]{1,0:T(8,128)S(1)}, f32[128,128]{1,0:T(8,128)S(1)}, u32[]{:S(2)}, u32[]{:S(2)}) collective-permute-start(f32[128,128]{1,0:T(8,128)S(1)} %slice_bitcast_fusion), channel_id=1, source_target_pairs={{0,16},{2,18},{4,20},{6,22},{8,24},{10,26},{12,28},{14,30},{1,17},... | collective-permute-start | bytes 196616 | tf_op jit(solution)/shard_map/ppermute | solution.py:234
  40.2 0.6 copy-start.4
  43.4 5.6 %copy-start.2 = (f32[8,128,128]{2,1,0:T(8,128)}, f32[8,128,128]{2,1,0:T(8,128)S(1)}, u32[]{:S(2)}) copy-start(f32[8,128,128]{2,1,0:T(8,128)S(1)} %all-to-all-done.2.d_ref) | copy-start | bytes 1572868
  43.4 17.7 %all-to-all-start.1 = ((f32[8,128,128]{2,1,0:T(8,128)}), f32[8,128,128]{2,1,0:T(8,128)S(1)}, u32[]{:S(2)}, u32[]{:S(2)}) async-start(f32[8,128,128]{2,1,0:T(8,128)} %get-tuple-element.28), calls=%async_computation.1 | async-start | bytes 1048576 | tf_op jit(solution)/shard_map/all_to_all | solution.py:192
  51.1 7.5 %collective-permute-start.1 = (f32[128,128]{1,0:T(8,128)}, f32[128,128]{1,0:T(8,128)S(1)}, u32[]{:S(2)}, u32[]{:S(2)}) collective-permute-start(f32[128,128]{1,0:T(8,128)} %get-tuple-element.32), channel_id=1, source_target_pairs={{0,16},{2,18},{4,20},{6,22},{8,24},{10,26},{12,28},{14,30},{1,17},... | collective-permute-start | bytes 196616 | tf_op jit(solution)/shard_map/ppermute | solution.py:251
  58.6 0.6 copy-start.5
  61.2 5.7 %copy-start.3 = (f32[8,128,128]{2,1,0:T(8,128)}, f32[8,128,128]{2,1,0:T(8,128)S(1)}, u32[]{:S(2)}) copy-start(f32[8,128,128]{2,1,0:T(8,128)S(1)} %all-to-all-done.1.s_ref) | copy-start | bytes 1572868
  61.2 17.5 %all-to-all-start.3 = ((f32[8,128,128]{2,1,0:T(8,128)}), f32[8,128,128]{2,1,0:T(8,128)S(1)}, u32[]{:S(2)}, u32[]{:S(2)}) async-start(f32[8,128,128]{2,1,0:T(8,128)} %owner_add.1), calls=%async_computation.3 | async-start | bytes 1048576 | tf_op jit(solution)/shard_map/all_to_all | solution.py:192
  78.7 0.8 copy-start.1
  85.3 1.4 %collective-permute-start.2 = (f32[8,1024]{1,0:T(8,128)}, f32[8,1024]{1,0:T(8,128)S(1)}, u32[]{:S(2)}, u32[]{:S(2)}) collective-permute-start(f32[8,1024]{1,0:T(8,128)} %get-tuple-element.34.mine_ref), channel_id=1, source_target_pairs={{0,1},{1,0},{2,3},{3,2},{4,5},{5,4},{6,7},{7,6},{8,9},{9,8},{10,11... | collective-permute-start | bytes 98312 | tf_op jit(solution)/shard_map/ppermute | solution.py:287
  86.7 0.6 copy-start.6

commit v3 on v2

v3 whole, which is shorter than its diff:
```python
import functools

import jax
import jax.numpy as jnp
from jax import lax
from jax.experimental import pallas as pl
from jax.experimental.pallas import tpu as pltpu
from jax.sharding import PartitionSpec as P

BLK = 128
CHUNK = 256
PAIR = 2
SMALL = 8 * 1024 * 1024
LARGE = 60 * 1024 * 1024

epsilon = 1e-06
f32, bf16 = jnp.float32, jnp.bfloat16

NN = (((1,), (0,)), ((), ()))
NT = (((1,), (1,)), ((), ()))
TN = (((0,), (0,)), ((), ()))


def dot(a, b, dims=NN):
    return lax.dot_general(a, b, dims, preferred_element_type=f32)


def split(a):
    high = a.astype(bf16)
    return high, (a - high.astype(f32)).astype(bf16)


def lanes(*parts):
    return jnp.concatenate(parts, axis=1)


def rows(*parts):
    return jnp.concatenate(parts, axis=0)


def dot_f32(a, b):
    a_high, a_low = split(a)
    b_high, b_low = split(b)
    return dot(lanes(a_high, a_low), rows(b_high, b_high)) + dot(a_high, b_low)


def ordered(size):
    shape = (size, size)
    return lax.broadcasted_iota(jnp.int32, shape, 0) - lax.broadcasted_iota(jnp.int32, shape, 1)


def span(j, size=BLK):
    return slice(j * size, (j + 1) * size)


def columns(p):
    return pl.ds(pl.multiple_of(p * PAIR * BLK, PAIR * BLK), PAIR * BLK)


def copies(moves, sems, p):
    return [
        pltpu.make_async_copy(source(p), target(p), sems.at[n, p])
        for n, (source, target) in enumerate(moves)
    ]


def streamed(pairs, reads, writes, read_sems, write_sems, body):
    for p in range(pairs):
        for copy in copies(reads, read_sems, p):
            copy.start()

    @pl.loop(0, pairs)
    def _(p):
        for copy in copies(reads, read_sems, p):
            copy.wait()
        body(p)
        for copy in copies(writes, write_sems, p):
            copy.start()

    for p in range(pairs):
        for copy in copies(writes, write_sems, p):
            copy.wait()


def by_columns(hbm):
    return lambda p: hbm.at[:, columns(p)]


def by_pair(ref):
    return lambda p: ref.at[p]


def moments_kernel(q_hbm, k_hbm, v_hbm, m_hbm, kt_hbm, vt_hbm, q_ref, k_ref, v_ref, m_ref, kt_ref, vt_ref, *sems):
    def body(p):
        for j in range(PAIR):
            k = k_ref[p, :, span(j)]
            kt, vt = k.T, v_ref[p, :, span(j)].T
            kt_ref[p, span(j)], vt_ref[p, span(j)] = kt, vt
            m_ref[p, j, :BLK] = dot(kt, k)
            m_ref[p, j, BLK:] = dot(vt, q_ref[p, :, span(j)])

    reads = [(by_columns(a), by_pair(b)) for a, b in ((k_hbm, k_ref), (v_hbm, v_ref), (q_hbm, q_ref))]
    writes = [(by_pair(a), by_pair(b)) for a, b in ((kt_ref, kt_hbm), (vt_ref, vt_hbm), (m_ref, m_hbm))]
    streamed(q_ref.shape[0], reads, writes, *sems, body)


def first_stage_kernel(
    q_hbm, k_hbm, kt_hbm, vt_hbm, r_hbm, d_hbm, qt_hbm, q_ref, k_ref, kt_ref, vt_ref, r_ref, d_ref, qt_ref, *sems
):
    steps = q_ref.shape[1] // CHUNK
    mask = ordered(CHUNK) >= 0

    def body(p):
        states = [jnp.zeros((BLK, BLK), f32)] * PAIR
        for i in range(steps):
            at = span(i, CHUNK)
            for j in range(PAIR):
                q, k, kt = q_ref[p, at, span(j)], k_ref[p, at, span(j)], kt_ref[p, span(j), at]
                qt_ref[p, span(j), at] = q.T
                r = dot(lanes(*split(jnp.where(mask, dot(q, kt), 0.0))), rows(k, k))
                if i > 0:
                    r = r + dot(lanes(q, q), rows(*split(states[j])))
                if i + 1 < steps:
                    states[j] = states[j] + dot(kt, k)
                r_ref[p, j, at] = lanes(*split(r))
        for j in range(PAIR):
            d = dot(vt_ref[p, span(j)], r_ref[p, j])
            d_ref[p, j] = d[:, :BLK] + d[:, BLK:]

    reads = [(by_columns(a), by_pair(b)) for a, b in ((q_hbm, q_ref), (k_hbm, k_ref))]
    reads += [(by_pair(a), by_pair(b)) for a, b in ((kt_hbm, kt_ref), (vt_hbm, vt_ref))]
    writes = [(by_pair(a), by_pair(b)) for a, b in ((r_ref, r_hbm), (d_ref, d_hbm), (qt_ref, qt_hbm))]
    streamed(q_ref.shape[0], reads, writes, *sems, body)


def second_stage_kernel(
    q_hbm, qt_hbm, vt_hbm, r_hbm, s_hbm, num_hbm, q_ref, qt_ref, vt_ref, r_ref, s_ref, num_ref, *sems
):
    steps = q_ref.shape[1] // CHUNK
    mask = ordered(CHUNK) <= 0

    def body(p):
        states = [jnp.zeros((BLK, BLK), f32)] * PAIR
        s_both = [rows(*split(s_ref[p, j])) for j in range(PAIR)]
        for i in range(steps):
            at = span(i, CHUNK)
            for j in range(PAIR):
                q, qt, vt = q_ref[p, at, span(j)], qt_ref[p, span(j), at], vt_ref[p, span(j), at]
                qt2 = rows(qt, qt)
                pair = r_ref[p, j, at].astype(f32)
                r = lanes(*split(pair[:, :BLK] + pair[:, BLK:] + dot(lanes(q, q), s_both[j])))
                num = dot(lanes(vt, vt), rows(*split(jnp.where(mask, dot(r, qt2), 0.0))))
                if i > 0:
                    num = num + dot(lanes(*split(states[j])), qt2)
                num_ref[p, span(j), at] = num
                if i + 1 < steps:
                    d = dot(vt, r)
                    states[j] = states[j] + d[:, :BLK] + d[:, BLK:]

    reads = [(by_columns(q_hbm), by_pair(q_ref))]
    reads += [
        (by_pair(a), by_pair(b))
        for a, b in ((s_hbm, s_ref), (r_hbm, r_ref), (qt_hbm, qt_ref), (vt_hbm, vt_ref))
    ]
    streamed(q_ref.shape[0], reads, [(by_pair(num_ref), by_pair(num_hbm))], *sems, body)


def owner_local_kernel(moments_ref, s_ref, c_ref, f_ref):
    members = moments_ref.shape[0]
    s = jnp.zeros((BLK, BLK), f32)
    c = jnp.zeros((BLK, BLK), f32)
    f = jnp.zeros((BLK, BLK), f32)
    for m in range(members):
        s_ref[m], c_ref[m], f_ref[m] = s, c, f
        c_own = moments_ref[m, BLK:]
        if m > 0:
            f = f + dot_f32(c_own, s)
        s = s + moments_ref[m, :BLK]
        c = c + c_own
    s_ref[members], c_ref[members], f_ref[members] = s, c, f


def owner_shift_kernel(s_ref, c_ref, f_ref, before_ref, back_ref, out_ref):
    members = back_ref.shape[0]
    before = before_ref[...]
    for m in range(members):
        back_ref[m] = s_ref[m] + before
    out_ref[0] = f_ref[0]
    for m in range(1, members + 1):
        out_ref[m] = f_ref[m] + dot_f32(c_ref[m], before)


def owner_sum_kernel(d_ref, h_ref, base_ref, total_ref):
    members = d_ref.shape[0]
    d = jnp.zeros((BLK, BLK), f32)
    for m in range(members):
        base_ref[m] = h_ref[m] + d
        d = d + d_ref[m]
    total_ref[...] = h_ref[members] + d


def add_kernel(base_ref, before_ref, out_ref):
    for m in range(out_ref.shape[0]):
        out_ref[m] = base_ref[m] + before_ref[...]


def scale_kernel(
    qt_hbm, num_hbm, d_hbm, gain_ref, scale_ref, y_hbm, part_ref, qt_ref, num_ref, d_ref, y_ref, *sems
):
    pairs, _, tokens = qt_ref.shape
    part_ref[...] = jnp.zeros_like(part_ref)

    def body(p):
        part = part_ref[...]
        for j in range(PAIR):
            h = p * PAIR + j
            qt = qt_ref[p, span(j)]
            y = (num_ref[p, span(j)] + dot(lanes(*split(d_ref[p, j])), rows(qt, qt))) * scale_ref[h]
            part = part + jnp.sum((y * y).reshape(BLK // 8, 8, tokens), axis=0)
            gain = jnp.broadcast_to(gain_ref[h], (BLK, BLK)).T
            for i in range(tokens // BLK):
                y_ref[p, span(j), span(i)] = y[:, span(i)] * gain
        part_ref[...] = part

    reads = [(by_pair(a), by_pair(b)) for a, b in ((d_hbm, d_ref), (qt_hbm, qt_ref), (num_hbm, num_ref))]
    streamed(pairs, reads, [(by_pair(y_ref), by_pair(y_hbm))], *sems, body)


def norm_kernel(features, y_hbm, mine_hbm, other_hbm, out_hbm, y_ref, parts_ref, out_ref, y_sems, part_sems, sems):
    pairs, wide, tokens = y_ref.shape
    steps = tokens // CHUNK

    def y_copy(i):
        at = span(i, CHUNK)
        return pltpu.make_async_copy(y_hbm.at[:, :, at], y_ref.at[:, :, at], y_sems.at[i])

    def out_copy(i):
        at = span(i, CHUNK)
        return pltpu.make_async_copy(out_ref.at[at], out_hbm.at[at], sems.at[i])

    def part_copy(n):
        return pltpu.make_async_copy((mine_hbm, other_hbm)[n], parts_ref.at[n], part_sems.at[n])

    part_copy(0).start()
    part_copy(1).start()
    for i in range(steps):
        y_copy(i).start()
    part_copy(0).wait()
    part_copy(1).wait()
    total = jnp.sum(parts_ref[0] + parts_ref[1], axis=0, keepdims=True)
    inv = lax.rsqrt(total * (1.0 / features) + epsilon)
    for i in range(steps):
        at = span(i, CHUNK)
        y_copy(i).wait()
        for p in range(pairs):
            out_ref[at, span(p, wide)] = (y_ref[p, :, at] * inv[:, at]).astype(bf16).T
        out_copy(i).start()
    for i in range(steps):
        out_copy(i).wait()


def params(limit=SMALL):
    return pltpu.CompilerParams(vmem_limit_bytes=limit)


def cost(us, moved):
    return pl.CostEstimate(flops=int(us * 4e8), bytes_accessed=int(moved), transcendentals=0)


def per_device(query_rows, key_rows, value_rows, head_scale, out_gain):
    tokens, width = query_rows.shape
    heads = head_scale.shape[0]
    seq = lax.axis_size("seq")
    members = heads
    groups = seq // members
    index_groups = [[g * members + m for m in range(members)] for g in range(groups)]
    onward = [(i, i + members) for i in range(seq - members)]

    def swap(a):
        return lax.all_to_all(a, "seq", 0, 0, axis_index_groups=index_groups)

    mats = lambda n: jax.ShapeDtypeStruct((n, BLK, BLK), f32)
    mat = jax.ShapeDtypeStruct((BLK, BLK), f32)
    pairs = heads // PAIR
    shape = jax.ShapeDtypeStruct
    upright = shape((pairs, tokens, PAIR * BLK), bf16)
    turned = shape((pairs, PAIR * BLK, tokens), bf16)
    turned_f32 = shape((pairs, PAIR * BLK, tokens), f32)
    twofold = shape((pairs, PAIR, tokens, 2 * BLK), bf16)
    pair_mats = shape((pairs, PAIR, BLK, BLK), f32)
    moment_mats = shape((pairs, PAIR, 2 * BLK, BLK), f32)
    in_hbm = pl.BlockSpec(memory_space=pltpu.HBM)

    def buffers(reads, writes):
        sems = [pltpu.SemaphoreType.DMA((len(a), pairs)) for a in (reads, writes)]
        return [pltpu.VMEM(a.shape, a.dtype) for a in reads + writes] + sems

    def stream_call(kernel, reads, writes, us, name):
        return pl.pallas_call(
            kernel,
            in_specs=[in_hbm] * len(reads),
            out_specs=[in_hbm] * len(writes),
            out_shape=writes,
            scratch_shapes=buffers(reads, writes),
            compiler_params=params(LARGE),
            cost_estimate=cost(us, 10 * tokens * width),
            name=name,
        )

    moments, k_t, v_t = pl.pallas_call(
        moments_kernel,
        in_specs=[in_hbm] * 3,
        out_specs=[in_hbm] * 3,
        out_shape=[moment_mats, turned, turned],
        scratch_shapes=buffers([upright] * 3, [moment_mats, turned, turned]),
        compiler_params=params(LARGE),
        name="moments",
    )(query_rows, key_rows, value_rows)
    moments_in = swap(moments.reshape(heads, 2 * BLK, BLK))

    r_local, d_local, q_t = stream_call(
        first_stage_kernel, [upright, upright, turned, turned], [twofold, pair_mats, turned], 10, "first_stage"
    )(query_rows, key_rows, k_t, v_t)
    d_in = swap(d_local.reshape(heads, BLK, BLK))

    s_part, c_part, f_part = pl.pallas_call(
        owner_local_kernel,
        out_shape=[mats(members + 1)] * 3,
        compiler_params=params(),
        name="owner_local",
    )(moments_in)
    s_before = jnp.zeros((BLK, BLK), f32)
    for _ in range(groups - 1):
        s_before = lax.ppermute(s_before + s_part[members], "seq", onward)
    s_back, h_part = pl.pallas_call(
        owner_shift_kernel,
        out_shape=[mats(members), mats(members + 1)],
        compiler_params=params(),
        name="owner_shift",
    )(s_part, c_part, f_part, s_before)
    s_pre = swap(s_back)

    d_base, d_total = pl.pallas_call(
        owner_sum_kernel,
        out_shape=[mats(members), mat],
        compiler_params=params(),
        name="owner_sum",
    )(d_in, h_part)
    d_before = jnp.zeros((BLK, BLK), f32)
    for _ in range(groups - 1):
        d_before = lax.ppermute(d_before + d_total, "seq", onward)
    d_back = pl.pallas_call(
        add_kernel, out_shape=mats(members), compiler_params=params(), name="owner_add"
    )(d_base, d_before)
    d_pre = swap(d_back)

    (num,) = stream_call(
        second_stage_kernel, [upright, turned, turned, twofold, pair_mats], [turned_f32], 10, "second_stage"
    )(query_rows, q_t, v_t, r_local, s_pre.reshape(pair_mats.shape))

    in_vmem = pl.BlockSpec(memory_space=pltpu.VMEM)
    part_shape = shape((8, tokens), f32)
    y, part = pl.pallas_call(
        scale_kernel,
        in_specs=[in_hbm] * 3 + [in_vmem, pl.BlockSpec(memory_space=pltpu.SMEM)],
        out_specs=[in_hbm, in_vmem],
        out_shape=[turned_f32, part_shape],
        scratch_shapes=buffers([turned, turned_f32, pair_mats], [turned_f32]),
        compiler_params=params(LARGE),
        name="scale_squares",
    )(q_t, num, d_pre.reshape(pair_mats.shape), out_gain.reshape(heads, 1, BLK), head_scale)
    shards = lax.axis_size("head")
    other = jnp.zeros_like(part)
    for turn in range(1, shards):
        other = other + lax.ppermute(part, "head", [(i, (i + turn) % shards) for i in range(shards)])
    steps = tokens // CHUNK
    return pl.pallas_call(
        functools.partial(norm_kernel, width * shards),
        in_specs=[in_hbm] * 3,
        out_specs=in_hbm,
        out_shape=shape((tokens, width), bf16),
        scratch_shapes=[
            pltpu.VMEM(turned_f32.shape, f32),
            pltpu.VMEM((2, 8, tokens), f32),
            pltpu.VMEM((tokens, width), bf16),
            pltpu.SemaphoreType.DMA((steps,)),
            pltpu.SemaphoreType.DMA((2,)),
            pltpu.SemaphoreType.DMA((steps,)),
        ],
        compiler_params=params(LARGE),
        name="norm",
    )(y, part, other)


def solution(mesh):
    return jax.shard_map(
        per_device,
        mesh=mesh,
        in_specs=(P("seq", "head"), P("seq", "head"), P("seq", "head"), P("head"), P("head")),
        out_specs=P("seq", "head"),
        check_vma=False,
    )
```

time: 92.8 us -> 82.1 us (0.88)
  Pallas kernels: 48.5 us -> 40.3 us
  local copies, waits for them, and re-layouts: 3.49 us -> 1.4 us
  starting transfers between devices: 30.7 us -> 29.4 us
    pallas_call x1, Pallas kernels: 2.73 us -> 0.38 us  [per_device(): pl.pallas_call(owner_local_kernel, out_shape=[mats(members + 1)] * 3, com...]
    pallas_call x1, Pallas kernels: 2.08 us -> 0.06 us  [per_device(): pl.pallas_call(owner_sum_kernel, out_shape=[mats(members), mat], compiler...]
    pallas_call x1, Pallas kernels: 2.63 us -> 0.85 us  [per_device(): pl.pallas_call(owner_shift_kernel, out_shape=[mats(members), mats(members...]
    all_to_all x4, starting transfers between devices: 20.9 us -> 19.6 us  [swap(): return lax.all_to_all(a, 'seq', 0, 0, axis_index_groups=index_groups)]
    unnamed x14 -> x6, local copies, waits for them, and re-layouts: 2.65 us -> 1.39 us
    pallas_call x1, Pallas kernels: 1.93 us -> 0.88 us  [per_device(): pl.pallas_call(add_kernel, out_shape=mats(members), compiler_params=param...]
  transfers between devices with their start and end apart: 7 -> 7, of which waited for: 4 -> 5; matrix products, arithmetic and copies ran while one was open for 1% -> 0% of each run, Pallas kernels for 35% -> 31%
where the time goes in v3:
time: 82.1 us; the launch traced here: 81.4 us
  Pallas kernels  40.3 us (49%)
  starting transfers between devices  29.4 us (36%)
  waiting for transfers between devices  10.1 us (12%)
  local copies, waits for them, and re-layouts  1.4 us (2%)
    all_to_all x4, starting transfers between devices, swap(): return lax.all_to_all(a, 'seq', 0, 0, axis_index_groups=index_groups)  19.6 us
    pallas_call x1, Pallas kernels, per_device(): stream_call(second_stage_kernel, [upright, turned, turned, twofold, pair_...  12 us
    pallas_call x1, Pallas kernels, per_device(): stream_call(first_stage_kernel, [upright, upright, turned, turned], [twof...  11.2 us
    pallas_call x1, Pallas kernels, per_device(): pl.pallas_call(scale_kernel, in_specs=[in_hbm] * 3 + [in_vmem, pl.BlockSp...  6.4 us
    ppermute x1, starting transfers between devices, per_device(): d_before = lax.ppermute(d_before + d_total, 'seq', onward)  5.26 us
    pallas_call x1, Pallas kernels, per_device(): pl.pallas_call(moments_kernel, in_specs=[in_hbm] * 3, out_specs=[in_hbm]...  5.16 us
    all_to_all x4, waiting for transfers between devices, swap(): return lax.all_to_all(a, 'seq', 0, 0, axis_index_groups=index_groups)  4.61 us
    ppermute x1, starting transfers between devices, per_device(): s_before = lax.ppermute(s_before + s_part[members], 'seq', onward)  4.5 us
  transfers between devices with their start and end apart: 7, of which 5 were waited for; matrix products, arithmetic and copies ran while one was open for 0% of the time, Pallas kernels for 31%

profile of v3, /device:TPU:0, one launch (start us, length us, event | category | flops | bytes accessed | tf_op | source)
XLA Modules:
  0.0 81.4 jit_solution(10602915006438042861)
XLA Ops:
  0.0 5.2 %moments.1 = (f32[4,2,256,128]{3,2,1,0:T(8,128)}, bf16[4,256,1024]{2,1,0:T(8,128)(2,1)}, bf16[4,256,1024]{2,1,0:T(8,128)(2,1)}) custom-call(bf16[1024,1024]{1,0:T(8,128)(2,1)} %q_hbm.5, bf16[1024,1024]{1,0:T(8,128)(2,1)} %k_hbm.3, bf16[1024,1024]{1,0:T(8,128)(2,1)} %v_hbm.1), custom_call_target="tpu_custom_call" | custom-call | tf_op jit(solution)/shard_map/moments/pallas_call | solution.py:310
  5.2 6.2 %all-to-all-start = ((f32[8,256,128]{2,1,0:T(8,128)}), f32[8,256,128]{2,1,0:T(8,128)S(1)}, u32[]{:S(2)}, u32[]{:S(2)}) async-start(f32[8,256,128]{2,1,0:T(8,128)} %bitcast.9), calls=%async_computation | async-start | bytes 2097152 | tf_op jit(solution)/shard_map/all_to_all | solution.py:280
  11.4 11.2 %first_stage.1 = (bf16[4,2,1024,256]{3,2,1,0:T(8,128)(2,1)}, f32[4,2,128,128]{3,2,1,0:T(8,128)}, bf16[4,256,1024]{2,1,0:T(8,128)(2,1)}) custom-call(bf16[1024,1024]{1,0:T(8,128)(2,1)} %q_hbm.5, bf16[1024,1024]{1,0:T(8,128)(2,1)} %k_hbm.3, bf16[4,256,1024]{2,1,0:T(8,128)(2,1)} %get-tuple-element.20.kt_hbm, bf16[4,256,1024]{2,1,0:T(8,128)(2,1)} %get-tuple-element.21.vt_hbm), custom_call_target="tpu_custom_call" | custom-call | flops 4000000000 | bytes 10485760 | tf_op jit(solution)/shard_map/first_stage/pallas_call | solution.py:321
  22.5 3.5 %all-to-all-done.moments_ref = f32[8,256,128]{2,1,0:T(8,128)S(1)} async-done(((f32[8,256,128]{2,1,0:T(8,128)}), f32[8,256,128]{2,1,0:T(8,128)S(1)}, u32[]{:S(2)}, u32[]{:S(2)}) %all-to-all-start) | async-done | bytes 1048608 | tf_op jit(solution)/shard_map/all_to_all | solution.py:280
  26.1 3.5 %all-to-all-start.2 = ((f32[8,128,128]{2,1,0:T(8,128)}), f32[8,128,128]{2,1,0:T(8,128)S(1)}, u32[]{:S(2)}, u32[]{:S(2)}) async-start(f32[8,128,128]{2,1,0:T(8,128)} %bitcast.10), calls=%async_computation.2 | async-start | bytes 1048576 | tf_op jit(solution)/shard_map/all_to_all | solution.py:280
  29.6 0.4 owner_local.1
  30.0 4.5 %collective-permute-start = (f32[128,128]{1,0:T(8,128)S(1)}, f32[128,128]{1,0:T(8,128)S(1)}, u32[]{:S(2)}, u32[]{:S(2)}) collective-permute-start(f32[128,128]{1,0:T(8,128)S(1)} %slice_bitcast_fusion), channel_id=1, source_target_pairs={{0,16},{2,18},{4,20},{6,22},{8,24},{10,26},{12,28},{14,30},{1,17},... | collective-permute-start | bytes 196616 | tf_op jit(solution)/shard_map/ppermute | solution.py:334
  34.5 2.2 %collective-permute-done.before_ref = f32[128,128]{1,0:T(8,128)S(1)} collective-permute-done((f32[128,128]{1,0:T(8,128)S(1)}, f32[128,128]{1,0:T(8,128)S(1)}, u32[]{:S(2)}, u32[]{:S(2)}) %collective-permute-start) | collective-permute-done | bytes 65568 | tf_op jit(solution)/shard_map/ppermute | solution.py:334
  36.7 0.8 %owner_shift.1 = (f32[8,128,128]{2,1,0:T(8,128)}, f32[9,128,128]{2,1,0:T(8,128)S(1)}) custom-call(f32[9,128,128]{2,1,0:T(8,128)S(1)} %get-tuple-element.25.s_ref, f32[9,128,128]{2,1,0:T(8,128)S(1)} %get-tuple-element.26.c_ref, f32[9,128,128]{2,1,0:T(8,128)S(1)} %get-tuple-element.27.f_ref, f32[128,128]{1,0:T(8,128)S(1)} %collective-permute-done.before_ref), custom_call_target="tpu_custom_call" | custom-call | tf_op jit(solution)/shard_map/owner_shift/pallas_call | solution.py:335
  37.5 1.1 %all-to-all-done.2.d_ref = f32[8,128,128]{2,1,0:T(8,128)S(1)} async-done(((f32[8,128,128]{2,1,0:T(8,128)}), f32[8,128,128]{2,1,0:T(8,128)S(1)}, u32[]{:S(2)}, u32[]{:S(2)}) %all-to-all-start.2) | async-done | bytes 524320 | tf_op jit(solution)/shard_map/all_to_all | solution.py:280
  38.6 4.3 %all-to-all-start.1 = ((f32[8,128,128]{2,1,0:T(8,128)}), f32[8,128,128]{2,1,0:T(8,128)S(1)}, u32[]{:S(2)}, u32[]{:S(2)}) async-start(f32[8,128,128]{2,1,0:T(8,128)} %get-tuple-element.28), calls=%async_computation.1 | async-start | bytes 1048576 | tf_op jit(solution)/shard_map/all_to_all | solution.py:280
  42.8 0.1 owner_sum.1
  42.9 5.3 %collective-permute-start.1 = (f32[128,128]{1,0:T(8,128)S(1)}, f32[128,128]{1,0:T(8,128)S(1)}, u32[]{:S(2)}, u32[]{:S(2)}) collective-permute-start(f32[128,128]{1,0:T(8,128)S(1)} %get-tuple-element.32), channel_id=1, source_target_pairs={{0,16},{2,18},{4,20},{6,22},{8,24},{10,26},{12,28},{14,30},{1,17},... | collective-permute-start | bytes 196616 | tf_op jit(solution)/shard_map/ppermute | solution.py:351
  48.2 1.9 %collective-permute-done.1.before_ref = f32[128,128]{1,0:T(8,128)S(1)} collective-permute-done((f32[128,128]{1,0:T(8,128)S(1)}, f32[128,128]{1,0:T(8,128)S(1)}, u32[]{:S(2)}, u32[]{:S(2)}) %collective-permute-start.1) | collective-permute-done | bytes 65568 | tf_op jit(solution)/shard_map/ppermute | solution.py:351
  50.1 0.9 %owner_add.1 = f32[8,128,128]{2,1,0:T(8,128)} custom-call(f32[8,128,128]{2,1,0:T(8,128)S(1)} %get-tuple-element.31.base_ref, f32[128,128]{1,0:T(8,128)S(1)} %collective-permute-done.1.before_ref), custom_call_target="tpu_custom_call" | custom-call | tf_op jit(solution)/shard_map/owner_add/pallas_call | solution.py:352
  50.9 5.7 %all-to-all-start.3 = ((f32[8,128,128]{2,1,0:T(8,128)}), f32[8,128,128]{2,1,0:T(8,128)S(1)}, u32[]{:S(2)}, u32[]{:S(2)}) async-start(f32[8,128,128]{2,1,0:T(8,128)} %owner_add.1), calls=%async_computation.3 | async-start | bytes 1048576 | tf_op jit(solution)/shard_map/all_to_all | solution.py:280
  56.6 12.0 %second_stage.1.num_hbm = f32[4,256,1024]{2,1,0:T(8,128)} custom-call(bf16[1024,1024]{1,0:T(8,128)(2,1)} %q_hbm.5, bf16[4,256,1024]{2,1,0:T(8,128)(2,1)} %get-tuple-element.22.qt_hbm, bf16[4,256,1024]{2,1,0:T(8,128)(2,1)} %get-tuple-element.21.vt_hbm, bf16[4,2,1024,256]{3,2,1,0:T(8,128)(2,1)} %get-tuple-element.23.r_hbm, f32[4,2,128,128]{3,2,1,0:T(8,128)} %bitcast.8), custom_call_target="tpu_custom_call" | custom-call | flops 4000000000 | bytes 10485760 | tf_op jit(solution)/shard_map/second_stage/pallas_call | solution.py:357
  68.6 0.0 copy-start
  68.6 0.8 copy-done
  69.4 6.4 %scale_squares.1 = (f32[4,256,1024]{2,1,0:T(8,128)}, f32[8,1024]{1,0:T(8,128)}) custom-call(bf16[4,256,1024]{2,1,0:T(8,128)(2,1)} %get-tuple-element.22.qt_hbm, f32[4,256,1024]{2,1,0:T(8,128)} %second_stage.1.num_hbm, f32[4,2,128,128]{3,2,1,0:T(8,128)} %bitcast.7, f32[8,1,128]{2,1,0:T(1,128)} %bitcast.11, f32[8]{0:T(128)} %scale_ref.1), custom_call_target="tpu_custom_call" | custom-call | tf_op jit(solution)/shard_map/scale_squares/pallas_call | solution.py:363
  75.8 0.1 collective-permute-start.2
  75.9 1.4 %collective-permute-done.2.other_hbm = f32[8,1024]{1,0:T(8,128)S(1)} collective-permute-done((f32[8,1024]{1,0:T(8,128)}, f32[8,1024]{1,0:T(8,128)S(1)}, u32[]{:S(2)}, u32[]{:S(2)}) %collective-permute-start.2) | collective-permute-done | bytes 32800 | tf_op jit(solution)/shard_map/ppermute | solution.py:375
  77.3 0.6 copy-done.2
  77.9 3.5 %norm.1 = bf16[1024,1024]{1,0:T(8,128)(2,1)} custom-call(f32[4,256,1024]{2,1,0:T(8,128)} %get-tuple-element.33.y_hbm, f32[8,1024]{1,0:T(8,128)} %get-tuple-element.34.mine_hbm, f32[8,1024]{1,0:T(8,128)} %copy-done.2), custom_call_target="tpu_custom_call" | custom-call | tf_op jit(solution)/shard_map/norm/pallas_call | solution.py:377
  (6 shorter events, 0.0 us)
Async XLA Ops:
  5.2 20.9 %all-to-all-start = ((f32[8,256,128]{2,1,0:T(8,128)}), f32[8,256,128]{2,1,0:T(8,128)S(1)}, u32[]{:S(2)}, u32[]{:S(2)}) async-start(f32[8,256,128]{2,1,0:T(8,128)} %bitcast.9), calls=%async_computation | async-start | bytes 2097152 | tf_op jit(solution)/shard_map/all_to_all | solution.py:280
  26.1 12.5 %all-to-all-start.2 = ((f32[8,128,128]{2,1,0:T(8,128)}), f32[8,128,128]{2,1,0:T(8,128)S(1)}, u32[]{:S(2)}, u32[]{:S(2)}) async-start(f32[8,128,128]{2,1,0:T(8,128)} %bitcast.10), calls=%async_computation.2 | async-start | bytes 1048576 | tf_op jit(solution)/shard_map/all_to_all | solution.py:280
  30.0 6.7 %collective-permute-start = (f32[128,128]{1,0:T(8,128)S(1)}, f32[128,128]{1,0:T(8,128)S(1)}, u32[]{:S(2)}, u32[]{:S(2)}) collective-permute-start(f32[128,128]{1,0:T(8,128)S(1)} %slice_bitcast_fusion), channel_id=1, source_target_pairs={{0,16},{2,18},{4,20},{6,22},{8,24},{10,26},{12,28},{14,30},{1,17},... | collective-permute-start | bytes 196616 | tf_op jit(solution)/shard_map/ppermute | solution.py:334
  38.6 12.3 %all-to-all-start.1 = ((f32[8,128,128]{2,1,0:T(8,128)}), f32[8,128,128]{2,1,0:T(8,128)S(1)}, u32[]{:S(2)}, u32[]{:S(2)}) async-start(f32[8,128,128]{2,1,0:T(8,128)} %get-tuple-element.28), calls=%async_computation.1 | async-start | bytes 1048576 | tf_op jit(solution)/shard_map/all_to_all | solution.py:280
  42.9 7.1 %collective-permute-start.1 = (f32[128,128]{1,0:T(8,128)S(1)}, f32[128,128]{1,0:T(8,128)S(1)}, u32[]{:S(2)}, u32[]{:S(2)}) collective-permute-start(f32[128,128]{1,0:T(8,128)S(1)} %get-tuple-element.32), channel_id=1, source_target_pairs={{0,16},{2,18},{4,20},{6,22},{8,24},{10,26},{12,28},{14,30},{1,17},... | collective-permute-start | bytes 196616 | tf_op jit(solution)/shard_map/ppermute | solution.py:351
  50.9 5.7 %copy-start.1 = (f32[8,128,128]{2,1,0:T(8,128)}, f32[8,128,128]{2,1,0:T(8,128)S(1)}, u32[]{:S(2)}) copy-start(f32[8,128,128]{2,1,0:T(8,128)S(1)} %all-to-all-done.1) | copy-start | bytes 1572868
  50.9 17.7 %all-to-all-start.3 = ((f32[8,128,128]{2,1,0:T(8,128)}), f32[8,128,128]{2,1,0:T(8,128)S(1)}, u32[]{:S(2)}, u32[]{:S(2)}) async-start(f32[8,128,128]{2,1,0:T(8,128)} %owner_add.1), calls=%async_computation.3 | async-start | bytes 1048576 | tf_op jit(solution)/shard_map/all_to_all | solution.py:280
  68.6 0.8 copy-start
  75.8 1.5 %collective-permute-start.2 = (f32[8,1024]{1,0:T(8,128)}, f32[8,1024]{1,0:T(8,128)S(1)}, u32[]{:S(2)}, u32[]{:S(2)}) collective-permute-start(f32[8,1024]{1,0:T(8,128)} %get-tuple-element.34.mine_hbm), channel_id=1, source_target_pairs={{0,1},{1,0},{2,3},{3,2},{4,5},{5,4},{6,7},{7,6},{8,9},{9,8},{10,11... | collective-permute-start | bytes 98312 | tf_op jit(solution)/shard_map/ppermute | solution.py:375
  77.3 0.6 copy-start.2

commit v4 on v3

--- a/solution.py
+++ b/solution.py
@@ -65,14 +65,19 @@
 
 
 def streamed(pairs, reads, writes, read_sems, write_sems, body):
-    for p in range(pairs):
-        for copy in copies(reads, read_sems, p):
-            copy.start()
+    for copy in copies(reads, read_sems, 0):
+        copy.start()
 
     @pl.loop(0, pairs)
     def _(p):
         for copy in copies(reads, read_sems, p):
             copy.wait()
+
+        @pl.when(p + 1 < pairs)
+        def _():
+            for copy in copies(reads, read_sems, p + 1):
+                copy.start()
+
         body(p)
         for copy in copies(writes, write_sems, p):
             copy.start()
@@ -180,9 +185,13 @@
     s_ref[members], c_ref[members], f_ref[members] = s, c, f
 
 
+def masked(ref, members):
+    return jnp.where(lax.axis_index("seq") < members, 0.0, ref[...])
+
+
 def owner_shift_kernel(s_ref, c_ref, f_ref, before_ref, back_ref, out_ref):
     members = back_ref.shape[0]
-    before = before_ref[...]
+    before = masked(before_ref, members)
     for m in range(members):
         back_ref[m] = s_ref[m] + before
     out_ref[0] = f_ref[0]
@@ -200,8 +209,10 @@
 
 
 def add_kernel(base_ref, before_ref, out_ref):
-    for m in range(out_ref.shape[0]):
-        out_ref[m] = base_ref[m] + before_ref[...]
+    members = out_ref.shape[0]
+    before = masked(before_ref, members)
+    for m in range(members):
+        out_ref[m] = base_ref[m] + before
 
 
 def scale_kernel(
@@ -275,6 +286,8 @@
     groups = seq // members
     index_groups = [[g * members + m for m in range(members)] for g in range(groups)]
     onward = [(i, i + members) for i in range(seq - members)]
+    if groups == 2:
+        onward += [(i + members, i) for i in range(members)]
 
     def swap(a):
         return lax.all_to_all(a, "seq", 0, 0, axis_index_groups=index_groups)
@@ -289,7 +302,7 @@
     twofold = shape((pairs, PAIR, tokens, 2 * BLK), bf16)
     pair_mats = shape((pairs, PAIR, BLK, BLK), f32)
     moment_mats = shape((pairs, PAIR, 2 * BLK, BLK), f32)
-    in_hbm = pl.BlockSpec(memory_space=pltpu.HBM)
+    in_hbm = pl.BlockSpec(memory_space=pl.ANY)
 
     def buffers(reads, writes):
         sems = [pltpu.SemaphoreType.DMA((len(a), pairs)) for a in (reads, writes)]

time: 82.1 us -> 90.3 us (1.100)
  Pallas kernels: 40.3 us -> 48.7 us
  starting transfers between devices: 29.4 us -> 21.4 us
  waiting for transfers between devices: 10.1 us -> 17.7 us
    ppermute x1, starting transfers between devices: 5.26 us -> 0.07 us  [per_device(): d_before = lax.ppermute(d_before + d_total, 'seq', onward)]
    ppermute x1, waiting for transfers between devices: 1.88 us -> 5.53 us  [per_device(): d_before = lax.ppermute(d_before + d_total, 'seq', onward)]
    pallas_call x1, Pallas kernels: 6.4 us -> 9.86 us  [per_device(): pl.pallas_call(scale_kernel, in_specs=[in_hbm] * 3 + [in_vmem, pl.BlockSp...]
    pallas_call x1, Pallas kernels: 5.16 us -> 8.38 us  [per_device(): pl.pallas_call(moments_kernel, in_specs=[in_hbm] * 3, out_specs=[in_hbm]...]
    all_to_all x4, waiting for transfers between devices: 4.61 us -> 6.68 us  [swap(): return lax.all_to_all(a, 'seq', 0, 0, axis_index_groups=index_groups)]
    ppermute x1, waiting for transfers between devices: 2.2 us -> 4.11 us  [per_device(): s_before = lax.ppermute(s_before + s_part[members], 'seq', onward)]
    ppermute x1, starting transfers between devices: 4.5 us -> 2.63 us  [per_device(): s_before = lax.ppermute(s_before + s_part[members], 'seq', onward)]
    pallas_call x1, Pallas kernels: 11.2 us -> 12.8 us  [per_device(): stream_call(first_stage_kernel, [upright, upright, turned, turned], [twof...]
  transfers between devices with their start and end apart: 7 -> 7, of which waited for: 5 -> 6; matrix products, arithmetic and copies ran while one was open for 0% -> 0% of each run, Pallas kernels for 31% -> 30%
where the time goes in v4:
time: 90.3 us; the launch traced here: 89.3 us
  Pallas kernels  48.7 us (54%)
  starting transfers between devices  21.4 us (24%)
  waiting for transfers between devices  17.7 us (20%)
  local copies, waits for them, and re-layouts  1.4 us (2%)
    all_to_all x4, starting transfers between devices, swap(): return lax.all_to_all(a, 'seq', 0, 0, axis_index_groups=index_groups)  18.6 us
    pallas_call x1, Pallas kernels, per_device(): stream_call(first_stage_kernel, [upright, upright, turned, turned], [twof...  12.8 us
    pallas_call x1, Pallas kernels, per_device(): stream_call(second_stage_kernel, [upright, turned, turned, twofold, pair_...  12 us
    pallas_call x1, Pallas kernels, per_device(): pl.pallas_call(scale_kernel, in_specs=[in_hbm] * 3 + [in_vmem, pl.BlockSp...  9.86 us
    pallas_call x1, Pallas kernels, per_device(): pl.pallas_call(moments_kernel, in_specs=[in_hbm] * 3, out_specs=[in_hbm]...  8.38 us
    all_to_all x4, waiting for transfers between devices, swap(): return lax.all_to_all(a, 'seq', 0, 0, axis_index_groups=index_groups)  6.68 us
    ppermute x1, waiting for transfers between devices, per_device(): d_before = lax.ppermute(d_before + d_total, 'seq', onward)  5.53 us
    ppermute x1, waiting for transfers between devices, per_device(): s_before = lax.ppermute(s_before + s_part[members], 'seq', onward)  4.11 us
  transfers between devices with their start and end apart: 7, of which 6 were waited for; matrix products, arithmetic and copies ran while one was open for 0% of the time, Pallas kernels for 30%

profile of v4, /device:TPU:0, one launch (start us, length us, event | category | flops | bytes accessed | tf_op | source)
XLA Modules:
  0.0 89.3 jit_solution(2993489154254509757)
XLA Ops:
  0.0 8.4 %moments.1 = (f32[4,2,256,128]{3,2,1,0:T(8,128)}, bf16[4,256,1024]{2,1,0:T(8,128)(2,1)}, bf16[4,256,1024]{2,1,0:T(8,128)(2,1)}) custom-call(bf16[1024,1024]{1,0:T(8,128)(2,1)} %q_hbm.5, bf16[1024,1024]{1,0:T(8,128)(2,1)} %k_hbm.3, bf16[1024,1024]{1,0:T(8,128)(2,1)} %v_hbm.1), custom_call_target="tpu_custom_call" | custom-call | tf_op jit(solution)/shard_map/moments/pallas_call | solution.py:323
  8.4 6.2 %all-to-all-start = ((f32[8,256,128]{2,1,0:T(8,128)}), f32[8,256,128]{2,1,0:T(8,128)S(1)}, u32[]{:S(2)}, u32[]{:S(2)}) async-start(f32[8,256,128]{2,1,0:T(8,128)} %bitcast.9), calls=%async_computation | async-start | bytes 2097152 | tf_op jit(solution)/shard_map/all_to_all | solution.py:293
  14.6 12.8 %first_stage.1 = (bf16[4,2,1024,256]{3,2,1,0:T(8,128)(2,1)}, f32[4,2,128,128]{3,2,1,0:T(8,128)}, bf16[4,256,1024]{2,1,0:T(8,128)(2,1)}) custom-call(bf16[1024,1024]{1,0:T(8,128)(2,1)} %q_hbm.5, bf16[1024,1024]{1,0:T(8,128)(2,1)} %k_hbm.3, bf16[4,256,1024]{2,1,0:T(8,128)(2,1)} %get-tuple-element.20.kt_hbm, bf16[4,256,1024]{2,1,0:T(8,128)(2,1)} %get-tuple-element.21.vt_hbm), custom_call_target="tpu_custom_call" | custom-call | flops 4000000000 | bytes 10485760 | tf_op jit(solution)/shard_map/first_stage/pallas_call | solution.py:334
  27.4 1.9 %all-to-all-done.moments_ref = f32[8,256,128]{2,1,0:T(8,128)S(1)} async-done(((f32[8,256,128]{2,1,0:T(8,128)}), f32[8,256,128]{2,1,0:T(8,128)S(1)}, u32[]{:S(2)}, u32[]{:S(2)}) %all-to-all-start) | async-done | bytes 1048608 | tf_op jit(solution)/shard_map/all_to_all | solution.py:293
  29.3 3.5 %all-to-all-start.2 = ((f32[8,128,128]{2,1,0:T(8,128)}), f32[8,128,128]{2,1,0:T(8,128)S(1)}, u32[]{:S(2)}, u32[]{:S(2)}) async-start(f32[8,128,128]{2,1,0:T(8,128)} %bitcast.10), calls=%async_computation.2 | async-start | bytes 1048576 | tf_op jit(solution)/shard_map/all_to_all | solution.py:293
  32.8 0.4 owner_local.1
  33.2 2.6 %collective-permute-start = (f32[128,128]{1,0:T(8,128)S(1)}, f32[128,128]{1,0:T(8,128)S(1)}, u32[]{:S(2)}, u32[]{:S(2)}) collective-permute-start(f32[128,128]{1,0:T(8,128)S(1)} %slice_bitcast_fusion), channel_id=1, source_target_pairs={{0,16},{2,18},{4,20},{6,22},{8,24},{10,26},{12,28},{14,30},{16,0},... | collective-permute-start | bytes 196616 | tf_op jit(solution)/shard_map/ppermute | solution.py:347
  35.8 4.1 %collective-permute-done.before_ref = f32[128,128]{1,0:T(8,128)S(1)} collective-permute-done((f32[128,128]{1,0:T(8,128)S(1)}, f32[128,128]{1,0:T(8,128)S(1)}, u32[]{:S(2)}, u32[]{:S(2)}) %collective-permute-start) | collective-permute-done | bytes 65568 | tf_op jit(solution)/shard_map/ppermute | solution.py:347
  39.9 0.8 owner_shift.1
  40.8 2.4 %all-to-all-done.2.d_ref = f32[8,128,128]{2,1,0:T(8,128)S(1)} async-done(((f32[8,128,128]{2,1,0:T(8,128)}), f32[8,128,128]{2,1,0:T(8,128)S(1)}, u32[]{:S(2)}, u32[]{:S(2)}) %all-to-all-start.2) | async-done | bytes 524320 | tf_op jit(solution)/shard_map/all_to_all | solution.py:293
  43.2 5.4 %all-to-all-start.1 = ((f32[8,128,128]{2,1,0:T(8,128)}), f32[8,128,128]{2,1,0:T(8,128)S(1)}, u32[]{:S(2)}, u32[]{:S(2)}) async-start(f32[8,128,128]{2,1,0:T(8,128)} %get-tuple-element.28), calls=%async_computation.1 | async-start | bytes 1048576 | tf_op jit(solution)/shard_map/all_to_all | solution.py:293
  48.6 0.1 owner_sum.1
  48.7 0.1 collective-permute-start.1
  48.8 5.5 %collective-permute-done.1.before_ref = f32[128,128]{1,0:T(8,128)S(1)} collective-permute-done((f32[128,128]{1,0:T(8,128)S(1)}, f32[128,128]{1,0:T(8,128)S(1)}, u32[]{:S(2)}, u32[]{:S(2)}) %collective-permute-start.1) | collective-permute-done | bytes 65568 | tf_op jit(solution)/shard_map/ppermute | solution.py:364
  54.3 0.9 owner_add.1
  55.2 2.4 %all-to-all-done.1 = f32[8,128,128]{2,1,0:T(8,128)S(1)} async-done(((f32[8,128,128]{2,1,0:T(8,128)}), f32[8,128,128]{2,1,0:T(8,128)S(1)}, u32[]{:S(2)}, u32[]{:S(2)}) %all-to-all-start.1) | async-done | bytes 524320 | tf_op jit(solution)/shard_map/all_to_all | solution.py:293
  57.6 3.5 %all-to-all-start.3 = ((f32[8,128,128]{2,1,0:T(8,128)}), f32[8,128,128]{2,1,0:T(8,128)S(1)}, u32[]{:S(2)}, u32[]{:S(2)}) async-start(f32[8,128,128]{2,1,0:T(8,128)} %owner_add.1), calls=%async_computation.3 | async-start | bytes 1048576 | tf_op jit(solution)/shard_map/all_to_all | solution.py:293
  61.1 12.0 %second_stage.1.num_hbm = f32[4,256,1024]{2,1,0:T(8,128)} custom-call(bf16[1024,1024]{1,0:T(8,128)(2,1)} %q_hbm.5, bf16[4,256,1024]{2,1,0:T(8,128)(2,1)} %get-tuple-element.22.qt_hbm, bf16[4,256,1024]{2,1,0:T(8,128)(2,1)} %get-tuple-element.21.vt_hbm, bf16[4,2,1024,256]{3,2,1,0:T(8,128)(2,1)} %get-tuple-element.23.r_hbm, f32[4,2,128,128]{3,2,1,0:T(8,128)} %bitcast.8), custom_call_target="tpu_custom_call" | custom-call | flops 4000000000 | bytes 10485760 | tf_op jit(solution)/shard_map/second_stage/pallas_call | solution.py:370
  73.1 0.8 copy-done
  73.9 9.9 %scale_squares.1 = (f32[4,256,1024]{2,1,0:T(8,128)}, f32[8,1024]{1,0:T(8,128)}) custom-call(bf16[4,256,1024]{2,1,0:T(8,128)(2,1)} %get-tuple-element.22.qt_hbm, f32[4,256,1024]{2,1,0:T(8,128)} %second_stage.1.num_hbm, f32[4,2,128,128]{3,2,1,0:T(8,128)} %bitcast.7, f32[8,1,128]{2,1,0:T(1,128)} %bitcast.11, f32[8]{0:T(128)} %scale_ref.1), custom_call_target="tpu_custom_call" | custom-call | tf_op jit(solution)/shard_map/scale_squares/pallas_call | solution.py:376
  83.8 0.1 collective-permute-start.2
  83.9 1.4 %collective-permute-done.2.other_hbm = f32[8,1024]{1,0:T(8,128)S(1)} collective-permute-done((f32[8,1024]{1,0:T(8,128)}, f32[8,1024]{1,0:T(8,128)S(1)}, u32[]{:S(2)}, u32[]{:S(2)}) %collective-permute-start.2) | collective-permute-done | bytes 32800 | tf_op jit(solution)/shard_map/ppermute | solution.py:388
  85.3 0.6 copy-done.2
  85.9 3.5 %norm.1 = bf16[1024,1024]{1,0:T(8,128)(2,1)} custom-call(f32[4,256,1024]{2,1,0:T(8,128)} %get-tuple-element.33.y_hbm, f32[8,1024]{1,0:T(8,128)} %get-tuple-element.34.mine_hbm, f32[8,1024]{1,0:T(8,128)} %copy-done.2), custom_call_target="tpu_custom_call" | custom-call | tf_op jit(solution)/shard_map/norm/pallas_call | solution.py:390
  (6 shorter events, 0.0 us)
Async XLA Ops:
  8.4 20.9 %all-to-all-start = ((f32[8,256,128]{2,1,0:T(8,128)}), f32[8,256,128]{2,1,0:T(8,128)S(1)}, u32[]{:S(2)}, u32[]{:S(2)}) async-start(f32[8,256,128]{2,1,0:T(8,128)} %bitcast.9), calls=%async_computation | async-start | bytes 2097152 | tf_op jit(solution)/shard_map/all_to_all | solution.py:293
  29.3 13.9 %all-to-all-start.2 = ((f32[8,128,128]{2,1,0:T(8,128)}), f32[8,128,128]{2,1,0:T(8,128)S(1)}, u32[]{:S(2)}, u32[]{:S(2)}) async-start(f32[8,128,128]{2,1,0:T(8,128)} %bitcast.10), calls=%async_computation.2 | async-start | bytes 1048576 | tf_op jit(solution)/shard_map/all_to_all | solution.py:293
  33.2 6.7 %collective-permute-start = (f32[128,128]{1,0:T(8,128)S(1)}, f32[128,128]{1,0:T(8,128)S(1)}, u32[]{:S(2)}, u32[]{:S(2)}) collective-permute-start(f32[128,128]{1,0:T(8,128)S(1)} %slice_bitcast_fusion), channel_id=1, source_target_pairs={{0,16},{2,18},{4,20},{6,22},{8,24},{10,26},{12,28},{14,30},{16,0},... | collective-permute-start | bytes 196616 | tf_op jit(solution)/shard_map/ppermute | solution.py:347
  43.2 14.4 %all-to-all-start.1 = ((f32[8,128,128]{2,1,0:T(8,128)}), f32[8,128,128]{2,1,0:T(8,128)S(1)}, u32[]{:S(2)}, u32[]{:S(2)}) async-start(f32[8,128,128]{2,1,0:T(8,128)} %get-tuple-element.28), calls=%async_computation.1 | async-start | bytes 1048576 | tf_op jit(solution)/shard_map/all_to_all | solution.py:293
  48.7 5.6 %collective-permute-start.1 = (f32[128,128]{1,0:T(8,128)S(1)}, f32[128,128]{1,0:T(8,128)S(1)}, u32[]{:S(2)}, u32[]{:S(2)}) collective-permute-start(f32[128,128]{1,0:T(8,128)S(1)} %get-tuple-element.32), channel_id=1, source_target_pairs={{0,16},{2,18},{4,20},{6,22},{8,24},{10,26},{12,28},{14,30},{16,0},... | collective-permute-start | bytes 196616 | tf_op jit(solution)/shard_map/ppermute | solution.py:364
  57.6 3.5 %copy-start.1 = (f32[8,128,128]{2,1,0:T(8,128)}, f32[8,128,128]{2,1,0:T(8,128)S(1)}, u32[]{:S(2)}) copy-start(f32[8,128,128]{2,1,0:T(8,128)S(1)} %all-to-all-done.1) | copy-start | bytes 1572868
  57.6 15.5 %all-to-all-start.3 = ((f32[8,128,128]{2,1,0:T(8,128)}), f32[8,128,128]{2,1,0:T(8,128)S(1)}, u32[]{:S(2)}, u32[]{:S(2)}) async-start(f32[8,128,128]{2,1,0:T(8,128)} %owner_add.1), calls=%async_computation.3 | async-start | bytes 1048576 | tf_op jit(solution)/shard_map/all_to_all | solution.py:293
  73.1 0.8 copy-start
  83.8 1.5 %collective-permute-start.2 = (f32[8,1024]{1,0:T(8,128)}, f32[8,1024]{1,0:T(8,128)S(1)}, u32[]{:S(2)}, u32[]{:S(2)}) collective-permute-start(f32[8,1024]{1,0:T(8,128)} %get-tuple-element.34.mine_hbm), channel_id=1, source_target_pairs={{0,1},{1,0},{2,3},{3,2},{4,5},{5,4},{6,7},{7,6},{8,9},{9,8},{10,11... | collective-permute-start | bytes 98312 | tf_op jit(solution)/shard_map/ppermute | solution.py:388
  85.3 0.6 copy-start.2

commit v5 on v3

v5 whole, which is shorter than its diff:
```python
import functools

import jax
import jax.numpy as jnp
from jax import lax
from jax.experimental import pallas as pl
from jax.experimental.pallas import tpu as pltpu
from jax.sharding import PartitionSpec as P

BLK = 128
CHUNK = 256
PAIR = 2
SMALL = 8 * 1024 * 1024
LARGE = 60 * 1024 * 1024
LATE = 52 * 1024 * 1024
LAST = 52 * 1024 * 1024

epsilon = 1e-06
f32, bf16 = jnp.float32, jnp.bfloat16

NN = (((1,), (0,)), ((), ()))
NT = (((1,), (1,)), ((), ()))
TN = (((0,), (0,)), ((), ()))


def dot(a, b, dims=NN):
    return lax.dot_general(a, b, dims, preferred_element_type=f32)


def split(a):
    high = a.astype(bf16)
    return high, (a - high.astype(f32)).astype(bf16)


def lanes(*parts):
    return jnp.concatenate(parts, axis=1)


def rows(*parts):
    return jnp.concatenate(parts, axis=0)


def dot_f32(a, b):
    a_high, a_low = split(a)
    b_high, b_low = split(b)
    return dot(lanes(a_high, a_low), rows(b_high, b_high)) + dot(a_high, b_low)


def ordered(size):
    shape = (size, size)
    return lax.broadcasted_iota(jnp.int32, shape, 0) - lax.broadcasted_iota(jnp.int32, shape, 1)


def span(j, size=BLK):
    return slice(j * size, (j + 1) * size)


def columns(p):
    return pl.ds(pl.multiple_of(p * PAIR * BLK, PAIR * BLK), PAIR * BLK)


def copies(moves, sems, p):
    return [
        pltpu.make_async_copy(source(p), target(p), sems.at[n, p])
        for n, (source, target) in enumerate(moves)
    ]


def start(moves, sems, first, last):
    for p in range(first, last):
        for copy in copies(moves, sems, p):
            copy.start()


def wait(moves, sems, p):
    for copy in copies(moves, sems, p):
        copy.wait()


def by_columns(hbm):
    return lambda p: hbm.at[:, columns(p)]


def by_pair(ref):
    return lambda p: ref.at[p]


def by_mats(ref):
    return lambda p: ref.at[pl.ds(p * PAIR, PAIR)]


def moments_kernel(q_hbm, k_hbm, v_hbm, m_hbm, q_ref, k_ref, v_ref, m_ref, read_sems, write_sems):
    pairs = q_ref.shape[0]
    reads = [(by_columns(a), by_pair(b)) for a, b in ((k_hbm, k_ref), (v_hbm, v_ref), (q_hbm, q_ref))]
    writes = [(by_pair(m_ref), by_pair(m_hbm))]
    start(reads, read_sems, 0, pairs)
    for p in range(pairs):
        wait(reads, read_sems, p)
        for j in range(PAIR):
            k = k_ref[p, :, span(j)]
            m_ref[p, j, :BLK] = dot(k.T, k)
            m_ref[p, j, BLK:] = dot(v_ref[p, :, span(j)].T, q_ref[p, :, span(j)])
        start(writes, write_sems, p, p + 1)
    for p in range(pairs):
        wait(writes, write_sems, p)


def first_stage_kernel(
    q_hbm, k_hbm, v_hbm, r_hbm, d_hbm, q_ref, k_ref, v_ref, r_ref, d_ref, read_sems, write_sems
):
    pairs, tokens, _ = q_ref.shape
    steps = tokens // CHUNK
    mask = ordered(CHUNK) >= 0
    reads = [(by_columns(a), by_pair(b)) for a, b in ((q_hbm, q_ref), (k_hbm, k_ref), (v_hbm, v_ref))]
    writes = [(by_pair(r_ref), by_pair(r_hbm)), (by_pair(d_ref), by_pair(d_hbm))]
    start(reads, read_sems, 0, pairs)

    @pl.loop(0, pairs)
    def _(p):
        wait(reads, read_sems, p)
        states = [jnp.zeros((BLK, BLK), f32)] * PAIR
        for i in range(steps):
            at = span(i, CHUNK)
            for j in range(PAIR):
                q, k = q_ref[p, at, span(j)], k_ref[p, at, span(j)]
                kt = k.T
                r = dot(lanes(*split(jnp.where(mask, dot(q, kt), 0.0))), rows(k, k))
                if i > 0:
                    r = r + dot(lanes(q, q), rows(*split(states[j])))
                if i + 1 < steps:
                    states[j] = states[j] + dot(kt, k)
                r_ref[p, j, at] = lanes(*split(r))
        for j in range(PAIR):
            d = dot(v_ref[p, :, span(j)].T, r_ref[p, j])
            d_ref[p, j] = d[:, :BLK] + d[:, BLK:]
        for copy in copies(writes, write_sems, p):
            copy.start()

    for p in range(pairs):
        wait(writes, write_sems, p)


def second_stage(p, q_ref, v_ref, r_ref, s_ref, states, store):
    tokens = q_ref.shape[1]
    steps = tokens // CHUNK
    mask = ordered(CHUNK) <= 0
    s_both = [rows(*split(s_ref[p * PAIR + j])) for j in range(PAIR)]
    for i in range(steps):
        at = span(i, CHUNK)
        for j in range(PAIR):
            q = q_ref[p, at, span(j)]
            qt, vt = q.T, v_ref[p, at, span(j)].T
            qt2 = rows(qt, qt)
            pair = r_ref[p, j, at].astype(f32)
            r = lanes(*split(pair[:, :BLK] + pair[:, BLK:] + dot(lanes(q, q), s_both[j])))
            num = dot(lanes(vt, vt), rows(*split(jnp.where(mask, dot(r, qt2), 0.0))))
            if states[j] is not None:
                num = num + dot(lanes(*split(states[j])), qt2)
            store(i, j, num)
            if i + 1 < steps:
                d = dot(vt, r)
                d = d[:, :BLK] + d[:, BLK:]
                states[j] = d if states[j] is None else states[j] + d


def early_kernel(
    q_hbm, v_hbm, r_hbm, s_ref, num_hbm, q_ref, v_ref, r_ref, num_ref, read_sems, write_sems
):
    pairs = q_ref.shape[0]
    reads = [(by_columns(q_hbm), by_pair(q_ref)), (by_pair(r_hbm), by_pair(r_ref)), (by_columns(v_hbm), by_pair(v_ref))]
    writes = [(by_pair(num_ref), by_pair(num_hbm))]
    start(reads, read_sems, 0, pairs)

    @pl.loop(0, pairs)
    def _(p):
        wait(reads, read_sems, p)

        def store(i, j, num):
            num_ref[p, span(j), span(i, CHUNK)] = num

        second_stage(p, q_ref, v_ref, r_ref, s_ref, [None] * PAIR, store)
        for copy in copies(writes, write_sems, p):
            copy.start()

    for p in range(pairs):
        wait(writes, write_sems, p)


def late_kernel(
    q_hbm, v_hbm, r_hbm, s_hbm, num_hbm, d_ref, gain_ref, scale_ref, y_hbm, part_ref,
    q_ref, v_ref, r_ref, s_ref, num_ref, y_ref, gains_ref, early_sems, late_sems, write_sems
):
    pairs = q_ref.shape[0]
    early = num_ref.shape[0]
    tokens = q_ref.shape[1]
    reads_early = [(by_columns(q_hbm), by_pair(q_ref)), (by_pair(num_hbm), by_pair(num_ref))]
    reads_late = [
        (by_columns(q_hbm), by_pair(q_ref)),
        (by_columns(v_hbm), by_pair(v_ref)),
        (by_pair(r_hbm), by_pair(r_ref)),
        (by_mats(s_hbm), by_mats(s_ref)),
    ]
    writes = [(by_pair(y_ref), by_pair(y_hbm))]
    start(reads_late, late_sems, early, pairs)
    start(reads_early, early_sems, 0, early)
    part_ref[...] = jnp.zeros_like(part_ref)
    for h in range(pairs * PAIR):
        gains_ref[h] = jnp.broadcast_to(gain_ref[h], (BLK, BLK)).T

    def finish(p, i, j, num):
        h = p * PAIR + j
        y = num * scale_ref[h]
        part_ref[:, span(i, CHUNK)] += jnp.sum((y * y).reshape(BLK // 8, 8, CHUNK), axis=0)
        y_ref[p, span(j), span(i, CHUNK)] = y * lanes(*[gains_ref[h]] * (CHUNK // BLK))

    @pl.loop(early, pairs)
    def _(p):
        wait(reads_late, late_sems, p)
        states = [d_ref[p * PAIR + j] for j in range(PAIR)]
        second_stage(p, q_ref, v_ref, r_ref, s_ref, states, functools.partial(finish, p))
        for copy in copies(writes, write_sems, p):
            copy.start()

    @pl.loop(0, early)
    def _(p):
        wait(reads_early, early_sems, p)
        for j in range(PAIR):
            before = lanes(*split(d_ref[p * PAIR + j]))
            for i in range(tokens // CHUNK):
                qt = q_ref[p, span(i, CHUNK), span(j)].T
                finish(p, i, j, num_ref[p, span(j), span(i, CHUNK)] + dot(before, rows(qt, qt)))
        for copy in copies(writes, write_sems, p):
            copy.start()

    for p in range(pairs):
        wait(writes, write_sems, p)


def owner_local_kernel(moments_ref, s_ref, c_ref, f_ref):
    members = moments_ref.shape[0]
    s = jnp.zeros((BLK, BLK), f32)
    c = jnp.zeros((BLK, BLK), f32)
    f = jnp.zeros((BLK, BLK), f32)
    for m in range(members):
        s_ref[m], c_ref[m], f_ref[m] = s, c, f
        c_own = moments_ref[m, BLK:]
        if m > 0:
            f = f + dot_f32(c_own, s)
        s = s + moments_ref[m, :BLK]
        c = c + c_own
    s_ref[members], c_ref[members], f_ref[members] = s, c, f


def owner_shift_kernel(s_ref, c_ref, f_ref, before_ref, back_ref, out_ref):
    members = back_ref.shape[0]
    before = before_ref[...]
    for m in range(members):
        back_ref[m] = s_ref[m] + before
    out_ref[0] = f_ref[0]
    for m in range(1, members + 1):
        out_ref[m] = f_ref[m] + dot_f32(c_ref[m], before)


def owner_sum_kernel(d_ref, h_ref, base_ref, total_ref):
    members = d_ref.shape[0]
    d = jnp.zeros((BLK, BLK), f32)
    for m in range(members):
        base_ref[m] = h_ref[m] + d
        d = d + d_ref[m]
    total_ref[...] = h_ref[members] + d


def add_kernel(base_ref, before_ref, out_ref):
    for m in range(out_ref.shape[0]):
        out_ref[m] = base_ref[m] + before_ref[...]


def norm_kernel(features, y_hbm, mine_ref, other_ref, out_hbm, y_ref, out_ref, read_sems, write_sems):
    pairs, wide, tokens = y_ref.shape
    steps = tokens // CHUNK

    def y_copy(i):
        at = span(i, CHUNK)
        return pltpu.make_async_copy(y_hbm.at[:, :, at], y_ref.at[:, :, at], read_sems.at[i])

    def out_copy(i):
        at = span(i, CHUNK)
        return pltpu.make_async_copy(out_ref.at[at], out_hbm.at[at], write_sems.at[i])

    for i in range(steps):
        y_copy(i).start()
    total = jnp.sum(mine_ref[...] + other_ref[...], axis=0, keepdims=True)
    inv = lax.rsqrt(total * (1.0 / features) + epsilon)
    for i in range(steps):
        at = span(i, CHUNK)
        y_copy(i).wait()
        for p in range(pairs):
            out_ref[at, span(p, wide)] = (y_ref[p, :, at] * inv[:, at]).astype(bf16).T
        out_copy(i).start()
    for i in range(steps):
        out_copy(i).wait()


def params(limit=SMALL):
    return pltpu.CompilerParams(vmem_limit_bytes=limit)


def cost(us, moved):
    return pl.CostEstimate(flops=int(us * 4e8), bytes_accessed=int(moved), transcendentals=0)


def per_device(query_rows, key_rows, value_rows, head_scale, out_gain):
    tokens, width = query_rows.shape
    heads = head_scale.shape[0]
    seq = lax.axis_size("seq")
    members = heads
    groups = seq // members
    index_groups = [[g * members + m for m in range(members)] for g in range(groups)]
    onward = [(i, i + members) for i in range(seq - members)]

    def swap(a):
        return lax.all_to_all(a, "seq", 0, 0, axis_index_groups=index_groups)

    mats = lambda n: jax.ShapeDtypeStruct((n, BLK, BLK), f32)
    mat = jax.ShapeDtypeStruct((BLK, BLK), f32)
    pairs = heads // PAIR
    early = pairs // 2
    shape = jax.ShapeDtypeStruct
    upright = shape((pairs, tokens, PAIR * BLK), bf16)
    turned_f32 = shape((pairs, PAIR * BLK, tokens), f32)
    twofold = shape((pairs, PAIR, tokens, 2 * BLK), bf16)
    pair_mats = shape((pairs, PAIR, BLK, BLK), f32)
    moment_mats = shape((pairs, PAIR, 2 * BLK, BLK), f32)
    anywhere = pl.BlockSpec(memory_space=pl.ANY)
    in_vmem = pl.BlockSpec(memory_space=pltpu.VMEM)
    in_smem = pl.BlockSpec(memory_space=pltpu.SMEM)

    def cut(a, n):
        return shape((n,) + a.shape[1:], a.dtype)

    def vmem(*arrays):
        return [pltpu.VMEM(a.shape, a.dtype) for a in arrays]

    def sems(*counts):
        return [pltpu.SemaphoreType.DMA((n, pairs)) for n in counts]

    moments = pl.pallas_call(
        moments_kernel,
        in_specs=[anywhere] * 3,
        out_specs=anywhere,
        out_shape=moment_mats,
        scratch_shapes=vmem(upright, upright, upright, moment_mats) + sems(3, 1),
        compiler_params=params(LARGE),
        name="moments",
    )(query_rows, key_rows, value_rows)
    moments_in = swap(moments.reshape(heads, 2 * BLK, BLK))

    r_local, d_local = pl.pallas_call(
        first_stage_kernel,
        in_specs=[anywhere] * 3,
        out_specs=[anywhere] * 2,
        out_shape=[twofold, pair_mats],
        scratch_shapes=vmem(upright, upright, upright, twofold, pair_mats) + sems(3, 2),
        compiler_params=params(LARGE),
        cost_estimate=cost(10, 10 * tokens * width),
        name="first_stage",
    )(query_rows, key_rows, value_rows)
    d_in = swap(d_local.reshape(heads, BLK, BLK))

    s_part, c_part, f_part = pl.pallas_call(
        owner_local_kernel,
        out_shape=[mats(members + 1)] * 3,
        compiler_params=params(),
        name="owner_local",
    )(moments_in)
    s_before = jnp.zeros((BLK, BLK), f32)
    for _ in range(groups - 1):
        s_before = lax.ppermute(s_before + s_part[members], "seq", onward)
    s_back, h_part = pl.pallas_call(
        owner_shift_kernel,
        out_shape=[mats(members), mats(members + 1)],
        compiler_params=params(),
        name="owner_shift",
    )(s_part, c_part, f_part, s_before)
    s_pre = swap(s_back)

    d_base, d_total = pl.pallas_call(
        owner_sum_kernel,
        out_shape=[mats(members), mat],
        compiler_params=params(),
        name="owner_sum",
    )(d_in, h_part)
    d_before = jnp.zeros((BLK, BLK), f32)
    for _ in range(groups - 1):
        d_before = lax.ppermute(d_before + d_total, "seq", onward)
    d_back = pl.pallas_call(
        add_kernel, out_shape=mats(members), compiler_params=params(), name="owner_add"
    )(d_base, d_before)
    d_pre = swap(d_back)

    num = pl.pallas_call(
        early_kernel,
        in_specs=[anywhere] * 3 + [in_vmem],
        out_specs=anywhere,
        out_shape=cut(turned_f32, early),
        scratch_shapes=vmem(*[cut(a, early) for a in (upright, upright, twofold, turned_f32)]) + sems(3, 1),
        compiler_params=params(LARGE),
        cost_estimate=cost(6, 6 * tokens * width),
        name="second_early",
    )(query_rows, value_rows, r_local, s_pre)

    part_shape = shape((8, tokens), f32)
    y, part = pl.pallas_call(
        late_kernel,
        in_specs=[anywhere] * 5 + [in_vmem, in_vmem, in_smem],
        out_specs=[anywhere, in_vmem],
        out_shape=[turned_f32, part_shape],
        scratch_shapes=vmem(
            upright, upright, twofold, mats(heads), cut(turned_f32, early), turned_f32, mats(heads)
        )
        + sems(2, 4, 1),
        compiler_params=params(LATE),
        name="second_late",
    )(query_rows, value_rows, r_local, s_pre, num, d_pre, out_gain.reshape(heads, 1, BLK), head_scale)
    shards = lax.axis_size("head")
    other = jnp.zeros_like(part)
    for turn in range(1, shards):
        other = other + lax.ppermute(part, "head", [(i, (i + turn) % shards) for i in range(shards)])
    return pl.pallas_call(
        functools.partial(norm_kernel, width * shards),
        in_specs=[anywhere, in_vmem, in_vmem],
        out_specs=anywhere,
        out_shape=shape((tokens, width), bf16),
        scratch_shapes=vmem(turned_f32, shape((tokens, width), bf16))
        + [pltpu.SemaphoreType.DMA((tokens // CHUNK,))] * 2,
        compiler_params=params(LAST),
        name="norm",
    )(y, part, other)


def solution(mesh):
    return jax.shard_map(
        per_device,
        mesh=mesh,
        in_specs=(P("seq", "head"), P("seq", "head"), P("seq", "head"), P("head"), P("head")),
        out_specs=P("seq", "head"),
        check_vma=False,
    )
```

time: 82.1 us -> 79 us (0.962)
  Pallas kernels: 40.3 us -> 37.6 us
    pallas_call x4, Pallas kernels: 34.7 us -> 32.2 us  [the longest x1 11 us: per_device(): pl.pallas_call(first_stage_kernel, in_specs=[anywhere] * 3, out_specs=[an...]
  transfers between devices with their start and end apart: 7 -> 7, of which waited for: 5 -> 5; matrix products, arithmetic and copies ran while one was open for 0% -> 0% of each run, Pallas kernels for 31% -> 27%
where the time goes in v5:
time: 79 us; the launch traced here: 78.3 us
  Pallas kernels  37.6 us (48%)
  starting transfers between devices  29.4 us (37%)
  waiting for transfers between devices  10 us (13%)
  local copies, waits for them, and re-layouts  1.06 us (1%)
    all_to_all x4, starting transfers between devices, swap(): return lax.all_to_all(a, 'seq', 0, 0, axis_index_groups=index_groups)  19.6 us
    pallas_call x1, Pallas kernels, per_device(): pl.pallas_call(first_stage_kernel, in_specs=[anywhere] * 3, out_specs=[an...  11 us
    pallas_call x1, Pallas kernels, per_device(): pl.pallas_call(late_kernel, in_specs=[anywhere] * 5 + [in_vmem, in_vmem,...  8.74 us
    pallas_call x1, Pallas kernels, per_device(): pl.pallas_call(early_kernel, in_specs=[anywhere] * 3 + [in_vmem], out_spe...  8.17 us
    ppermute x1, starting transfers between devices, per_device(): d_before = lax.ppermute(d_before + d_total, 'seq', onward)  5.26 us
    all_to_all x4, waiting for transfers between devices, swap(): return lax.all_to_all(a, 'seq', 0, 0, axis_index_groups=index_groups)  4.77 us
    ppermute x1, starting transfers between devices, per_device(): s_before = lax.ppermute(s_before + s_part[members], 'seq', onward)  4.49 us
    pallas_call x1, Pallas kernels, per_device(): pl.pallas_call(moments_kernel, in_specs=[anywhere] * 3, out_specs=anywher...  4.27 us
  transfers between devices with their start and end apart: 7, of which 5 were waited for; matrix products, arithmetic and copies ran while one was open for 0% of the time, Pallas kernels for 27%

profile of v5, /device:TPU:0, one launch (start us, length us, event | category | flops | bytes accessed | tf_op | source)
XLA Modules:
  0.0 78.3 jit_solution(12286286327624874714)
XLA Ops:
  0.0 4.3 %moments.1 = f32[4,2,256,128]{3,2,1,0:T(8,128)} custom-call(bf16[1024,1024]{1,0:T(8,128)(2,1)} %q_hbm.7, bf16[1024,1024]{1,0:T(8,128)(2,1)} %k_hbm.3, bf16[1024,1024]{1,0:T(8,128)(2,1)} %v_hbm.7), custom_call_target="tpu_custom_call" | custom-call | tf_op jit(solution)/shard_map/moments/pallas_call | solution.py:347
  4.3 6.2 %all-to-all-start = ((f32[8,256,128]{2,1,0:T(8,128)}), f32[8,256,128]{2,1,0:T(8,128)S(1)}, u32[]{:S(2)}, u32[]{:S(2)}) async-start(f32[8,256,128]{2,1,0:T(8,128)} %bitcast.6), calls=%async_computation | async-start | bytes 2097152 | tf_op jit(solution)/shard_map/all_to_all | solution.py:322
  10.5 11.0 %first_stage.1 = (bf16[4,2,1024,256]{3,2,1,0:T(8,128)(2,1)}, f32[4,2,128,128]{3,2,1,0:T(8,128)}) custom-call(bf16[1024,1024]{1,0:T(8,128)(2,1)} %q_hbm.7, bf16[1024,1024]{1,0:T(8,128)(2,1)} %k_hbm.3, bf16[1024,1024]{1,0:T(8,128)(2,1)} %v_hbm.7), custom_call_target="tpu_custom_call" | custom-call | flops 4000000000 | bytes 10485760 | tf_op jit(solution)/shard_map/first_stage/pallas_call | solution.py:358
  21.5 3.7 %all-to-all-done.moments_ref = f32[8,256,128]{2,1,0:T(8,128)S(1)} async-done(((f32[8,256,128]{2,1,0:T(8,128)}), f32[8,256,128]{2,1,0:T(8,128)S(1)}, u32[]{:S(2)}, u32[]{:S(2)}) %all-to-all-start) | async-done | bytes 1048608 | tf_op jit(solution)/shard_map/all_to_all | solution.py:322
  25.2 3.5 %all-to-all-start.2 = ((f32[8,128,128]{2,1,0:T(8,128)}), f32[8,128,128]{2,1,0:T(8,128)S(1)}, u32[]{:S(2)}, u32[]{:S(2)}) async-start(f32[8,128,128]{2,1,0:T(8,128)} %bitcast.7), calls=%async_computation.2 | async-start | bytes 1048576 | tf_op jit(solution)/shard_map/all_to_all | solution.py:322
  28.7 0.4 owner_local.1
  29.1 4.5 %collective-permute-start = (f32[128,128]{1,0:T(8,128)S(1)}, f32[128,128]{1,0:T(8,128)S(1)}, u32[]{:S(2)}, u32[]{:S(2)}) collective-permute-start(f32[128,128]{1,0:T(8,128)S(1)} %slice_bitcast_fusion), channel_id=1, source_target_pairs={{0,16},{2,18},{4,20},{6,22},{8,24},{10,26},{12,28},{14,30},{1,17},... | collective-permute-start | bytes 196616 | tf_op jit(solution)/shard_map/ppermute | solution.py:378
  33.6 2.2 %collective-permute-done.before_ref = f32[128,128]{1,0:T(8,128)S(1)} collective-permute-done((f32[128,128]{1,0:T(8,128)S(1)}, f32[128,128]{1,0:T(8,128)S(1)}, u32[]{:S(2)}, u32[]{:S(2)}) %collective-permute-start) | collective-permute-done | bytes 65568 | tf_op jit(solution)/shard_map/ppermute | solution.py:378
  35.8 0.8 %owner_shift.1 = (f32[8,128,128]{2,1,0:T(8,128)}, f32[9,128,128]{2,1,0:T(8,128)S(1)}) custom-call(f32[9,128,128]{2,1,0:T(8,128)S(1)} %get-tuple-element.17.s_ref, f32[9,128,128]{2,1,0:T(8,128)S(1)} %get-tuple-element.18.c_ref, f32[9,128,128]{2,1,0:T(8,128)S(1)} %get-tuple-element.19.f_ref, f32[128,128]{1,0:T(8,128)S(1)} %collective-permute-done.before_ref), custom_call_target="tpu_custom_call" | custom-call | tf_op jit(solution)/shard_map/owner_shift/pallas_call | solution.py:379
  36.6 1.1 %all-to-all-done.2.d_ref = f32[8,128,128]{2,1,0:T(8,128)S(1)} async-done(((f32[8,128,128]{2,1,0:T(8,128)}), f32[8,128,128]{2,1,0:T(8,128)S(1)}, u32[]{:S(2)}, u32[]{:S(2)}) %all-to-all-start.2) | async-done | bytes 524320 | tf_op jit(solution)/shard_map/all_to_all | solution.py:322
  37.7 4.2 %all-to-all-start.1 = ((f32[8,128,128]{2,1,0:T(8,128)}), f32[8,128,128]{2,1,0:T(8,128)S(1)}, u32[]{:S(2)}, u32[]{:S(2)}) async-start(f32[8,128,128]{2,1,0:T(8,128)} %get-tuple-element.20), calls=%async_computation.1 | async-start | bytes 1048576 | tf_op jit(solution)/shard_map/all_to_all | solution.py:322
  42.0 0.1 owner_sum.1
  42.0 5.3 %collective-permute-start.1 = (f32[128,128]{1,0:T(8,128)S(1)}, f32[128,128]{1,0:T(8,128)S(1)}, u32[]{:S(2)}, u32[]{:S(2)}) collective-permute-start(f32[128,128]{1,0:T(8,128)S(1)} %get-tuple-element.24), channel_id=1, source_target_pairs={{0,16},{2,18},{4,20},{6,22},{8,24},{10,26},{12,28},{14,30},{1,17},... | collective-permute-start | bytes 196616 | tf_op jit(solution)/shard_map/ppermute | solution.py:395
  47.3 1.9 %collective-permute-done.1.before_ref = f32[128,128]{1,0:T(8,128)S(1)} collective-permute-done((f32[128,128]{1,0:T(8,128)S(1)}, f32[128,128]{1,0:T(8,128)S(1)}, u32[]{:S(2)}, u32[]{:S(2)}) %collective-permute-start.1) | collective-permute-done | bytes 65568 | tf_op jit(solution)/shard_map/ppermute | solution.py:395
  49.2 0.8 %owner_add.1 = f32[8,128,128]{2,1,0:T(8,128)} custom-call(f32[8,128,128]{2,1,0:T(8,128)S(1)} %get-tuple-element.23.base_ref, f32[128,128]{1,0:T(8,128)S(1)} %collective-permute-done.1.before_ref), custom_call_target="tpu_custom_call" | custom-call | tf_op jit(solution)/shard_map/owner_add/pallas_call | solution.py:396
  50.0 5.7 %all-to-all-start.3 = ((f32[8,128,128]{2,1,0:T(8,128)}), f32[8,128,128]{2,1,0:T(8,128)S(1)}, u32[]{:S(2)}, u32[]{:S(2)}) async-start(f32[8,128,128]{2,1,0:T(8,128)} %owner_add.1), calls=%async_computation.3 | async-start | bytes 1048576 | tf_op jit(solution)/shard_map/all_to_all | solution.py:322
  55.7 0.0 copy-start.2
  55.7 0.0 copy-start.3
  55.7 8.2 %second_early.1.num_hbm = f32[2,256,1024]{2,1,0:T(8,128)} custom-call(bf16[1024,1024]{1,0:T(8,128)(2,1)} %q_hbm.7, bf16[1024,1024]{1,0:T(8,128)(2,1)} %v_hbm.7, bf16[4,2,1024,256]{3,2,1,0:T(8,128)(2,1)} %get-tuple-element.16.r_hbm, f32[8,128,128]{2,1,0:T(8,128)} %copy-done), custom_call_target="tpu_custom_call" | custom-call | flops 2400000000 | bytes 6291456 | tf_op jit(solution)/shard_map/second_early/pallas_call | solution.py:401
  63.9 1.0 %copy-done.1 = f32[8,128,128]{2,1,0:T(8,128)S(1)} copy-done((f32[8,128,128]{2,1,0:T(8,128)S(1)}, f32[8,128,128]{2,1,0:T(8,128)}, u32[]{:S(2)}) %copy-start.1) | copy-done | bytes 524312
  65.0 8.7 %second_late.1 = (f32[4,256,1024]{2,1,0:T(8,128)}, f32[8,1024]{1,0:T(8,128)S(1)}) custom-call(bf16[1024,1024]{1,0:T(8,128)(2,1)} %q_hbm.7, bf16[1024,1024]{1,0:T(8,128)(2,1)} %v_hbm.7, bf16[4,2,1024,256]{3,2,1,0:T(8,128)(2,1)} %get-tuple-element.16.r_hbm, f32[8,128,128]{2,1,0:T(8,128)S(1)} %copy-done.1, f32[2,256,1024]{2,1,0:T(8,128)} %second_early.1.num_hbm, ...), custom_call_target="tpu_custom_call" | custom-call | tf_op jit(solution)/shard_map/second_late/pallas_call | solution.py:413
  73.7 0.1 collective-permute-start.2
  73.8 1.2 %collective-permute-done.2.other_ref = f32[8,1024]{1,0:T(8,128)S(1)} collective-permute-done((f32[8,1024]{1,0:T(8,128)S(1)}, f32[8,1024]{1,0:T(8,128)S(1)}, u32[]{:S(2)}, u32[]{:S(2)}) %collective-permute-start.2) | collective-permute-done | bytes 32800 | tf_op jit(solution)/shard_map/ppermute | solution.py:428
  75.0 3.3 %norm.1 = bf16[1024,1024]{1,0:T(8,128)(2,1)} custom-call(f32[4,256,1024]{2,1,0:T(8,128)} %get-tuple-element.25.y_hbm, f32[8,1024]{1,0:T(8,128)S(1)} %get-tuple-element.26.mine_ref, f32[8,1024]{1,0:T(8,128)S(1)} %collective-permute-done.2.other_ref), custom_call_target="tpu_custom_call" | custom-call | tf_op jit(solution)/shard_map/norm/pallas_call | solution.py:429
  (8 shorter events, 0.0 us)
Async XLA Ops:
  4.3 20.9 %all-to-all-start = ((f32[8,256,128]{2,1,0:T(8,128)}), f32[8,256,128]{2,1,0:T(8,128)S(1)}, u32[]{:S(2)}, u32[]{:S(2)}) async-start(f32[8,256,128]{2,1,0:T(8,128)} %bitcast.6), calls=%async_computation | async-start | bytes 2097152 | tf_op jit(solution)/shard_map/all_to_all | solution.py:322
  25.2 12.5 %all-to-all-start.2 = ((f32[8,128,128]{2,1,0:T(8,128)}), f32[8,128,128]{2,1,0:T(8,128)S(1)}, u32[]{:S(2)}, u32[]{:S(2)}) async-start(f32[8,128,128]{2,1,0:T(8,128)} %bitcast.7), calls=%async_computation.2 | async-start | bytes 1048576 | tf_op jit(solution)/shard_map/all_to_all | solution.py:322
  29.1 6.7 %collective-permute-start = (f32[128,128]{1,0:T(8,128)S(1)}, f32[128,128]{1,0:T(8,128)S(1)}, u32[]{:S(2)}, u32[]{:S(2)}) collective-permute-start(f32[128,128]{1,0:T(8,128)S(1)} %slice_bitcast_fusion), channel_id=1, source_target_pairs={{0,16},{2,18},{4,20},{6,22},{8,24},{10,26},{12,28},{14,30},{1,17},... | collective-permute-start | bytes 196616 | tf_op jit(solution)/shard_map/ppermute | solution.py:378
  37.7 12.3 %all-to-all-start.1 = ((f32[8,128,128]{2,1,0:T(8,128)}), f32[8,128,128]{2,1,0:T(8,128)S(1)}, u32[]{:S(2)}, u32[]{:S(2)}) async-start(f32[8,128,128]{2,1,0:T(8,128)} %get-tuple-element.20), calls=%async_computation.1 | async-start | bytes 1048576 | tf_op jit(solution)/shard_map/all_to_all | solution.py:322
  42.0 7.1 %collective-permute-start.1 = (f32[128,128]{1,0:T(8,128)S(1)}, f32[128,128]{1,0:T(8,128)S(1)}, u32[]{:S(2)}, u32[]{:S(2)}) collective-permute-start(f32[128,128]{1,0:T(8,128)S(1)} %get-tuple-element.24), channel_id=1, source_target_pairs={{0,16},{2,18},{4,20},{6,22},{8,24},{10,26},{12,28},{14,30},{1,17},... | collective-permute-start | bytes 196616 | tf_op jit(solution)/shard_map/ppermute | solution.py:395
  50.0 5.7 %copy-start = (f32[8,128,128]{2,1,0:T(8,128)}, f32[8,128,128]{2,1,0:T(8,128)S(1)}, u32[]{:S(2)}) copy-start(f32[8,128,128]{2,1,0:T(8,128)S(1)} %all-to-all-done.1.s_ref.s_hbm) | copy-start | bytes 1572868
  50.0 13.9 %all-to-all-start.3 = ((f32[8,128,128]{2,1,0:T(8,128)}), f32[8,128,128]{2,1,0:T(8,128)S(1)}, u32[]{:S(2)}, u32[]{:S(2)}) async-start(f32[8,128,128]{2,1,0:T(8,128)} %owner_add.1), calls=%async_computation.3 | async-start | bytes 1048576 | tf_op jit(solution)/shard_map/all_to_all | solution.py:322
  55.7 8.2 %copy-start.2 = (f32[1024]{0:T(1024)S(1)}, f32[1024]{0:T(1024)}, u32[]{:S(2)}) copy-start(f32[1024]{0:T(1024)} %param.9) | copy-start | bytes 12292
  55.7 8.2 %copy-start.3 = (f32[8]{0:T(128)S(1)}, f32[8]{0:T(128)}, u32[]{:S(2)}) copy-start(f32[8]{0:T(128)} %scale_ref.1) | copy-start | bytes 100
  63.9 1.0 %copy-start.1 = (f32[8,128,128]{2,1,0:T(8,128)S(1)}, f32[8,128,128]{2,1,0:T(8,128)}, u32[]{:S(2)}) copy-start(f32[8,128,128]{2,1,0:T(8,128)} %copy-done) | copy-start | bytes 1572868
  73.7 1.3 %collective-permute-start.2 = (f32[8,1024]{1,0:T(8,128)S(1)}, f32[8,1024]{1,0:T(8,128)S(1)}, u32[]{:S(2)}, u32[]{:S(2)}) collective-permute-start(f32[8,1024]{1,0:T(8,128)S(1)} %get-tuple-element.26.mine_ref), channel_id=1, source_target_pairs={{0,1},{1,0},{2,3},{3,2},{4,5},{5,4},{6,7},{7,6},{8,9},{9,8},{10,11... | collective-permute-start | bytes 98312 | tf_op jit(solution)/shard_map/ppermute | solution.py:428

commit v6 on v5

--- a/solution.py
+++ b/solution.py
@@ -105,12 +105,28 @@
         wait(writes, write_sems, p)
 
 
+def running(parts, first=None):
+    totals = [first]
+    for part in parts:
+        totals.append(part if totals[-1] is None else totals[-1] + part)
+    return totals
+
+
+def halves_sum(a):
+    return a[:, :BLK] + a[:, BLK:]
+
+
+def chunk_units(tokens):
+    return [(i, j, span(i, CHUNK), span(j)) for i in range(tokens // CHUNK) for j in range(PAIR)]
+
+
 def first_stage_kernel(
-    q_hbm, k_hbm, v_hbm, r_hbm, d_hbm, q_ref, k_ref, v_ref, r_ref, d_ref, read_sems, write_sems
+    q_hbm, k_hbm, v_hbm, r_hbm, d_hbm, q_ref, k_ref, v_ref, r_ref, d_ref, a_ref, read_sems, write_sems
 ):
     pairs, tokens, _ = q_ref.shape
     steps = tokens // CHUNK
-    mask = ordered(CHUNK) >= 0
+    units = chunk_units(tokens)
+    mask = ordered(CHUNK) <= 0
     reads = [(by_columns(a), by_pair(b)) for a, b in ((q_hbm, q_ref), (k_hbm, k_ref), (v_hbm, v_ref))]
     writes = [(by_pair(r_ref), by_pair(r_hbm)), (by_pair(d_ref), by_pair(d_hbm))]
     start(reads, read_sems, 0, pairs)
@@ -118,53 +134,62 @@
     @pl.loop(0, pairs)
     def _(p):
         wait(reads, read_sems, p)
-        states = [jnp.zeros((BLK, BLK), f32)] * PAIR
+        for i, j, at, cols in units:
+            a = dot(k_ref[p, at, cols], q_ref[p, at, cols].T)
+            a_ref[j, i] = rows(*split(jnp.where(mask, a, 0.0)))
+        states = []
+        for j in range(PAIR):
+            blocks = [k_ref[p, span(i, CHUNK), span(j)] for i in range(steps - 1)]
+            states.append(running([dot(k.T, k) for k in blocks]))
+        for i, j, at, cols in units:
+            kt = k_ref[p, at, cols].T
+            r = dot(lanes(kt, kt), a_ref[j, i])
+            if i > 0:
+                qt = q_ref[p, at, cols].T
+                r = r + dot(lanes(*split(states[j][i])), rows(qt, qt))
+            r_high, r_low = split(r)
+            r_ref[p, j, at] = lanes(r_high.T, r_low.T)
+        for j in range(PAIR):
+            d_ref[p, j] = halves_sum(dot(v_ref[p, :, span(j)].T, r_ref[p, j]))
+        for copy in copies(writes, write_sems, p):
+            copy.start()
+
+    for p in range(pairs):
+        wait(writes, write_sems, p)
+
+
+def second_stage(p, q_ref, v_ref, r_ref, s_ref, a_ref, first, store):
+    tokens = q_ref.shape[1]
+    steps = tokens // CHUNK
+    units = chunk_units(tokens)
+    mask = ordered(CHUNK) <= 0
+    s_both = [rows(*split(s_ref[p * PAIR + j])) for j in range(PAIR)]
+    for j in range(PAIR):
         for i in range(steps):
             at = span(i, CHUNK)
-            for j in range(PAIR):
-                q, k = q_ref[p, at, span(j)], k_ref[p, at, span(j)]
-                kt = k.T
-                r = dot(lanes(*split(jnp.where(mask, dot(q, kt), 0.0))), rows(k, k))
-                if i > 0:
-                    r = r + dot(lanes(q, q), rows(*split(states[j])))
-                if i + 1 < steps:
-                    states[j] = states[j] + dot(kt, k)
-                r_ref[p, j, at] = lanes(*split(r))
-        for j in range(PAIR):
-            d = dot(v_ref[p, :, span(j)].T, r_ref[p, j])
-            d_ref[p, j] = d[:, :BLK] + d[:, BLK:]
-        for copy in copies(writes, write_sems, p):
-            copy.start()
-
-    for p in range(pairs):
-        wait(writes, write_sems, p)
-
-
-def second_stage(p, q_ref, v_ref, r_ref, s_ref, states, store):
-    tokens = q_ref.shape[1]
-    steps = tokens // CHUNK
-    mask = ordered(CHUNK) <= 0
-    s_both = [rows(*split(s_ref[p * PAIR + j])) for j in range(PAIR)]
-    for i in range(steps):
-        at = span(i, CHUNK)
-        for j in range(PAIR):
             q = q_ref[p, at, span(j)]
-            qt, vt = q.T, v_ref[p, at, span(j)].T
-            qt2 = rows(qt, qt)
-            pair = r_ref[p, j, at].astype(f32)
-            r = lanes(*split(pair[:, :BLK] + pair[:, BLK:] + dot(lanes(q, q), s_both[j])))
-            num = dot(lanes(vt, vt), rows(*split(jnp.where(mask, dot(r, qt2), 0.0))))
-            if states[j] is not None:
-                num = num + dot(lanes(*split(states[j])), qt2)
-            store(i, j, num)
-            if i + 1 < steps:
-                d = dot(vt, r)
-                d = d[:, :BLK] + d[:, BLK:]
-                states[j] = d if states[j] is None else states[j] + d
+            r = halves_sum(r_ref[p, j, at].astype(f32)) + dot(lanes(q, q), s_both[j])
+            r_ref[p, j, at] = lanes(*split(r))
+    for i, j, at, cols in units:
+        qt = q_ref[p, at, cols].T
+        a = dot(r_ref[p, j, at], rows(qt, qt))
+        a_ref[j, i] = rows(*split(jnp.where(mask, a, 0.0)))
+    sums = [[] for _ in range(PAIR)]
+    for i, j, at, cols in units:
+        if i + 1 < steps:
+            sums[j].append(halves_sum(dot(v_ref[p, at, cols].T, r_ref[p, j, at])))
+    states = [running(sums[j], first[j]) for j in range(PAIR)]
+    for i, j, at, cols in units:
+        vt = v_ref[p, at, cols].T
+        num = dot(lanes(vt, vt), a_ref[j, i])
+        if states[j][i] is not None:
+            qt = q_ref[p, at, cols].T
+            num = num + dot(lanes(*split(states[j][i])), rows(qt, qt))
+        store(i, j, num)
 
 
 def early_kernel(
-    q_hbm, v_hbm, r_hbm, s_ref, num_hbm, q_ref, v_ref, r_ref, num_ref, read_sems, write_sems
+    q_hbm, v_hbm, r_hbm, s_ref, num_hbm, q_ref, v_ref, r_ref, num_ref, a_ref, read_sems, write_sems
 ):
     pairs = q_ref.shape[0]
     reads = [(by_columns(q_hbm), by_pair(q_ref)), (by_pair(r_hbm), by_pair(r_ref)), (by_columns(v_hbm), by_pair(v_ref))]
@@ -178,7 +203,7 @@
         def store(i, j, num):
             num_ref[p, span(j), span(i, CHUNK)] = num
 
-        second_stage(p, q_ref, v_ref, r_ref, s_ref, [None] * PAIR, store)
+        second_stage(p, q_ref, v_ref, r_ref, s_ref, a_ref, [None] * PAIR, store)
         for copy in copies(writes, write_sems, p):
             copy.start()
 
@@ -188,7 +213,7 @@
 
 def late_kernel(
     q_hbm, v_hbm, r_hbm, s_hbm, num_hbm, d_ref, gain_ref, scale_ref, y_hbm, part_ref,
-    q_ref, v_ref, r_ref, s_ref, num_ref, y_ref, gains_ref, early_sems, late_sems, write_sems
+    q_ref, v_ref, r_ref, s_ref, num_ref, y_ref, gains_ref, a_ref, early_sems, late_sems, write_sems
 ):
     pairs = q_ref.shape[0]
     early = num_ref.shape[0]
@@ -217,7 +242,7 @@
     def _(p):
         wait(reads_late, late_sems, p)
         states = [d_ref[p * PAIR + j] for j in range(PAIR)]
-        second_stage(p, q_ref, v_ref, r_ref, s_ref, states, functools.partial(finish, p))
+        second_stage(p, q_ref, v_ref, r_ref, s_ref, a_ref, states, functools.partial(finish, p))
         for copy in copies(writes, write_sems, p):
             copy.start()
 
@@ -330,6 +355,7 @@
     turned_f32 = shape((pairs, PAIR * BLK, tokens), f32)
     twofold = shape((pairs, PAIR, tokens, 2 * BLK), bf16)
     pair_mats = shape((pairs, PAIR, BLK, BLK), f32)
+    scores = shape((PAIR, tokens // CHUNK, 2 * CHUNK, CHUNK), bf16)
     moment_mats = shape((pairs, PAIR, 2 * BLK, BLK), f32)
     anywhere = pl.BlockSpec(memory_space=pl.ANY)
     in_vmem = pl.BlockSpec(memory_space=pltpu.VMEM)
@@ -360,7 +386,7 @@
         in_specs=[anywhere] * 3,
         out_specs=[anywhere] * 2,
         out_shape=[twofold, pair_mats],
-        scratch_shapes=vmem(upright, upright, upright, twofold, pair_mats) + sems(3, 2),
+        scratch_shapes=vmem(upright, upright, upright, twofold, pair_mats, scores) + sems(3, 2),
         compiler_params=params(LARGE),
         cost_estimate=cost(10, 10 * tokens * width),
         name="first_stage",
@@ -403,7 +429,7 @@
         in_specs=[anywhere] * 3 + [in_vmem],
         out_specs=anywhere,
         out_shape=cut(turned_f32, early),
-        scratch_shapes=vmem(*[cut(a, early) for a in (upright, upright, twofold, turned_f32)]) + sems(3, 1),
+        scratch_shapes=vmem(*[cut(a, early) for a in (upright, upright, twofold, turned_f32)], scores) + sems(3, 1),
         compiler_params=params(LARGE),
         cost_estimate=cost(6, 6 * tokens * width),
         name="second_early",
@@ -416,7 +442,7 @@
         out_specs=[anywhere, in_vmem],
         out_shape=[turned_f32, part_shape],
         scratch_shapes=vmem(
-            upright, upright, twofold, mats(heads), cut(turned_f32, early), turned_f32, mats(heads)
+            upright, upright, twofold, mats(heads), cut(turned_f32, early), turned_f32, mats(heads), scores
         )
         + sems(2, 4, 1),
         compiler_params=params(LATE),

time: 79 us -> 76.2 us (0.965)
  Pallas kernels: 37.6 us -> 30 us
  waiting for transfers between devices: 10 us -> 15.1 us
    all_to_all x4, waiting for transfers between devices: 4.77 us -> 9.84 us  [swap(): return lax.all_to_all(a, 'seq', 0, 0, axis_index_groups=index_groups)]
    pallas_call x1, Pallas kernels: 11 us -> 7.46 us  [per_device(): pl.pallas_call(first_stage_kernel, in_specs=[anywhere] * 3, out_specs=[an...]
    pallas_call x1, Pallas kernels: 8.17 us -> 6.1 us  [per_device(): pl.pallas_call(early_kernel, in_specs=[anywhere] * 3 + [in_vmem], out_spe...]
    pallas_call x1, Pallas kernels: 8.74 us -> 6.77 us  [per_device(): pl.pallas_call(late_kernel, in_specs=[anywhere] * 5 + [in_vmem, in_vmem,...]
  transfers between devices with their start and end apart: 7 -> 7, of which waited for: 5 -> 6; matrix products, arithmetic and copies ran while one was open for 0% -> 0% of each run, Pallas kernels for 27% -> 21%
where the time goes in v6:
time: 76.2 us; the launch traced here: 75.7 us
  Pallas kernels  30 us (39%)
  starting transfers between devices  29.4 us (39%)
  waiting for transfers between devices  15.1 us (20%)
  local copies, waits for them, and re-layouts  1.07 us (1%)
    all_to_all x4, starting transfers between devices, swap(): return lax.all_to_all(a, 'seq', 0, 0, axis_index_groups=index_groups)  19.6 us
    all_to_all x4, waiting for transfers between devices, swap(): return lax.all_to_all(a, 'seq', 0, 0, axis_index_groups=index_groups)  9.84 us
    pallas_call x1, Pallas kernels, per_device(): pl.pallas_call(first_stage_kernel, in_specs=[anywhere] * 3, out_specs=[an...  7.46 us
    pallas_call x1, Pallas kernels, per_device(): pl.pallas_call(late_kernel, in_specs=[anywhere] * 5 + [in_vmem, in_vmem,...  6.77 us
    pallas_call x1, Pallas kernels, per_device(): pl.pallas_call(early_kernel, in_specs=[anywhere] * 3 + [in_vmem], out_spe...  6.1 us
    ppermute x1, starting transfers between devices, per_device(): d_before = lax.ppermute(d_before + d_total, 'seq', onward)  5.26 us
    ppermute x1, starting transfers between devices, per_device(): s_before = lax.ppermute(s_before + s_part[members], 'seq', onward)  4.49 us
    pallas_call x1, Pallas kernels, per_device(): pl.pallas_call(moments_kernel, in_specs=[anywhere] * 3, out_specs=anywher...  4.27 us
  transfers between devices with their start and end apart: 7, of which 6 were waited for; matrix products, arithmetic and copies ran while one was open for 0% of the time, Pallas kernels for 21%

profile of v6, /device:TPU:0, one launch (start us, length us, event | category | flops | bytes accessed | tf_op | source)
XLA Modules:
  0.0 75.7 jit_solution(2467400069795602063)
XLA Ops:
  0.0 4.3 %moments.1 = f32[4,2,256,128]{3,2,1,0:T(8,128)} custom-call(bf16[1024,1024]{1,0:T(8,128)(2,1)} %q_hbm.7, bf16[1024,1024]{1,0:T(8,128)(2,1)} %k_hbm.3, bf16[1024,1024]{1,0:T(8,128)(2,1)} %v_hbm.7), custom_call_target="tpu_custom_call" | custom-call | tf_op jit(solution)/shard_map/moments/pallas_call | solution.py:373
  4.3 6.2 %all-to-all-start = ((f32[8,256,128]{2,1,0:T(8,128)}), f32[8,256,128]{2,1,0:T(8,128)S(1)}, u32[]{:S(2)}, u32[]{:S(2)}) async-start(f32[8,256,128]{2,1,0:T(8,128)} %bitcast.6), calls=%async_computation | async-start | bytes 2097152 | tf_op jit(solution)/shard_map/all_to_all | solution.py:347
  10.5 7.5 %first_stage.1 = (bf16[4,2,1024,256]{3,2,1,0:T(8,128)(2,1)}, f32[4,2,128,128]{3,2,1,0:T(8,128)}) custom-call(bf16[1024,1024]{1,0:T(8,128)(2,1)} %q_hbm.7, bf16[1024,1024]{1,0:T(8,128)(2,1)} %k_hbm.3, bf16[1024,1024]{1,0:T(8,128)(2,1)} %v_hbm.7), custom_call_target="tpu_custom_call" | custom-call | flops 4000000000 | bytes 10485760 | tf_op jit(solution)/shard_map/first_stage/pallas_call | solution.py:384
  17.9 7.2 %all-to-all-done.moments_ref = f32[8,256,128]{2,1,0:T(8,128)S(1)} async-done(((f32[8,256,128]{2,1,0:T(8,128)}), f32[8,256,128]{2,1,0:T(8,128)S(1)}, u32[]{:S(2)}, u32[]{:S(2)}) %all-to-all-start) | async-done | bytes 1048608 | tf_op jit(solution)/shard_map/all_to_all | solution.py:347
  25.2 3.5 %all-to-all-start.2 = ((f32[8,128,128]{2,1,0:T(8,128)}), f32[8,128,128]{2,1,0:T(8,128)S(1)}, u32[]{:S(2)}, u32[]{:S(2)}) async-start(f32[8,128,128]{2,1,0:T(8,128)} %bitcast.7), calls=%async_computation.2 | async-start | bytes 1048576 | tf_op jit(solution)/shard_map/all_to_all | solution.py:347
  28.7 0.4 owner_local.1
  29.1 4.5 %collective-permute-start = (f32[128,128]{1,0:T(8,128)S(1)}, f32[128,128]{1,0:T(8,128)S(1)}, u32[]{:S(2)}, u32[]{:S(2)}) collective-permute-start(f32[128,128]{1,0:T(8,128)S(1)} %slice_bitcast_fusion), channel_id=1, source_target_pairs={{0,16},{2,18},{4,20},{6,22},{8,24},{10,26},{12,28},{14,30},{1,17},... | collective-permute-start | bytes 196616 | tf_op jit(solution)/shard_map/ppermute | solution.py:404
  33.6 2.2 %collective-permute-done.before_ref = f32[128,128]{1,0:T(8,128)S(1)} collective-permute-done((f32[128,128]{1,0:T(8,128)S(1)}, f32[128,128]{1,0:T(8,128)S(1)}, u32[]{:S(2)}, u32[]{:S(2)}) %collective-permute-start) | collective-permute-done | bytes 65568 | tf_op jit(solution)/shard_map/ppermute | solution.py:404
  35.8 0.8 %owner_shift.1 = (f32[8,128,128]{2,1,0:T(8,128)}, f32[9,128,128]{2,1,0:T(8,128)S(1)}) custom-call(f32[9,128,128]{2,1,0:T(8,128)S(1)} %get-tuple-element.17.s_ref, f32[9,128,128]{2,1,0:T(8,128)S(1)} %get-tuple-element.18.c_ref, f32[9,128,128]{2,1,0:T(8,128)S(1)} %get-tuple-element.19.f_ref, f32[128,128]{1,0:T(8,128)S(1)} %collective-permute-done.before_ref), custom_call_target="tpu_custom_call" | custom-call | tf_op jit(solution)/shard_map/owner_shift/pallas_call | solution.py:405
  36.6 1.1 %all-to-all-done.2.d_ref = f32[8,128,128]{2,1,0:T(8,128)S(1)} async-done(((f32[8,128,128]{2,1,0:T(8,128)}), f32[8,128,128]{2,1,0:T(8,128)S(1)}, u32[]{:S(2)}, u32[]{:S(2)}) %all-to-all-start.2) | async-done | bytes 524320 | tf_op jit(solution)/shard_map/all_to_all | solution.py:347
  37.7 4.2 %all-to-all-start.1 = ((f32[8,128,128]{2,1,0:T(8,128)}), f32[8,128,128]{2,1,0:T(8,128)S(1)}, u32[]{:S(2)}, u32[]{:S(2)}) async-start(f32[8,128,128]{2,1,0:T(8,128)} %get-tuple-element.20), calls=%async_computation.1 | async-start | bytes 1048576 | tf_op jit(solution)/shard_map/all_to_all | solution.py:347
  42.0 0.1 owner_sum.1
  42.0 5.3 %collective-permute-start.1 = (f32[128,128]{1,0:T(8,128)S(1)}, f32[128,128]{1,0:T(8,128)S(1)}, u32[]{:S(2)}, u32[]{:S(2)}) collective-permute-start(f32[128,128]{1,0:T(8,128)S(1)} %get-tuple-element.24), channel_id=1, source_target_pairs={{0,16},{2,18},{4,20},{6,22},{8,24},{10,26},{12,28},{14,30},{1,17},... | collective-permute-start | bytes 196616 | tf_op jit(solution)/shard_map/ppermute | solution.py:421
  47.3 1.9 %collective-permute-done.1.before_ref = f32[128,128]{1,0:T(8,128)S(1)} collective-permute-done((f32[128,128]{1,0:T(8,128)S(1)}, f32[128,128]{1,0:T(8,128)S(1)}, u32[]{:S(2)}, u32[]{:S(2)}) %collective-permute-start.1) | collective-permute-done | bytes 65568 | tf_op jit(solution)/shard_map/ppermute | solution.py:421
  49.2 0.8 %owner_add.1 = f32[8,128,128]{2,1,0:T(8,128)} custom-call(f32[8,128,128]{2,1,0:T(8,128)S(1)} %get-tuple-element.23.base_ref, f32[128,128]{1,0:T(8,128)S(1)} %collective-permute-done.1.before_ref), custom_call_target="tpu_custom_call" | custom-call | tf_op jit(solution)/shard_map/owner_add/pallas_call | solution.py:422
  50.0 5.7 %all-to-all-start.3 = ((f32[8,128,128]{2,1,0:T(8,128)}), f32[8,128,128]{2,1,0:T(8,128)S(1)}, u32[]{:S(2)}, u32[]{:S(2)}) async-start(f32[8,128,128]{2,1,0:T(8,128)} %owner_add.1), calls=%async_computation.3 | async-start | bytes 1048576 | tf_op jit(solution)/shard_map/all_to_all | solution.py:347
  55.7 0.0 copy-start.2
  55.7 6.1 %second_early.1.num_hbm = f32[2,256,1024]{2,1,0:T(8,128)} custom-call(bf16[1024,1024]{1,0:T(8,128)(2,1)} %q_hbm.7, bf16[1024,1024]{1,0:T(8,128)(2,1)} %v_hbm.7, bf16[4,2,1024,256]{3,2,1,0:T(8,128)(2,1)} %get-tuple-element.16.r_hbm, f32[8,128,128]{2,1,0:T(8,128)} %copy-done), custom_call_target="tpu_custom_call" | custom-call | flops 2400000000 | bytes 6291456 | tf_op jit(solution)/shard_map/second_early/pallas_call | solution.py:427
  61.8 1.5 %all-to-all-done.3.d_ref = f32[8,128,128]{2,1,0:T(8,128)S(1)} async-done(((f32[8,128,128]{2,1,0:T(8,128)}), f32[8,128,128]{2,1,0:T(8,128)S(1)}, u32[]{:S(2)}, u32[]{:S(2)}) %all-to-all-start.3) | async-done | bytes 524320 | tf_op jit(solution)/shard_map/all_to_all | solution.py:347
  63.4 1.0 %copy-done.1 = f32[8,128,128]{2,1,0:T(8,128)S(1)} copy-done((f32[8,128,128]{2,1,0:T(8,128)S(1)}, f32[8,128,128]{2,1,0:T(8,128)}, u32[]{:S(2)}) %copy-start.1) | copy-done | bytes 524312
  64.4 6.8 %second_late.1 = (f32[4,256,1024]{2,1,0:T(8,128)}, f32[8,1024]{1,0:T(8,128)S(1)}) custom-call(bf16[1024,1024]{1,0:T(8,128)(2,1)} %q_hbm.7, bf16[1024,1024]{1,0:T(8,128)(2,1)} %v_hbm.7, bf16[4,2,1024,256]{3,2,1,0:T(8,128)(2,1)} %get-tuple-element.16.r_hbm, f32[8,128,128]{2,1,0:T(8,128)S(1)} %copy-done.1, f32[2,256,1024]{2,1,0:T(8,128)} %second_early.1.num_hbm, ...), custom_call_target="tpu_custom_call" | custom-call | tf_op jit(solution)/shard_map/second_late/pallas_call | solution.py:439
  71.2 0.1 collective-permute-start.2
  71.3 1.2 %collective-permute-done.2.other_ref = f32[8,1024]{1,0:T(8,128)S(1)} collective-permute-done((f32[8,1024]{1,0:T(8,128)S(1)}, f32[8,1024]{1,0:T(8,128)S(1)}, u32[]{:S(2)}, u32[]{:S(2)}) %collective-permute-start.2) | collective-permute-done | bytes 32800 | tf_op jit(solution)/shard_map/ppermute | solution.py:454
  72.5 3.3 %norm.1 = bf16[1024,1024]{1,0:T(8,128)(2,1)} custom-call(f32[4,256,1024]{2,1,0:T(8,128)} %get-tuple-element.25.y_hbm, f32[8,1024]{1,0:T(8,128)S(1)} %get-tuple-element.26.mine_ref, f32[8,1024]{1,0:T(8,128)S(1)} %collective-permute-done.2.other_ref), custom_call_target="tpu_custom_call" | custom-call | tf_op jit(solution)/shard_map/norm/pallas_call | solution.py:455
  (8 shorter events, 0.0 us)
Async XLA Ops:
  4.3 20.9 %all-to-all-start = ((f32[8,256,128]{2,1,0:T(8,128)}), f32[8,256,128]{2,1,0:T(8,128)S(1)}, u32[]{:S(2)}, u32[]{:S(2)}) async-start(f32[8,256,128]{2,1,0:T(8,128)} %bitcast.6), calls=%async_computation | async-start | bytes 2097152 | tf_op jit(solution)/shard_map/all_to_all | solution.py:347
  25.2 12.5 %all-to-all-start.2 = ((f32[8,128,128]{2,1,0:T(8,128)}), f32[8,128,128]{2,1,0:T(8,128)S(1)}, u32[]{:S(2)}, u32[]{:S(2)}) async-start(f32[8,128,128]{2,1,0:T(8,128)} %bitcast.7), calls=%async_computation.2 | async-start | bytes 1048576 | tf_op jit(solution)/shard_map/all_to_all | solution.py:347
  29.1 6.7 %collective-permute-start = (f32[128,128]{1,0:T(8,128)S(1)}, f32[128,128]{1,0:T(8,128)S(1)}, u32[]{:S(2)}, u32[]{:S(2)}) collective-permute-start(f32[128,128]{1,0:T(8,128)S(1)} %slice_bitcast_fusion), channel_id=1, source_target_pairs={{0,16},{2,18},{4,20},{6,22},{8,24},{10,26},{12,28},{14,30},{1,17},... | collective-permute-start | bytes 196616 | tf_op jit(solution)/shard_map/ppermute | solution.py:404
  37.7 12.3 %all-to-all-start.1 = ((f32[8,128,128]{2,1,0:T(8,128)}), f32[8,128,128]{2,1,0:T(8,128)S(1)}, u32[]{:S(2)}, u32[]{:S(2)}) async-start(f32[8,128,128]{2,1,0:T(8,128)} %get-tuple-element.20), calls=%async_computation.1 | async-start | bytes 1048576 | tf_op jit(solution)/shard_map/all_to_all | solution.py:347
  42.0 7.1 %collective-permute-start.1 = (f32[128,128]{1,0:T(8,128)S(1)}, f32[128,128]{1,0:T(8,128)S(1)}, u32[]{:S(2)}, u32[]{:S(2)}) collective-permute-start(f32[128,128]{1,0:T(8,128)S(1)} %get-tuple-element.24), channel_id=1, source_target_pairs={{0,16},{2,18},{4,20},{6,22},{8,24},{10,26},{12,28},{14,30},{1,17},... | collective-permute-start | bytes 196616 | tf_op jit(solution)/shard_map/ppermute | solution.py:421
  50.0 5.7 %copy-start = (f32[8,128,128]{2,1,0:T(8,128)}, f32[8,128,128]{2,1,0:T(8,128)S(1)}, u32[]{:S(2)}) copy-start(f32[8,128,128]{2,1,0:T(8,128)S(1)} %all-to-all-done.1.s_ref.s_hbm) | copy-start | bytes 1572868
  50.0 13.4 %all-to-all-start.3 = ((f32[8,128,128]{2,1,0:T(8,128)}), f32[8,128,128]{2,1,0:T(8,128)S(1)}, u32[]{:S(2)}, u32[]{:S(2)}) async-start(f32[8,128,128]{2,1,0:T(8,128)} %owner_add.1), calls=%async_computation.3 | async-start | bytes 1048576 | tf_op jit(solution)/shard_map/all_to_all | solution.py:347
  55.7 7.7 %copy-start.2 = (f32[1024]{0:T(1024)S(1)}, f32[1024]{0:T(1024)}, u32[]{:S(2)}) copy-start(f32[1024]{0:T(1024)} %param.9) | copy-start | bytes 12292
  55.7 7.7 %copy-start.3 = (f32[8]{0:T(128)S(1)}, f32[8]{0:T(128)}, u32[]{:S(2)}) copy-start(f32[8]{0:T(128)} %scale_ref.1) | copy-start | bytes 100
  63.4 1.0 %copy-start.1 = (f32[8,128,128]{2,1,0:T(8,128)S(1)}, f32[8,128,128]{2,1,0:T(8,128)}, u32[]{:S(2)}) copy-start(f32[8,128,128]{2,1,0:T(8,128)} %copy-done) | copy-start | bytes 1572868
  71.2 1.3 %collective-permute-start.2 = (f32[8,1024]{1,0:T(8,128)S(1)}, f32[8,1024]{1,0:T(8,128)S(1)}, u32[]{:S(2)}, u32[]{:S(2)}) collective-permute-start(f32[8,1024]{1,0:T(8,128)S(1)} %get-tuple-element.26.mine_ref), channel_id=1, source_target_pairs={{0,1},{1,0},{2,3},{3,2},{4,5},{5,4},{6,7},{7,6},{8,9},{9,8},{10,11... | collective-permute-start | bytes 98312 | tf_op jit(solution)/shard_map/ppermute | solution.py:454

commit v7 on v6

--- a/solution.py
+++ b/solution.py
@@ -10,6 +10,8 @@
 BLK = 128
 CHUNK = 256
 PAIR = 2
+HALF = BLK // 2
+PACKED = HALF + 8
 SMALL = 8 * 1024 * 1024
 LARGE = 60 * 1024 * 1024
 LATE = 52 * 1024 * 1024
@@ -53,6 +55,29 @@
 
 def span(j, size=BLK):
     return slice(j * size, (j + 1) * size)
+
+
+def half_indices():
+    shape = (HALF, BLK)
+    return lax.broadcasted_iota(jnp.int32, shape, 0), lax.broadcasted_iota(jnp.int32, shape, 1)
+
+
+def pack(s):
+    row, lane = half_indices()
+    corner = pltpu.roll(s[HALF:], HALF, 1)
+    diagonal = jnp.sum(jnp.where(lane == row, corner, 0.0), axis=0, keepdims=True)
+    return rows(jnp.where(lane >= row, s[:HALF], corner), jnp.broadcast_to(diagonal, (8, BLK)))
+
+
+def unpack(packed):
+    row, lane = half_indices()
+    top, diagonal = packed[:HALF], packed[HALF : HALF + 1]
+    flipped = rows(top, jnp.zeros_like(top)).T
+    corner = jnp.where(lane < row, top, jnp.where(lane == row, diagonal, flipped[:HALF]))
+    return rows(
+        jnp.where(lane >= row, top, flipped[:HALF]),
+        jnp.where(lane < HALF, flipped[HALF:], pltpu.roll(corner, HALF, 1)),
+    )
 
 
 def columns(p):
@@ -83,10 +108,6 @@
 
 def by_pair(ref):
     return lambda p: ref.at[p]
-
-
-def by_mats(ref):
-    return lambda p: ref.at[pl.ds(p * PAIR, PAIR)]
 
 
 def moments_kernel(q_hbm, k_hbm, v_hbm, m_hbm, q_ref, k_ref, v_ref, m_ref, read_sems, write_sems):
@@ -98,8 +119,8 @@
         wait(reads, read_sems, p)
         for j in range(PAIR):
             k = k_ref[p, :, span(j)]
-            m_ref[p, j, :BLK] = dot(k.T, k)
-            m_ref[p, j, BLK:] = dot(v_ref[p, :, span(j)].T, q_ref[p, :, span(j)])
+            m_ref[p, j, :PACKED] = pack(dot(k.T, k))
+            m_ref[p, j, PACKED:] = dot(v_ref[p, :, span(j)].T, q_ref[p, :, span(j)])
         start(writes, write_sems, p, p + 1)
     for p in range(pairs):
         wait(writes, write_sems, p)
@@ -158,12 +179,11 @@
         wait(writes, write_sems, p)
 
 
-def second_stage(p, q_ref, v_ref, r_ref, s_ref, a_ref, first, store):
+def second_stage(p, q_ref, v_ref, r_ref, s_both, a_ref, first, store):
     tokens = q_ref.shape[1]
     steps = tokens // CHUNK
     units = chunk_units(tokens)
     mask = ordered(CHUNK) <= 0
-    s_both = [rows(*split(s_ref[p * PAIR + j])) for j in range(PAIR)]
     for j in range(PAIR):
         for i in range(steps):
             at = span(i, CHUNK)
@@ -181,79 +201,35 @@
     states = [running(sums[j], first[j]) for j in range(PAIR)]
     for i, j, at, cols in units:
         vt = v_ref[p, at, cols].T
-        num = dot(lanes(vt, vt), a_ref[j, i])
-        if states[j][i] is not None:
-            qt = q_ref[p, at, cols].T
-            num = num + dot(lanes(*split(states[j][i])), rows(qt, qt))
+        qt = q_ref[p, at, cols].T
+        num = dot(lanes(vt, vt), a_ref[j, i]) + dot(lanes(*split(states[j][i])), rows(qt, qt))
         store(i, j, num)
 
 
-def early_kernel(
-    q_hbm, v_hbm, r_hbm, s_ref, num_hbm, q_ref, v_ref, r_ref, num_ref, a_ref, read_sems, write_sems
+def second_stage_kernel(
+    q_hbm, v_hbm, r_hbm, back_ref, gain_ref, scale_ref, y_hbm, part_ref,
+    q_ref, v_ref, r_ref, y_ref, gains_ref, a_ref, read_sems, write_sems
 ):
     pairs = q_ref.shape[0]
     reads = [(by_columns(q_hbm), by_pair(q_ref)), (by_pair(r_hbm), by_pair(r_ref)), (by_columns(v_hbm), by_pair(v_ref))]
-    writes = [(by_pair(num_ref), by_pair(num_hbm))]
+    writes = [(by_pair(y_ref), by_pair(y_hbm))]
     start(reads, read_sems, 0, pairs)
-
-    @pl.loop(0, pairs)
-    def _(p):
-        wait(reads, read_sems, p)
-
-        def store(i, j, num):
-            num_ref[p, span(j), span(i, CHUNK)] = num
-
-        second_stage(p, q_ref, v_ref, r_ref, s_ref, a_ref, [None] * PAIR, store)
-        for copy in copies(writes, write_sems, p):
-            copy.start()
-
-    for p in range(pairs):
-        wait(writes, write_sems, p)
-
-
-def late_kernel(
-    q_hbm, v_hbm, r_hbm, s_hbm, num_hbm, d_ref, gain_ref, scale_ref, y_hbm, part_ref,
-    q_ref, v_ref, r_ref, s_ref, num_ref, y_ref, gains_ref, a_ref, early_sems, late_sems, write_sems
-):
-    pairs = q_ref.shape[0]
-    early = num_ref.shape[0]
-    tokens = q_ref.shape[1]
-    reads_early = [(by_columns(q_hbm), by_pair(q_ref)), (by_pair(num_hbm), by_pair(num_ref))]
-    reads_late = [
-        (by_columns(q_hbm), by_pair(q_ref)),
-        (by_columns(v_hbm), by_pair(v_ref)),
-        (by_pair(r_hbm), by_pair(r_ref)),
-        (by_mats(s_hbm), by_mats(s_ref)),
-    ]
-    writes = [(by_pair(y_ref), by_pair(y_hbm))]
-    start(reads_late, late_sems, early, pairs)
-    start(reads_early, early_sems, 0, early)
     part_ref[...] = jnp.zeros_like(part_ref)
     for h in range(pairs * PAIR):
         gains_ref[h] = jnp.broadcast_to(gain_ref[h], (BLK, BLK)).T
 
-    def finish(p, i, j, num):
-        h = p * PAIR + j
-        y = num * scale_ref[h]
-        part_ref[:, span(i, CHUNK)] += jnp.sum((y * y).reshape(BLK // 8, 8, CHUNK), axis=0)
-        y_ref[p, span(j), span(i, CHUNK)] = y * lanes(*[gains_ref[h]] * (CHUNK // BLK))
-
-    @pl.loop(early, pairs)
+    @pl.loop(0, pairs)
     def _(p):
-        wait(reads_late, late_sems, p)
-        states = [d_ref[p * PAIR + j] for j in range(PAIR)]
-        second_stage(p, q_ref, v_ref, r_ref, s_ref, a_ref, states, functools.partial(finish, p))
-        for copy in copies(writes, write_sems, p):
-            copy.start()
-
-    @pl.loop(0, early)
-    def _(p):
-        wait(reads_early, early_sems, p)
-        for j in range(PAIR):
-            before = lanes(*split(d_ref[p * PAIR + j]))
-            for i in range(tokens // CHUNK):
-                qt = q_ref[p, span(i, CHUNK), span(j)].T
-                finish(p, i, j, num_ref[p, span(j), span(i, CHUNK)] + dot(before, rows(qt, qt)))
+        def finish(i, j, num):
+            h = p * PAIR + j
+            y = num * scale_ref[h]
+            part_ref[:, span(i, CHUNK)] += jnp.sum((y * y).reshape(BLK // 8, 8, CHUNK), axis=0)
+            y_ref[p, span(j), span(i, CHUNK)] = y * lanes(*[gains_ref[h]] * (CHUNK // BLK))
+
+        backs = [back_ref[p * PAIR + j] for j in range(PAIR)]
+        s_both = [rows(*split(unpack(back[:PACKED]))) for back in backs]
+        wait(reads, read_sems, p)
+        second_stage(p, q_ref, v_ref, r_ref, s_both, a_ref, [back[PACKED:] for back in backs], finish)
         for copy in copies(writes, write_sems, p):
             copy.start()
 
@@ -268,36 +244,30 @@
     f = jnp.zeros((BLK, BLK), f32)
     for m in range(members):
         s_ref[m], c_ref[m], f_ref[m] = s, c, f
-        c_own = moments_ref[m, BLK:]
+        c_own = moments_ref[m, PACKED:]
         if m > 0:
             f = f + dot_f32(c_own, s)
-        s = s + moments_ref[m, :BLK]
+        s = s + unpack(moments_ref[m, :PACKED])
         c = c + c_own
     s_ref[members], c_ref[members], f_ref[members] = s, c, f
 
 
-def owner_shift_kernel(s_ref, c_ref, f_ref, before_ref, back_ref, out_ref):
-    members = back_ref.shape[0]
-    before = before_ref[...]
-    for m in range(members):
-        back_ref[m] = s_ref[m] + before
-    out_ref[0] = f_ref[0]
-    for m in range(1, members + 1):
-        out_ref[m] = f_ref[m] + dot_f32(c_ref[m], before)
-
-
-def owner_sum_kernel(d_ref, h_ref, base_ref, total_ref):
+def owner_sum_kernel(d_ref, s_ref, f_ref, base_ref, total_ref):
     members = d_ref.shape[0]
     d = jnp.zeros((BLK, BLK), f32)
     for m in range(members):
-        base_ref[m] = h_ref[m] + d
+        base_ref[m] = f_ref[m] + d
         d = d + d_ref[m]
-    total_ref[...] = h_ref[members] + d
-
-
-def add_kernel(base_ref, before_ref, out_ref):
-    for m in range(out_ref.shape[0]):
-        out_ref[m] = base_ref[m] + before_ref[...]
+    total_ref[:BLK] = s_ref[members]
+    total_ref[BLK:] = f_ref[members] + d
+
+
+def owner_back_kernel(s_ref, c_ref, base_ref, before_ref, back_ref):
+    s_before, d_before = before_ref[:BLK], before_ref[BLK:]
+    for m in range(back_ref.shape[0]):
+        back_ref[m, :PACKED] = pack(s_ref[m] + s_before)
+        d = base_ref[m] + d_before
+        back_ref[m, PACKED:] = d if m == 0 else d + dot_f32(c_ref[m], s_before)
 
 
 def norm_kernel(features, y_hbm, mine_ref, other_ref, out_hbm, y_ref, out_ref, read_sems, write_sems):
@@ -347,22 +317,17 @@
         return lax.all_to_all(a, "seq", 0, 0, axis_index_groups=index_groups)
 
     mats = lambda n: jax.ShapeDtypeStruct((n, BLK, BLK), f32)
-    mat = jax.ShapeDtypeStruct((BLK, BLK), f32)
     pairs = heads // PAIR
-    early = pairs // 2
     shape = jax.ShapeDtypeStruct
     upright = shape((pairs, tokens, PAIR * BLK), bf16)
     turned_f32 = shape((pairs, PAIR * BLK, tokens), f32)
     twofold = shape((pairs, PAIR, tokens, 2 * BLK), bf16)
     pair_mats = shape((pairs, PAIR, BLK, BLK), f32)
     scores = shape((PAIR, tokens // CHUNK, 2 * CHUNK, CHUNK), bf16)
-    moment_mats = shape((pairs, PAIR, 2 * BLK, BLK), f32)
+    moment_mats = shape((pairs, PAIR, PACKED + BLK, BLK), f32)
     anywhere = pl.BlockSpec(memory_space=pl.ANY)
     in_vmem = pl.BlockSpec(memory_space=pltpu.VMEM)
     in_smem = pl.BlockSpec(memory_space=pltpu.SMEM)
-
-    def cut(a, n):
-        return shape((n,) + a.shape[1:], a.dtype)
 
     def vmem(*arrays):
         return [pltpu.VMEM(a.shape, a.dtype) for a in arrays]
@@ -379,7 +344,7 @@
         compiler_params=params(LARGE),
         name="moments",
     )(query_rows, key_rows, value_rows)
-    moments_in = swap(moments.reshape(heads, 2 * BLK, BLK))
+    moments_in = swap(moments.reshape(heads, PACKED + BLK, BLK))
 
     r_local, d_local = pl.pallas_call(
         first_stage_kernel,
@@ -399,55 +364,36 @@
         compiler_params=params(),
         name="owner_local",
     )(moments_in)
-    s_before = jnp.zeros((BLK, BLK), f32)
-    for _ in range(groups - 1):
-        s_before = lax.ppermute(s_before + s_part[members], "seq", onward)
-    s_back, h_part = pl.pallas_call(
-        owner_shift_kernel,
-        out_shape=[mats(members), mats(members + 1)],
-        compiler_params=params(),
-        name="owner_shift",
-    )(s_part, c_part, f_part, s_before)
-    s_pre = swap(s_back)
-
-    d_base, d_total = pl.pallas_call(
+    d_base, total = pl.pallas_call(
         owner_sum_kernel,
-        out_shape=[mats(members), mat],
+        out_shape=[mats(members), shape((2 * BLK, BLK), f32)],
         compiler_params=params(),
         name="owner_sum",
-    )(d_in, h_part)
-    d_before = jnp.zeros((BLK, BLK), f32)
-    for _ in range(groups - 1):
-        d_before = lax.ppermute(d_before + d_total, "seq", onward)
-    d_back = pl.pallas_call(
-        add_kernel, out_shape=mats(members), compiler_params=params(), name="owner_add"
-    )(d_base, d_before)
-    d_pre = swap(d_back)
-
-    num = pl.pallas_call(
-        early_kernel,
-        in_specs=[anywhere] * 3 + [in_vmem],
-        out_specs=anywhere,
-        out_shape=cut(turned_f32, early),
-        scratch_shapes=vmem(*[cut(a, early) for a in (upright, upright, twofold, turned_f32)], scores) + sems(3, 1),
-        compiler_params=params(LARGE),
-        cost_estimate=cost(6, 6 * tokens * width),
-        name="second_early",
-    )(query_rows, value_rows, r_local, s_pre)
+    )(d_in, s_part, f_part)
+    before = jnp.zeros_like(total)
+    for turn in range(groups - 1):
+        if turn > 0:
+            crossed = jnp.dot(c_part[members], before[:BLK], precision=lax.Precision.HIGHEST)
+            before = before + jnp.concatenate([jnp.zeros_like(crossed), crossed])
+        before = lax.ppermute(before + total, "seq", onward)
+    back = pl.pallas_call(
+        owner_back_kernel,
+        out_shape=shape((members, PACKED + BLK, BLK), f32),
+        compiler_params=params(),
+        name="owner_back",
+    )(s_part, c_part, d_base, before)
+    back_in = swap(back)
 
     part_shape = shape((8, tokens), f32)
     y, part = pl.pallas_call(
-        late_kernel,
-        in_specs=[anywhere] * 5 + [in_vmem, in_vmem, in_smem],
+        second_stage_kernel,
+        in_specs=[anywhere] * 3 + [in_vmem, in_vmem, in_smem],
         out_specs=[anywhere, in_vmem],
         out_shape=[turned_f32, part_shape],
-        scratch_shapes=vmem(
-            upright, upright, twofold, mats(heads), cut(turned_f32, early), turned_f32, mats(heads), scores
-        )
-        + sems(2, 4, 1),
+        scratch_shapes=vmem(upright, upright, twofold, turned_f32, mats(heads), scores) + sems(3, 1),
         compiler_params=params(LATE),
-        name="second_late",
-    )(query_rows, value_rows, r_local, s_pre, num, d_pre, out_gain.reshape(heads, 1, BLK), head_scale)
+        name="second_stage",
+    )(query_rows, value_rows, r_local, back_in, out_gain.reshape(heads, 1, BLK), head_scale)
     shards = lax.axis_size("head")
     other = jnp.zeros_like(part)
     for turn in range(1, shards):

time: 76.2 us -> 74.1 us (0.972)
  blocking collectives: 0 us -> 18.1 us
  starting transfers between devices: 29.4 us -> 14.3 us
  Pallas kernels: 30 us -> 24.9 us
  waiting for transfers between devices: 15.1 us -> 16.4 us
  local copies, waits for them, and re-layouts: 1.07 us -> 0.01 us
    all_to_all x0 -> x1, blocking collectives: none -> 18.1 us  [swap(): return lax.all_to_all(a, 'seq', 0, 0, axis_index_groups=index_groups)]
    all_to_all x4 -> x2, starting transfers between devices: 19.6 us -> 9.69 us  [swap(): return lax.all_to_all(a, 'seq', 0, 0, axis_index_groups=index_groups)]
    pallas_call x5 -> x3, Pallas kernels: 14.6 us -> 9.29 us  [the longest x1 8.89 us: per_device(): pl.pallas_call(second_stage_kernel, in_specs=[anywhere] * 3 + [in_vmem, i...]
    ppermute x2 -> x1, starting transfers between devices: 9.75 us -> 4.5 us  [per_device(): before = lax.ppermute(before + total, 'seq', onward)]
    all_to_all x4 -> x2, waiting for transfers between devices: 9.84 us -> 12.7 us  [swap(): return lax.all_to_all(a, 'seq', 0, 0, axis_index_groups=index_groups)]
    ppermute x2 -> x1, waiting for transfers between devices: 4.09 us -> 2.51 us  [per_device(): before = lax.ppermute(before + total, 'seq', onward)]
    unnamed x8 -> x4, local copies, waits for them, and re-layouts: 1.06 us -> 0.01 us
  transfers between devices with their start and end apart: 7 -> 4, of which waited for: 6 -> 4; matrix products, arithmetic and copies ran while one was open for 0% -> 0% of each run, Pallas kernels for 21% -> 11%
where the time goes in v7:
time: 74.1 us; the launch traced here: 73.7 us
  Pallas kernels  24.9 us (34%)
  blocking collectives  18.1 us (24%)
  waiting for transfers between devices  16.4 us (22%)
  starting transfers between devices  14.3 us (19%)
    all_to_all x1, blocking collectives, swap(): return lax.all_to_all(a, 'seq', 0, 0, axis_index_groups=index_groups)  18.1 us
    all_to_all x2, waiting for transfers between devices, swap(): return lax.all_to_all(a, 'seq', 0, 0, axis_index_groups=index_groups)  12.7 us
    all_to_all x2, starting transfers between devices, swap(): return lax.all_to_all(a, 'seq', 0, 0, axis_index_groups=index_groups)  9.69 us
    pallas_call x1, Pallas kernels, per_device(): pl.pallas_call(second_stage_kernel, in_specs=[anywhere] * 3 + [in_vmem, i...  8.89 us
    pallas_call x1, Pallas kernels, per_device(): pl.pallas_call(first_stage_kernel, in_specs=[anywhere] * 3, out_specs=[an...  7.44 us
    ppermute x1, starting transfers between devices, per_device(): before = lax.ppermute(before + total, 'seq', onward)  4.5 us
    pallas_call x1, Pallas kernels, per_device(): pl.pallas_call(moments_kernel, in_specs=[anywhere] * 3, out_specs=anywher...  4.24 us
    pallas_call x1, Pallas kernels, per_device(): pl.pallas_call(functools.partial(norm_kernel, width * shards), in_specs=[...  3.26 us
  transfers between devices with their start and end apart: 4, of which 4 were waited for; matrix products, arithmetic and copies ran while one was open for 0% of the time, Pallas kernels for 11%

profile of v7, /device:TPU:0, one launch (start us, length us, event | category | flops | bytes accessed | tf_op | source)
XLA Modules:
  0.0 73.7 jit_solution(17029408352559507642)
XLA Ops:
  0.0 4.2 %moments.1 = f32[4,2,200,128]{3,2,1,0:T(8,128)} custom-call(bf16[1024,1024]{1,0:T(8,128)(2,1)} %q_hbm.5, bf16[1024,1024]{1,0:T(8,128)(2,1)} %k_hbm.3, bf16[1024,1024]{1,0:T(8,128)(2,1)} %v_hbm.5), custom_call_target="tpu_custom_call" | custom-call | tf_op jit(solution)/shard_map/moments/pallas_call | solution.py:338
  4.2 6.2 %all-to-all-start = ((f32[8,200,128]{2,1,0:T(8,128)}), f32[8,200,128]{2,1,0:T(8,128)S(1)}, u32[]{:S(2)}, u32[]{:S(2)}) async-start(f32[8,200,128]{2,1,0:T(8,128)} %bitcast.4), calls=%async_computation | async-start | bytes 1638400 | tf_op jit(solution)/shard_map/all_to_all | solution.py:317
  10.4 7.4 %first_stage.1 = (bf16[4,2,1024,256]{3,2,1,0:T(8,128)(2,1)}, f32[4,2,128,128]{3,2,1,0:T(8,128)}) custom-call(bf16[1024,1024]{1,0:T(8,128)(2,1)} %q_hbm.5, bf16[1024,1024]{1,0:T(8,128)(2,1)} %k_hbm.3, bf16[1024,1024]{1,0:T(8,128)(2,1)} %v_hbm.5), custom_call_target="tpu_custom_call" | custom-call | flops 4000000000 | bytes 10485760 | tf_op jit(solution)/shard_map/first_stage/pallas_call | solution.py:349
  17.9 4.6 %all-to-all-done.moments_ref = f32[8,200,128]{2,1,0:T(8,128)S(1)} async-done(((f32[8,200,128]{2,1,0:T(8,128)}), f32[8,200,128]{2,1,0:T(8,128)S(1)}, u32[]{:S(2)}, u32[]{:S(2)}) %all-to-all-start) | async-done | bytes 819232 | tf_op jit(solution)/shard_map/all_to_all | solution.py:317
  22.5 3.5 %all-to-all-start.1 = ((f32[8,128,128]{2,1,0:T(8,128)}), f32[8,128,128]{2,1,0:T(8,128)S(1)}, u32[]{:S(2)}, u32[]{:S(2)}) async-start(f32[8,128,128]{2,1,0:T(8,128)} %bitcast.5), calls=%async_computation.1 | async-start | bytes 1048576 | tf_op jit(solution)/shard_map/all_to_all | solution.py:317
  26.0 0.6 owner_local.1
  26.7 8.1 %all-to-all-done.1.d_ref = f32[8,128,128]{2,1,0:T(8,128)S(1)} async-done(((f32[8,128,128]{2,1,0:T(8,128)}), f32[8,128,128]{2,1,0:T(8,128)S(1)}, u32[]{:S(2)}, u32[]{:S(2)}) %all-to-all-start.1) | async-done | bytes 524320 | tf_op jit(solution)/shard_map/all_to_all | solution.py:317
  34.7 0.1 owner_sum.1
  34.8 4.5 %collective-permute-start = (f32[256,128]{1,0:T(8,128)S(1)}, f32[256,128]{1,0:T(8,128)S(1)}, u32[]{:S(2)}, u32[]{:S(2)}) collective-permute-start(f32[256,128]{1,0:T(8,128)S(1)} %get-tuple-element.20), channel_id=1, source_target_pairs={{0,16},{2,18},{4,20},{6,22},{8,24},{10,26},{12,28},{14,30},{1,17},... | collective-permute-start | bytes 393224 | tf_op jit(solution)/shard_map/ppermute | solution.py:378
  39.3 2.5 %collective-permute-done.before_ref = f32[256,128]{1,0:T(8,128)S(1)} collective-permute-done((f32[256,128]{1,0:T(8,128)S(1)}, f32[256,128]{1,0:T(8,128)S(1)}, u32[]{:S(2)}, u32[]{:S(2)}) %collective-permute-start) | collective-permute-done | bytes 131104 | tf_op jit(solution)/shard_map/ppermute | solution.py:378
  41.8 0.0 copy-start
  41.8 0.0 copy-start.1
  41.8 0.3 owner_back.1
  42.2 18.1 %all_to_all.15.back_ref = f32[8,200,128]{2,1,0:T(8,128)S(1)} all-to-all(f32[8,200,128]{2,1,0:T(8,128)S(1)} %owner_back.1), channel_id=1, replica_groups={{0,2,4,6,8,10,12,14},{16,18,20,22,24,26,28,30},{1,3,5,7,9,11,13,15},{17..., dimensions={0} | all-to-all | bytes 1638400 | tf_op jit(solution)/shard_map/all_to_all | solution.py:317
  60.3 0.0 copy-done
  60.3 0.0 copy-done.1
  60.3 8.9 %second_stage.1 = (f32[4,256,1024]{2,1,0:T(8,128)}, f32[8,1024]{1,0:T(8,128)S(1)}) custom-call(bf16[1024,1024]{1,0:T(8,128)(2,1)} %q_hbm.5, bf16[1024,1024]{1,0:T(8,128)(2,1)} %v_hbm.5, bf16[4,2,1024,256]{3,2,1,0:T(8,128)(2,1)} %get-tuple-element.14.r_hbm, f32[8,200,128]{2,1,0:T(8,128)S(1)} %all_to_all.15.back_ref, f32[8,1,128]{2,1,0:T(1,128)S(1)} %bitcast.3, ...), custom_call_target="tpu_custom_call" | custom-call | tf_op jit(solution)/shard_map/second_stage/pallas_call | solution.py:388
  69.2 0.1 collective-permute-start.1
  69.3 1.2 %collective-permute-done.1.other_ref = f32[8,1024]{1,0:T(8,128)S(1)} collective-permute-done((f32[8,1024]{1,0:T(8,128)S(1)}, f32[8,1024]{1,0:T(8,128)S(1)}, u32[]{:S(2)}, u32[]{:S(2)}) %collective-permute-start.1) | collective-permute-done | bytes 32800 | tf_op jit(solution)/shard_map/ppermute | solution.py:400
  70.5 3.3 %norm.1 = bf16[1024,1024]{1,0:T(8,128)(2,1)} custom-call(f32[4,256,1024]{2,1,0:T(8,128)} %get-tuple-element.21.y_hbm, f32[8,1024]{1,0:T(8,128)S(1)} %get-tuple-element.22.mine_ref, f32[8,1024]{1,0:T(8,128)S(1)} %collective-permute-done.1.other_ref), custom_call_target="tpu_custom_call" | custom-call | tf_op jit(solution)/shard_map/norm/pallas_call | solution.py:401
Async XLA Ops:
  4.2 18.3 %all-to-all-start = ((f32[8,200,128]{2,1,0:T(8,128)}), f32[8,200,128]{2,1,0:T(8,128)S(1)}, u32[]{:S(2)}, u32[]{:S(2)}) async-start(f32[8,200,128]{2,1,0:T(8,128)} %bitcast.4), calls=%async_computation | async-start | bytes 1638400 | tf_op jit(solution)/shard_map/all_to_all | solution.py:317
  22.5 12.2 %all-to-all-start.1 = ((f32[8,128,128]{2,1,0:T(8,128)}), f32[8,128,128]{2,1,0:T(8,128)S(1)}, u32[]{:S(2)}, u32[]{:S(2)}) async-start(f32[8,128,128]{2,1,0:T(8,128)} %bitcast.5), calls=%async_computation.1 | async-start | bytes 1048576 | tf_op jit(solution)/shard_map/all_to_all | solution.py:317
  34.8 7.0 %collective-permute-start = (f32[256,128]{1,0:T(8,128)S(1)}, f32[256,128]{1,0:T(8,128)S(1)}, u32[]{:S(2)}, u32[]{:S(2)}) collective-permute-start(f32[256,128]{1,0:T(8,128)S(1)} %get-tuple-element.20), channel_id=1, source_target_pairs={{0,16},{2,18},{4,20},{6,22},{8,24},{10,26},{12,28},{14,30},{1,17},... | collective-permute-start | bytes 393224 | tf_op jit(solution)/shard_map/ppermute | solution.py:378
  41.8 18.5 %copy-start = (f32[1024]{0:T(1024)S(1)}, f32[1024]{0:T(1024)}, u32[]{:S(2)}) copy-start(f32[1024]{0:T(1024)} %param.9) | copy-start | bytes 12292
  41.8 18.5 %copy-start.1 = (f32[8]{0:T(128)S(1)}, f32[8]{0:T(128)}, u32[]{:S(2)}) copy-start(f32[8]{0:T(128)} %scale_ref.1) | copy-start | bytes 100
  69.2 1.3 %collective-permute-start.1 = (f32[8,1024]{1,0:T(8,128)S(1)}, f32[8,1024]{1,0:T(8,128)S(1)}, u32[]{:S(2)}, u32[]{:S(2)}) collective-permute-start(f32[8,1024]{1,0:T(8,128)S(1)} %get-tuple-element.22.mine_ref), channel_id=1, source_target_pairs={{0,1},{1,0},{2,3},{3,2},{4,5},{5,4},{6,7},{7,6},{8,9},{9,8},{10,11... | collective-permute-start | bytes 98312 | tf_op jit(solution)/shard_map/ppermute | solution.py:400

commit v8 on v7

--- a/solution.py
+++ b/solution.py
@@ -12,6 +12,8 @@
 PAIR = 2
 HALF = BLK // 2
 PACKED = HALF + 8
+TWO = PACKED + BLK
+THREE = TWO + BLK
 SMALL = 8 * 1024 * 1024
 LARGE = 60 * 1024 * 1024
 LATE = 52 * 1024 * 1024
@@ -110,22 +112,6 @@
     return lambda p: ref.at[p]
 
 
-def moments_kernel(q_hbm, k_hbm, v_hbm, m_hbm, q_ref, k_ref, v_ref, m_ref, read_sems, write_sems):
-    pairs = q_ref.shape[0]
-    reads = [(by_columns(a), by_pair(b)) for a, b in ((k_hbm, k_ref), (v_hbm, v_ref), (q_hbm, q_ref))]
-    writes = [(by_pair(m_ref), by_pair(m_hbm))]
-    start(reads, read_sems, 0, pairs)
-    for p in range(pairs):
-        wait(reads, read_sems, p)
-        for j in range(PAIR):
-            k = k_ref[p, :, span(j)]
-            m_ref[p, j, :PACKED] = pack(dot(k.T, k))
-            m_ref[p, j, PACKED:] = dot(v_ref[p, :, span(j)].T, q_ref[p, :, span(j)])
-        start(writes, write_sems, p, p + 1)
-    for p in range(pairs):
-        wait(writes, write_sems, p)
-
-
 def running(parts, first=None):
     totals = [first]
     for part in parts:
@@ -142,14 +128,14 @@
 
 
 def first_stage_kernel(
-    q_hbm, k_hbm, v_hbm, r_hbm, d_hbm, q_ref, k_ref, v_ref, r_ref, d_ref, a_ref, read_sems, write_sems
+    q_hbm, k_hbm, v_hbm, r_hbm, m_hbm, q_ref, k_ref, v_ref, r_ref, m_ref, a_ref, read_sems, write_sems
 ):
     pairs, tokens, _ = q_ref.shape
     steps = tokens // CHUNK
     units = chunk_units(tokens)
     mask = ordered(CHUNK) <= 0
     reads = [(by_columns(a), by_pair(b)) for a, b in ((q_hbm, q_ref), (k_hbm, k_ref), (v_hbm, v_ref))]
-    writes = [(by_pair(r_ref), by_pair(r_hbm)), (by_pair(d_ref), by_pair(d_hbm))]
+    writes = [(by_pair(m_ref), by_pair(m_hbm)), (by_pair(r_ref), by_pair(r_hbm))]
     start(reads, read_sems, 0, pairs)
 
     @pl.loop(0, pairs)
@@ -160,8 +146,9 @@
             a_ref[j, i] = rows(*split(jnp.where(mask, a, 0.0)))
         states = []
         for j in range(PAIR):
-            blocks = [k_ref[p, span(i, CHUNK), span(j)] for i in range(steps - 1)]
+            blocks = [k_ref[p, span(i, CHUNK), span(j)] for i in range(steps)]
             states.append(running([dot(k.T, k) for k in blocks]))
+            m_ref[p, j, :PACKED] = pack(states[j][steps])
         for i, j, at, cols in units:
             kt = k_ref[p, at, cols].T
             r = dot(lanes(kt, kt), a_ref[j, i])
@@ -171,7 +158,9 @@
             r_high, r_low = split(r)
             r_ref[p, j, at] = lanes(r_high.T, r_low.T)
         for j in range(PAIR):
-            d_ref[p, j] = halves_sum(dot(v_ref[p, :, span(j)].T, r_ref[p, j]))
+            vt = v_ref[p, :, span(j)].T
+            m_ref[p, j, PACKED:TWO] = dot(vt, q_ref[p, :, span(j)])
+            m_ref[p, j, TWO:] = halves_sum(dot(vt, r_ref[p, j]))
         for copy in copies(writes, write_sems, p):
             copy.start()
 
@@ -237,35 +226,36 @@
         wait(writes, write_sems, p)
 
 
-def owner_local_kernel(moments_ref, s_ref, c_ref, f_ref):
+def owner_kernel(moments_ref, s_ref, c_ref, base_ref, total_ref):
     members = moments_ref.shape[0]
-    s = jnp.zeros((BLK, BLK), f32)
+    packed = jnp.zeros((PACKED, BLK), f32)
     c = jnp.zeros((BLK, BLK), f32)
-    f = jnp.zeros((BLK, BLK), f32)
-    for m in range(members):
-        s_ref[m], c_ref[m], f_ref[m] = s, c, f
-        c_own = moments_ref[m, PACKED:]
-        if m > 0:
-            f = f + dot_f32(c_own, s)
-        s = s + unpack(moments_ref[m, :PACKED])
-        c = c + c_own
-    s_ref[members], c_ref[members], f_ref[members] = s, c, f
-
-
-def owner_sum_kernel(d_ref, s_ref, f_ref, base_ref, total_ref):
-    members = d_ref.shape[0]
     d = jnp.zeros((BLK, BLK), f32)
     for m in range(members):
-        base_ref[m] = f_ref[m] + d
-        d = d + d_ref[m]
-    total_ref[:BLK] = s_ref[members]
-    total_ref[BLK:] = f_ref[members] + d
+        s_ref[m], c_ref[m], base_ref[m] = packed, c, d
+        c_own = moments_ref[m, PACKED:TWO]
+        d = d + moments_ref[m, TWO:]
+        if m > 0:
+            d = d + dot_f32(c_own, unpack(packed))
+        packed = packed + moments_ref[m, :PACKED]
+        c = c + c_own
+    c_ref[members] = c
+    total_ref[:PACKED] = packed
+    total_ref[PACKED:] = d
+
+
+def owner_onward_kernel(c_ref, total_ref, before_ref, out_ref):
+    s_before = before_ref[:PACKED]
+    out_ref[:PACKED] = total_ref[:PACKED] + s_before
+    crossed = dot_f32(c_ref[c_ref.shape[0] - 1], unpack(s_before))
+    out_ref[PACKED:] = total_ref[PACKED:] + before_ref[PACKED:] + crossed
 
 
 def owner_back_kernel(s_ref, c_ref, base_ref, before_ref, back_ref):
-    s_before, d_before = before_ref[:BLK], before_ref[BLK:]
+    packed, d_before = before_ref[:PACKED], before_ref[PACKED:]
+    s_before = unpack(packed)
     for m in range(back_ref.shape[0]):
-        back_ref[m, :PACKED] = pack(s_ref[m] + s_before)
+        back_ref[m, :PACKED] = s_ref[m] + packed
         d = base_ref[m] + d_before
         back_ref[m, PACKED:] = d if m == 0 else d + dot_f32(c_ref[m], s_before)
 
@@ -300,10 +290,6 @@
     return pltpu.CompilerParams(vmem_limit_bytes=limit)
 
 
-def cost(us, moved):
-    return pl.CostEstimate(flops=int(us * 4e8), bytes_accessed=int(moved), transcendentals=0)
-
-
 def per_device(query_rows, key_rows, value_rows, head_scale, out_gain):
     tokens, width = query_rows.shape
     heads = head_scale.shape[0]
@@ -322,9 +308,8 @@
     upright = shape((pairs, tokens, PAIR * BLK), bf16)
     turned_f32 = shape((pairs, PAIR * BLK, tokens), f32)
     twofold = shape((pairs, PAIR, tokens, 2 * BLK), bf16)
-    pair_mats = shape((pairs, PAIR, BLK, BLK), f32)
     scores = shape((PAIR, tokens // CHUNK, 2 * CHUNK, CHUNK), bf16)
-    moment_mats = shape((pairs, PAIR, PACKED + BLK, BLK), f32)
+    moment_mats = shape((pairs, PAIR, THREE, BLK), f32)
     anywhere = pl.BlockSpec(memory_space=pl.ANY)
     in_vmem = pl.BlockSpec(memory_space=pltpu.VMEM)
     in_smem = pl.BlockSpec(memory_space=pltpu.SMEM)
@@ -335,50 +320,34 @@
     def sems(*counts):
         return [pltpu.SemaphoreType.DMA((n, pairs)) for n in counts]
 
-    moments = pl.pallas_call(
-        moments_kernel,
-        in_specs=[anywhere] * 3,
-        out_specs=anywhere,
-        out_shape=moment_mats,
-        scratch_shapes=vmem(upright, upright, upright, moment_mats) + sems(3, 1),
-        compiler_params=params(LARGE),
-        name="moments",
-    )(query_rows, key_rows, value_rows)
-    moments_in = swap(moments.reshape(heads, PACKED + BLK, BLK))
-
-    r_local, d_local = pl.pallas_call(
+    r_local, moments = pl.pallas_call(
         first_stage_kernel,
         in_specs=[anywhere] * 3,
         out_specs=[anywhere] * 2,
-        out_shape=[twofold, pair_mats],
-        scratch_shapes=vmem(upright, upright, upright, twofold, pair_mats, scores) + sems(3, 2),
+        out_shape=[twofold, moment_mats],
+        scratch_shapes=vmem(upright, upright, upright, twofold, moment_mats, scores) + sems(3, 2),
         compiler_params=params(LARGE),
-        cost_estimate=cost(10, 10 * tokens * width),
         name="first_stage",
     )(query_rows, key_rows, value_rows)
-    d_in = swap(d_local.reshape(heads, BLK, BLK))
-
-    s_part, c_part, f_part = pl.pallas_call(
-        owner_local_kernel,
-        out_shape=[mats(members + 1)] * 3,
+    moments_in = swap(moments.reshape(heads, THREE, BLK))
+
+    one = shape((TWO, BLK), f32)
+    s_part, c_part, d_base, total = pl.pallas_call(
+        owner_kernel,
+        out_shape=[shape((members, PACKED, BLK), f32), mats(members + 1), mats(members), one],
         compiler_params=params(),
-        name="owner_local",
+        name="owner",
     )(moments_in)
-    d_base, total = pl.pallas_call(
-        owner_sum_kernel,
-        out_shape=[mats(members), shape((2 * BLK, BLK), f32)],
-        compiler_params=params(),
-        name="owner_sum",
-    )(d_in, s_part, f_part)
-    before = jnp.zeros_like(total)
+    before, passed = jnp.zeros_like(total), total
     for turn in range(groups - 1):
         if turn > 0:
-            crossed = jnp.dot(c_part[members], before[:BLK], precision=lax.Precision.HIGHEST)
-            before = before + jnp.concatenate([jnp.zeros_like(crossed), crossed])
-        before = lax.ppermute(before + total, "seq", onward)
+            passed = pl.pallas_call(
+                owner_onward_kernel, out_shape=one, compiler_params=params(), name="owner_onward"
+            )(c_part, total, before)
+        before = lax.ppermute(passed, "seq", onward)
     back = pl.pallas_call(
         owner_back_kernel,
-        out_shape=shape((members, PACKED + BLK, BLK), f32),
+        out_shape=shape((members, TWO, BLK), f32),
         compiler_params=params(),
         name="owner_back",
     )(s_part, c_part, d_base, before)

time: 74.1 us -> 67.6 us (0.912)
  blocking collectives: 18.1 us -> 38.2 us
  waiting for transfers between devices: 16.4 us -> 3.42 us
  starting transfers between devices: 14.3 us -> 4.58 us
  Pallas kernels: 24.9 us -> 21.1 us
    all_to_all x1 -> x2, blocking collectives: 18.1 us -> 38.2 us  [swap(): return lax.all_to_all(a, 'seq', 0, 0, axis_index_groups=index_groups)]
    all_to_all x2 -> x0, waiting for transfers between devices: 12.7 us -> none  [swap(): return lax.all_to_all(a, 'seq', 0, 0, axis_index_groups=index_groups)]
    all_to_all x2 -> x0, starting transfers between devices: 9.69 us -> none  [swap(): return lax.all_to_all(a, 'seq', 0, 0, axis_index_groups=index_groups)]
    pallas_call x4 -> x2, Pallas kernels: 5.28 us -> 1.12 us  [the longest x1 0.64 us: per_device(): pl.pallas_call(owner_kernel, out_shape=[shape((members, PACKED, BLK), f32...]
  transfers between devices with their start and end apart: 4 -> 2, of which waited for: 4 -> 2; matrix products, arithmetic and copies ran while one was open for 0% -> 0% of each run, Pallas kernels for 11% -> 0%
where the time goes in v8:
time: 67.6 us; the launch traced here: 67.3 us
  blocking collectives  38.2 us (57%)
  Pallas kernels  21.1 us (31%)
  starting transfers between devices  4.58 us (7%)
  waiting for transfers between devices  3.42 us (5%)
    all_to_all x2, blocking collectives, swap(): return lax.all_to_all(a, 'seq', 0, 0, axis_index_groups=index_groups)  38.2 us
    pallas_call x1, Pallas kernels, per_device(): pl.pallas_call(second_stage_kernel, in_specs=[anywhere] * 3 + [in_vmem, i...  8.9 us
    pallas_call x1, Pallas kernels, per_device(): pl.pallas_call(first_stage_kernel, in_specs=[anywhere] * 3, out_specs=[an...  7.82 us
    ppermute x1, starting transfers between devices, per_device(): before = lax.ppermute(passed, 'seq', onward)  4.51 us
    pallas_call x1, Pallas kernels, per_device(): pl.pallas_call(functools.partial(norm_kernel, width * shards), in_specs=[...  3.26 us
    ppermute x1, waiting for transfers between devices, per_device(): before = lax.ppermute(passed, 'seq', onward)  2.23 us
  transfers between devices with their start and end apart: 2, of which 2 were waited for; matrix products, arithmetic and copies ran while one was open for 0% of the time, Pallas kernels for 0%

profile of v8, /device:TPU:0, one launch (start us, length us, event | category | flops | bytes accessed | tf_op | source)
XLA Modules:
  0.0 67.3 jit_solution(2757261603327713058)
XLA Ops:
  0.0 7.8 %first_stage.1 = (bf16[4,2,1024,256]{3,2,1,0:T(8,128)(2,1)}, f32[4,2,328,128]{3,2,1,0:T(8,128)}) custom-call(bf16[1024,1024]{1,0:T(8,128)(2,1)} %q_hbm.3, bf16[1024,1024]{1,0:T(8,128)(2,1)} %k_hbm.1, bf16[1024,1024]{1,0:T(8,128)(2,1)} %v_hbm.3), custom_call_target="tpu_custom_call" | custom-call | tf_op jit(solution)/shard_map/first_stage/pallas_call | solution.py:323
  7.8 24.7 %all_to_all.10.moments_ref = f32[8,328,128]{2,1,0:T(8,128)S(1)} all-to-all(f32[8,328,128]{2,1,0:T(8,128)} %bitcast.3), channel_id=1, replica_groups={{0,2,4,6,8,10,12,14},{16,18,20,22,24,26,28,30},{1,3,5,7,9,11,13,15},{17..., dimensions={0} | all-to-all | bytes 2686976 | tf_op jit(solution)/shard_map/all_to_all | solution.py:303
  32.5 0.6 owner.1
  33.2 0.0 copy-start
  33.2 0.0 copy-start.1
  33.2 4.5 %collective-permute-start = (f32[200,128]{1,0:T(8,128)S(1)}, f32[200,128]{1,0:T(8,128)S(1)}, u32[]{:S(2)}, u32[]{:S(2)}) collective-permute-start(f32[200,128]{1,0:T(8,128)S(1)} %get-tuple-element.18), channel_id=1, source_target_pairs={{0,16},{2,18},{4,20},{6,22},{8,24},{10,26},{12,28},{14,30},{1,17},... | collective-permute-start | bytes 307208 | tf_op jit(solution)/shard_map/ppermute | solution.py:347
  37.7 2.2 %collective-permute-done.before_ref = f32[200,128]{1,0:T(8,128)S(1)} collective-permute-done((f32[200,128]{1,0:T(8,128)S(1)}, f32[200,128]{1,0:T(8,128)S(1)}, u32[]{:S(2)}, u32[]{:S(2)}) %collective-permute-start) | collective-permute-done | bytes 102432 | tf_op jit(solution)/shard_map/ppermute | solution.py:347
  39.9 0.5 owner_back.1
  40.4 13.5 %all_to_all.11.back_ref = f32[8,200,128]{2,1,0:T(8,128)S(1)} all-to-all(f32[8,200,128]{2,1,0:T(8,128)S(1)} %owner_back.1), channel_id=1, replica_groups={{0,2,4,6,8,10,12,14},{16,18,20,22,24,26,28,30},{1,3,5,7,9,11,13,15},{17..., dimensions={0} | all-to-all | bytes 1638400 | tf_op jit(solution)/shard_map/all_to_all | solution.py:303
  53.9 0.0 copy-done
  53.9 0.0 copy-done.1
  53.9 8.9 %second_stage.1 = (f32[4,256,1024]{2,1,0:T(8,128)}, f32[8,1024]{1,0:T(8,128)S(1)}) custom-call(bf16[1024,1024]{1,0:T(8,128)(2,1)} %q_hbm.3, bf16[1024,1024]{1,0:T(8,128)(2,1)} %v_hbm.3, bf16[4,2,1024,256]{3,2,1,0:T(8,128)(2,1)} %get-tuple-element.13.r_hbm, f32[8,200,128]{2,1,0:T(8,128)S(1)} %all_to_all.11.back_ref, f32[8,1,128]{2,1,0:T(1,128)S(1)} %bitcast.2, ...), custom_call_target="tpu_custom_call" | custom-call | tf_op jit(solution)/shard_map/second_stage/pallas_call | solution.py:357
  62.8 0.1 collective-permute-start.1
  62.9 1.2 %collective-permute-done.1.other_ref = f32[8,1024]{1,0:T(8,128)S(1)} collective-permute-done((f32[8,1024]{1,0:T(8,128)S(1)}, f32[8,1024]{1,0:T(8,128)S(1)}, u32[]{:S(2)}, u32[]{:S(2)}) %collective-permute-start.1) | collective-permute-done | bytes 32800 | tf_op jit(solution)/shard_map/ppermute | solution.py:369
  64.1 3.3 %norm.1 = bf16[1024,1024]{1,0:T(8,128)(2,1)} custom-call(f32[4,256,1024]{2,1,0:T(8,128)} %get-tuple-element.19.y_hbm, f32[8,1024]{1,0:T(8,128)S(1)} %get-tuple-element.20.mine_ref, f32[8,1024]{1,0:T(8,128)S(1)} %collective-permute-done.1.other_ref), custom_call_target="tpu_custom_call" | custom-call | tf_op jit(solution)/shard_map/norm/pallas_call | solution.py:370
Async XLA Ops:
  33.2 20.7 %copy-start = (f32[1024]{0:T(1024)S(1)}, f32[1024]{0:T(1024)}, u32[]{:S(2)}) copy-start(f32[1024]{0:T(1024)} %param.9) | copy-start | bytes 12292
  33.2 20.7 %copy-start.1 = (f32[8]{0:T(128)S(1)}, f32[8]{0:T(128)}, u32[]{:S(2)}) copy-start(f32[8]{0:T(128)} %scale_ref.1) | copy-start | bytes 100
  33.2 6.7 %collective-permute-start = (f32[200,128]{1,0:T(8,128)S(1)}, f32[200,128]{1,0:T(8,128)S(1)}, u32[]{:S(2)}, u32[]{:S(2)}) collective-permute-start(f32[200,128]{1,0:T(8,128)S(1)} %get-tuple-element.18), channel_id=1, source_target_pairs={{0,16},{2,18},{4,20},{6,22},{8,24},{10,26},{12,28},{14,30},{1,17},... | collective-permute-start | bytes 307208 | tf_op jit(solution)/shard_map/ppermute | solution.py:347
  62.8 1.3 %collective-permute-start.1 = (f32[8,1024]{1,0:T(8,128)S(1)}, f32[8,1024]{1,0:T(8,128)S(1)}, u32[]{:S(2)}, u32[]{:S(2)}) collective-permute-start(f32[8,1024]{1,0:T(8,128)S(1)} %get-tuple-element.20.mine_ref), channel_id=1, source_target_pairs={{0,1},{1,0},{2,3},{3,2},{4,5},{5,4},{6,7},{7,6},{8,9},{9,8},{10,11... | collective-permute-start | bytes 98312 | tf_op jit(solution)/shard_map/ppermute | solution.py:369

commit v9 on v8

--- a/solution.py
+++ b/solution.py
@@ -16,8 +16,8 @@
 THREE = TWO + BLK
 SMALL = 8 * 1024 * 1024
 LARGE = 60 * 1024 * 1024
-LATE = 52 * 1024 * 1024
-LAST = 52 * 1024 * 1024
+LATE = 24 * 1024 * 1024
+LAST = 12 * 1024 * 1024
 
 epsilon = 1e-06
 f32, bf16 = jnp.float32, jnp.bfloat16
@@ -168,62 +168,44 @@
         wait(writes, write_sems, p)
 
 
-def second_stage(p, q_ref, v_ref, r_ref, s_both, a_ref, first, store):
-    tokens = q_ref.shape[1]
+def second_stage_kernel(
+    q_ref, v_ref, r_ref, back_ref, gain_ref, scale_ref, y_ref, part_ref, rr_ref, gains_ref, a_ref
+):
+    pairs, _, tokens, _ = r_ref.shape
+    units = chunk_units(tokens)
     steps = tokens // CHUNK
-    units = chunk_units(tokens)
     mask = ordered(CHUNK) <= 0
-    for j in range(PAIR):
-        for i in range(steps):
-            at = span(i, CHUNK)
-            q = q_ref[p, at, span(j)]
-            r = halves_sum(r_ref[p, j, at].astype(f32)) + dot(lanes(q, q), s_both[j])
-            r_ref[p, j, at] = lanes(*split(r))
-    for i, j, at, cols in units:
-        qt = q_ref[p, at, cols].T
-        a = dot(r_ref[p, j, at], rows(qt, qt))
-        a_ref[j, i] = rows(*split(jnp.where(mask, a, 0.0)))
-    sums = [[] for _ in range(PAIR)]
-    for i, j, at, cols in units:
-        if i + 1 < steps:
-            sums[j].append(halves_sum(dot(v_ref[p, at, cols].T, r_ref[p, j, at])))
-    states = [running(sums[j], first[j]) for j in range(PAIR)]
-    for i, j, at, cols in units:
-        vt = v_ref[p, at, cols].T
-        qt = q_ref[p, at, cols].T
-        num = dot(lanes(vt, vt), a_ref[j, i]) + dot(lanes(*split(states[j][i])), rows(qt, qt))
-        store(i, j, num)
-
-
-def second_stage_kernel(
-    q_hbm, v_hbm, r_hbm, back_ref, gain_ref, scale_ref, y_hbm, part_ref,
-    q_ref, v_ref, r_ref, y_ref, gains_ref, a_ref, read_sems, write_sems
-):
-    pairs = q_ref.shape[0]
-    reads = [(by_columns(q_hbm), by_pair(q_ref)), (by_pair(r_hbm), by_pair(r_ref)), (by_columns(v_hbm), by_pair(v_ref))]
-    writes = [(by_pair(y_ref), by_pair(y_hbm))]
-    start(reads, read_sems, 0, pairs)
     part_ref[...] = jnp.zeros_like(part_ref)
     for h in range(pairs * PAIR):
         gains_ref[h] = jnp.broadcast_to(gain_ref[h], (BLK, BLK)).T
 
     @pl.loop(0, pairs)
     def _(p):
-        def finish(i, j, num):
-            h = p * PAIR + j
-            y = num * scale_ref[h]
-            part_ref[:, span(i, CHUNK)] += jnp.sum((y * y).reshape(BLK // 8, 8, CHUNK), axis=0)
-            y_ref[p, span(j), span(i, CHUNK)] = y * lanes(*[gains_ref[h]] * (CHUNK // BLK))
-
         backs = [back_ref[p * PAIR + j] for j in range(PAIR)]
         s_both = [rows(*split(unpack(back[:PACKED]))) for back in backs]
-        wait(reads, read_sems, p)
-        second_stage(p, q_ref, v_ref, r_ref, s_both, a_ref, [back[PACKED:] for back in backs], finish)
-        for copy in copies(writes, write_sems, p):
-            copy.start()
-
-    for p in range(pairs):
-        wait(writes, write_sems, p)
+        heads = [pl.ds(pl.multiple_of((p * PAIR + j) * BLK, BLK), BLK) for j in range(PAIR)]
+        for j in range(PAIR):
+            for i in range(steps):
+                at = span(i, CHUNK)
+                q = q_ref[at, heads[j]]
+                r = halves_sum(r_ref[p, j, at].astype(f32)) + dot(lanes(q, q), s_both[j])
+                rr_ref[j, at] = lanes(*split(r))
+        for i, j, at, cols in units:
+            qt = q_ref[at, heads[j]].T
+            a = dot(rr_ref[j, at], rows(qt, qt))
+            a_ref[j, i] = rows(*split(jnp.where(mask, a, 0.0)))
+        sums = [[] for _ in range(PAIR)]
+        for i, j, at, cols in units:
+            if i + 1 < steps:
+                sums[j].append(halves_sum(dot(v_ref[at, heads[j]].T, rr_ref[j, at])))
+        states = [running(sums[j], backs[j][PACKED:]) for j in range(PAIR)]
+        for i, j, at, cols in units:
+            h = p * PAIR + j
+            vt, qt = v_ref[at, heads[j]].T, q_ref[at, heads[j]].T
+            num = dot(lanes(vt, vt), a_ref[j, i]) + dot(lanes(*split(states[j][i])), rows(qt, qt))
+            y = num * scale_ref[h]
+            part_ref[:, at] += jnp.sum((y * y).reshape(BLK // 8, 8, CHUNK), axis=0)
+            y_ref[p, cols, at] = y * lanes(*[gains_ref[h]] * (CHUNK // BLK))
 
 
 def owner_kernel(moments_ref, s_ref, c_ref, base_ref, total_ref):
@@ -260,30 +242,19 @@
         back_ref[m, PACKED:] = d if m == 0 else d + dot_f32(c_ref[m], s_before)
 
 
-def norm_kernel(features, y_hbm, mine_ref, other_ref, out_hbm, y_ref, out_ref, read_sems, write_sems):
+def norm_kernel(features, y_ref, mine_ref, other_ref, out_hbm, out_ref, sems):
     pairs, wide, tokens = y_ref.shape
-    steps = tokens // CHUNK
-
-    def y_copy(i):
-        at = span(i, CHUNK)
-        return pltpu.make_async_copy(y_hbm.at[:, :, at], y_ref.at[:, :, at], read_sems.at[i])
-
-    def out_copy(i):
-        at = span(i, CHUNK)
-        return pltpu.make_async_copy(out_ref.at[at], out_hbm.at[at], write_sems.at[i])
-
-    for i in range(steps):
-        y_copy(i).start()
     total = jnp.sum(mine_ref[...] + other_ref[...], axis=0, keepdims=True)
     inv = lax.rsqrt(total * (1.0 / features) + epsilon)
-    for i in range(steps):
+    moves = []
+    for i in range(tokens // CHUNK):
         at = span(i, CHUNK)
-        y_copy(i).wait()
         for p in range(pairs):
             out_ref[at, span(p, wide)] = (y_ref[p, :, at] * inv[:, at]).astype(bf16).T
-        out_copy(i).start()
-    for i in range(steps):
-        out_copy(i).wait()
+        moves.append(pltpu.make_async_copy(out_ref.at[at], out_hbm.at[at], sems.at[i]))
+        moves[-1].start()
+    for copy in moves:
+        copy.wait()
 
 
 def params(limit=SMALL):
@@ -356,10 +327,9 @@
     part_shape = shape((8, tokens), f32)
     y, part = pl.pallas_call(
         second_stage_kernel,
-        in_specs=[anywhere] * 3 + [in_vmem, in_vmem, in_smem],
-        out_specs=[anywhere, in_vmem],
+        in_specs=[in_vmem] * 5 + [in_smem],
         out_shape=[turned_f32, part_shape],
-        scratch_shapes=vmem(upright, upright, twofold, turned_f32, mats(heads), scores) + sems(3, 1),
+        scratch_shapes=vmem(shape(twofold.shape[1:], bf16), mats(heads), scores),
         compiler_params=params(LATE),
         name="second_stage",
     )(query_rows, value_rows, r_local, back_in, out_gain.reshape(heads, 1, BLK), head_scale)
@@ -369,11 +339,10 @@
         other = other + lax.ppermute(part, "head", [(i, (i + turn) % shards) for i in range(shards)])
     return pl.pallas_call(
         functools.partial(norm_kernel, width * shards),
-        in_specs=[anywhere, in_vmem, in_vmem],
+        in_specs=[in_vmem] * 3,
         out_specs=anywhere,
         out_shape=shape((tokens, width), bf16),
-        scratch_shapes=vmem(turned_f32, shape((tokens, width), bf16))
-        + [pltpu.SemaphoreType.DMA((tokens // CHUNK,))] * 2,
+        scratch_shapes=vmem(shape((tokens, width), bf16)) + [pltpu.SemaphoreType.DMA((tokens // CHUNK,))],
         compiler_params=params(LAST),
         name="norm",
     )(y, part, other)

time: 67.6 us -> 67.1 us (level)
  Pallas kernels: 21.1 us -> 18.3 us
  local copies, waits for them, and re-layouts: 0.01 us -> 2.2 us
    unnamed x4 -> x10, local copies, waits for them, and re-layouts: 0.01 us -> 2.2 us
    pallas_call x1, Pallas kernels: 3.26 us -> 1.56 us  [per_device(): pl.pallas_call(functools.partial(norm_kernel, width * shards), in_specs=[...]
    pallas_call x1, Pallas kernels: 8.9 us -> 7.78 us  [per_device(): pl.pallas_call(second_stage_kernel, in_specs=[in_vmem] * 5 + [in_smem], o...]
where the time goes in v9:
time: 67.1 us; the launch traced here: 66.9 us
  blocking collectives  38.2 us (57%)
  Pallas kernels  18.3 us (27%)
  starting transfers between devices  4.71 us (7%)
  waiting for transfers between devices  3.42 us (5%)
  local copies, waits for them, and re-layouts  2.2 us (3%)
    all_to_all x2, blocking collectives, swap(): return lax.all_to_all(a, 'seq', 0, 0, axis_index_groups=index_groups)  38.2 us
    pallas_call x1, Pallas kernels, per_device(): pl.pallas_call(first_stage_kernel, in_specs=[anywhere] * 3, out_specs=[an...  7.83 us
    pallas_call x1, Pallas kernels, per_device(): pl.pallas_call(second_stage_kernel, in_specs=[in_vmem] * 5 + [in_smem], o...  7.78 us
    ppermute x1, starting transfers between devices, per_device(): before = lax.ppermute(passed, 'seq', onward)  4.64 us
    ppermute x1, waiting for transfers between devices, per_device(): before = lax.ppermute(passed, 'seq', onward)  2.23 us
    unnamed x10, local copies, waits for them, and re-layouts  2.2 us
    pallas_call x1, Pallas kernels, per_device(): pl.pallas_call(functools.partial(norm_kernel, width * shards), in_specs=[...  1.56 us
  transfers between devices with their start and end apart: 2, of which 2 were waited for; matrix products, arithmetic and copies ran while one was open for 0% of the time, Pallas kernels for 0%

profile of v9, /device:TPU:0, one launch (start us, length us, event | category | flops | bytes accessed | tf_op | source)
XLA Modules:
  0.0 66.9 jit_solution(4053321291961326023)
XLA Ops:
  0.0 7.8 %first_stage.1 = (bf16[4,2,1024,256]{3,2,1,0:T(8,128)(2,1)}, f32[4,2,328,128]{3,2,1,0:T(8,128)}) custom-call(bf16[1024,1024]{1,0:T(8,128)(2,1)} %q_ref.1, bf16[1024,1024]{1,0:T(8,128)(2,1)} %k_hbm.1, bf16[1024,1024]{1,0:T(8,128)(2,1)} %v_ref.1), custom_call_target="tpu_custom_call" | custom-call | tf_op jit(solution)/shard_map/first_stage/pallas_call | solution.py:294
  7.8 24.7 %all_to_all.10.moments_ref = f32[8,328,128]{2,1,0:T(8,128)S(1)} all-to-all(f32[8,328,128]{2,1,0:T(8,128)} %bitcast.3), channel_id=1, replica_groups={{0,2,4,6,8,10,12,14},{16,18,20,22,24,26,28,30},{1,3,5,7,9,11,13,15},{17..., dimensions={0} | all-to-all | bytes 2686976 | tf_op jit(solution)/shard_map/all_to_all | solution.py:274
  32.5 0.0 copy-start.1
  32.5 0.6 owner.1
  33.2 0.0 copy-start
  33.2 0.0 copy-start.3
  33.2 0.0 copy-start.4
  33.2 4.6 %collective-permute-start = (f32[200,128]{1,0:T(8,128)S(1)}, f32[200,128]{1,0:T(8,128)S(1)}, u32[]{:S(2)}, u32[]{:S(2)}) collective-permute-start(f32[200,128]{1,0:T(8,128)S(1)} %get-tuple-element.18), channel_id=1, source_target_pairs={{0,16},{2,18},{4,20},{6,22},{8,24},{10,26},{12,28},{14,30},{1,17},... | collective-permute-start | bytes 307208 | tf_op jit(solution)/shard_map/ppermute | solution.py:318
  37.9 2.2 %collective-permute-done.before_ref = f32[200,128]{1,0:T(8,128)S(1)} collective-permute-done((f32[200,128]{1,0:T(8,128)S(1)}, f32[200,128]{1,0:T(8,128)S(1)}, u32[]{:S(2)}, u32[]{:S(2)}) %collective-permute-start) | collective-permute-done | bytes 102432 | tf_op jit(solution)/shard_map/ppermute | solution.py:318
  40.1 0.5 owner_back.1
  40.6 13.5 %all_to_all.11.back_ref = f32[8,200,128]{2,1,0:T(8,128)S(1)} all-to-all(f32[8,200,128]{2,1,0:T(8,128)S(1)} %owner_back.1), channel_id=1, replica_groups={{0,2,4,6,8,10,12,14},{16,18,20,22,24,26,28,30},{1,3,5,7,9,11,13,15},{17..., dimensions={0} | all-to-all | bytes 1638400 | tf_op jit(solution)/shard_map/all_to_all | solution.py:274
  54.0 0.0 copy-done.1
  54.0 0.0 copy-done
  54.0 0.0 copy-done.3
  54.0 0.0 copy-done.4
  54.1 0.0 copy-start.2
  54.1 2.2 %copy-done.2 = bf16[4,2,1024,256]{3,2,1,0:T(8,128)(2,1)S(1)} copy-done((bf16[4,2,1024,256]{3,2,1,0:T(8,128)(2,1)S(1)}, bf16[4,2,1024,256]{3,2,1,0:T(8,128)(2,1)}, u32[]{:S(2)}) %copy-start.2) | copy-done | bytes 4194328
  56.2 7.8 %second_stage.1 = (f32[4,256,1024]{2,1,0:T(8,128)S(1)}, f32[8,1024]{1,0:T(8,128)S(1)}) custom-call(bf16[1024,1024]{1,0:T(8,128)(2,1)S(1)} %copy-done, bf16[1024,1024]{1,0:T(8,128)(2,1)S(1)} %copy-done.1, bf16[4,2,1024,256]{3,2,1,0:T(8,128)(2,1)S(1)} %copy-done.2, f32[8,200,128]{2,1,0:T(8,128)S(1)} %all_to_all.11.back_ref, f32[8,1,128]{2,1,0:T(1,128)S(1)} %bitcast.2, ...), custom_call_target="tpu_custom_call" | custom-call | tf_op jit(solution)/shard_map/second_stage/pallas_call | solution.py:328
  64.0 0.1 collective-permute-start.1
  64.1 1.2 %collective-permute-done.1.other_ref = f32[8,1024]{1,0:T(8,128)S(1)} collective-permute-done((f32[8,1024]{1,0:T(8,128)S(1)}, f32[8,1024]{1,0:T(8,128)S(1)}, u32[]{:S(2)}, u32[]{:S(2)}) %collective-permute-start.1) | collective-permute-done | bytes 32800 | tf_op jit(solution)/shard_map/ppermute | solution.py:339
  65.3 1.6 %norm.1 = bf16[1024,1024]{1,0:T(8,128)(2,1)} custom-call(f32[4,256,1024]{2,1,0:T(8,128)S(1)} %get-tuple-element.19.y_ref, f32[8,1024]{1,0:T(8,128)S(1)} %get-tuple-element.20.mine_ref, f32[8,1024]{1,0:T(8,128)S(1)} %collective-permute-done.1.other_ref), custom_call_target="tpu_custom_call" | custom-call | tf_op jit(solution)/shard_map/norm/pallas_call | solution.py:340
Async XLA Ops:
  32.5 21.5 %copy-start.1 = (bf16[1024,1024]{1,0:T(8,128)(2,1)S(1)}, bf16[1024,1024]{1,0:T(8,128)(2,1)}, u32[]{:S(2)}) copy-start(bf16[1024,1024]{1,0:T(8,128)(2,1)} %v_ref.1) | copy-start | bytes 6291460
  33.2 20.9 %copy-start = (bf16[1024,1024]{1,0:T(8,128)(2,1)S(1)}, bf16[1024,1024]{1,0:T(8,128)(2,1)}, u32[]{:S(2)}) copy-start(bf16[1024,1024]{1,0:T(8,128)(2,1)} %q_ref.1) | copy-start | bytes 6291460
  33.2 20.9 %copy-start.3 = (f32[1024]{0:T(1024)S(1)}, f32[1024]{0:T(1024)}, u32[]{:S(2)}) copy-start(f32[1024]{0:T(1024)} %param.9) | copy-start | bytes 12292
  33.2 20.8 %copy-start.4 = (f32[8]{0:T(128)S(1)}, f32[8]{0:T(128)}, u32[]{:S(2)}) copy-start(f32[8]{0:T(128)} %scale_ref.1) | copy-start | bytes 100
  33.2 6.9 %collective-permute-start = (f32[200,128]{1,0:T(8,128)S(1)}, f32[200,128]{1,0:T(8,128)S(1)}, u32[]{:S(2)}, u32[]{:S(2)}) collective-permute-start(f32[200,128]{1,0:T(8,128)S(1)} %get-tuple-element.18), channel_id=1, source_target_pairs={{0,16},{2,18},{4,20},{6,22},{8,24},{10,26},{12,28},{14,30},{1,17},... | collective-permute-start | bytes 307208 | tf_op jit(solution)/shard_map/ppermute | solution.py:318
  54.1 2.2 %copy-start.2 = (bf16[4,2,1024,256]{3,2,1,0:T(8,128)(2,1)S(1)}, bf16[4,2,1024,256]{3,2,1,0:T(8,128)(2,1)}, u32[]{:S(2)}) copy-start(bf16[4,2,1024,256]{3,2,1,0:T(8,128)(2,1)} %get-tuple-element.13.r_ref) | copy-start | bytes 12582916
  64.0 1.3 %collective-permute-start.1 = (f32[8,1024]{1,0:T(8,128)S(1)}, f32[8,1024]{1,0:T(8,128)S(1)}, u32[]{:S(2)}, u32[]{:S(2)}) collective-permute-start(f32[8,1024]{1,0:T(8,128)S(1)} %get-tuple-element.20.mine_ref), channel_id=1, source_target_pairs={{0,1},{1,0},{2,3},{3,2},{4,5},{5,4},{6,7},{7,6},{8,9},{9,8},{10,11... | collective-permute-start | bytes 98312 | tf_op jit(solution)/shard_map/ppermute | solution.py:339

commit v10 on v9

--- a/solution.py
+++ b/solution.py
@@ -16,7 +16,7 @@
 THREE = TWO + BLK
 SMALL = 8 * 1024 * 1024
 LARGE = 60 * 1024 * 1024
-LATE = 24 * 1024 * 1024
+LATE = 42 * 1024 * 1024
 LAST = 12 * 1024 * 1024
 
 epsilon = 1e-06
@@ -128,15 +128,18 @@
 
 
 def first_stage_kernel(
-    q_hbm, k_hbm, v_hbm, r_hbm, m_hbm, q_ref, k_ref, v_ref, r_ref, m_ref, a_ref, read_sems, write_sems
+    q_hbm, k_hbm, v_hbm, r_hbm, m_hbm, q_ref, k_ref, v_ref, r_ref, m_ref, a_ref, read_sems, v_sems, r_sems, m_sems
 ):
     pairs, tokens, _ = q_ref.shape
     steps = tokens // CHUNK
     units = chunk_units(tokens)
     mask = ordered(CHUNK) <= 0
-    reads = [(by_columns(a), by_pair(b)) for a, b in ((q_hbm, q_ref), (k_hbm, k_ref), (v_hbm, v_ref))]
-    writes = [(by_pair(m_ref), by_pair(m_hbm)), (by_pair(r_ref), by_pair(r_hbm))]
-    start(reads, read_sems, 0, pairs)
+    reads = [(by_columns(a), by_pair(b)) for a, b in ((q_hbm, q_ref), (k_hbm, k_ref))]
+    v_reads = [(by_columns(v_hbm), by_pair(v_ref))]
+    r_writes, m_writes = [(by_pair(r_ref), by_pair(r_hbm))], [(by_pair(m_ref), by_pair(m_hbm))]
+    for p in range(pairs):
+        start(reads, read_sems, p, p + 1)
+        start(v_reads, v_sems, p, p + 1)
 
     @pl.loop(0, pairs)
     def _(p):
@@ -157,24 +160,30 @@
                 r = r + dot(lanes(*split(states[j][i])), rows(qt, qt))
             r_high, r_low = split(r)
             r_ref[p, j, at] = lanes(r_high.T, r_low.T)
+        for copy in copies(r_writes, r_sems, p):
+            copy.start()
+        wait(v_reads, v_sems, p)
         for j in range(PAIR):
             vt = v_ref[p, :, span(j)].T
             m_ref[p, j, PACKED:TWO] = dot(vt, q_ref[p, :, span(j)])
             m_ref[p, j, TWO:] = halves_sum(dot(vt, r_ref[p, j]))
-        for copy in copies(writes, write_sems, p):
+        for copy in copies(m_writes, m_sems, p):
             copy.start()
 
     for p in range(pairs):
-        wait(writes, write_sems, p)
+        wait(r_writes, r_sems, p)
+        wait(m_writes, m_sems, p)
 
 
 def second_stage_kernel(
-    q_ref, v_ref, r_ref, back_ref, gain_ref, scale_ref, y_ref, part_ref, rr_ref, gains_ref, a_ref
+    q_ref, v_ref, r_hbm, back_ref, gain_ref, scale_ref, y_ref, part_ref, r_ref, rr_ref, gains_ref, a_ref, read_sems
 ):
     pairs, _, tokens, _ = r_ref.shape
     units = chunk_units(tokens)
     steps = tokens // CHUNK
     mask = ordered(CHUNK) <= 0
+    reads = [(by_pair(r_hbm), by_pair(r_ref))]
+    start(reads, read_sems, 0, pairs)
     part_ref[...] = jnp.zeros_like(part_ref)
     for h in range(pairs * PAIR):
         gains_ref[h] = jnp.broadcast_to(gain_ref[h], (BLK, BLK)).T
@@ -184,6 +193,7 @@
         backs = [back_ref[p * PAIR + j] for j in range(PAIR)]
         s_both = [rows(*split(unpack(back[:PACKED]))) for back in backs]
         heads = [pl.ds(pl.multiple_of((p * PAIR + j) * BLK, BLK), BLK) for j in range(PAIR)]
+        wait(reads, read_sems, p)
         for j in range(PAIR):
             for i in range(steps):
                 at = span(i, CHUNK)
@@ -296,7 +306,7 @@
         in_specs=[anywhere] * 3,
         out_specs=[anywhere] * 2,
         out_shape=[twofold, moment_mats],
-        scratch_shapes=vmem(upright, upright, upright, twofold, moment_mats, scores) + sems(3, 2),
+        scratch_shapes=vmem(upright, upright, upright, twofold, moment_mats, scores) + sems(2, 1, 1, 1),
         compiler_params=params(LARGE),
         name="first_stage",
     )(query_rows, key_rows, value_rows)
@@ -327,9 +337,9 @@
     part_shape = shape((8, tokens), f32)
     y, part = pl.pallas_call(
         second_stage_kernel,
-        in_specs=[in_vmem] * 5 + [in_smem],
+        in_specs=[in_vmem, in_vmem, anywhere, in_vmem, in_vmem, in_smem],
         out_shape=[turned_f32, part_shape],
-        scratch_shapes=vmem(shape(twofold.shape[1:], bf16), mats(heads), scores),
+        scratch_shapes=vmem(twofold, shape(twofold.shape[1:], bf16), mats(heads), scores) + sems(1),
         compiler_params=params(LATE),
         name="second_stage",
     )(query_rows, value_rows, r_local, back_in, out_gain.reshape(heads, 1, BLK), head_scale)

time: 67.1 us -> 66.7 us (level)
  local copies, waits for them, and re-layouts: 2.2 us -> 0.02 us
  Pallas kernels: 18.3 us -> 20.1 us
    unnamed x10 -> x8, local copies, waits for them, and re-layouts: 2.2 us -> 0.02 us
    pallas_call x1, Pallas kernels: 7.78 us -> 8.73 us  [per_device(): pl.pallas_call(second_stage_kernel, in_specs=[in_vmem, in_vmem, anywhere,...]
    pallas_call x1, Pallas kernels: 7.83 us -> 8.71 us  [per_device(): pl.pallas_call(first_stage_kernel, in_specs=[anywhere] * 3, out_specs=[an...]
where the time goes in v10:
time: 66.7 us; the launch traced here: 66.5 us
  blocking collectives  38.1 us (57%)
  Pallas kernels  20.1 us (30%)
  starting transfers between devices  4.7 us (7%)
  waiting for transfers between devices  3.42 us (5%)
    all_to_all x2, blocking collectives, swap(): return lax.all_to_all(a, 'seq', 0, 0, axis_index_groups=index_groups)  38.1 us
    pallas_call x1, Pallas kernels, per_device(): pl.pallas_call(second_stage_kernel, in_specs=[in_vmem, in_vmem, anywhere,...  8.73 us
    pallas_call x1, Pallas kernels, per_device(): pl.pallas_call(first_stage_kernel, in_specs=[anywhere] * 3, out_specs=[an...  8.71 us
    ppermute x1, starting transfers between devices, per_device(): before = lax.ppermute(passed, 'seq', onward)  4.63 us
    ppermute x1, waiting for transfers between devices, per_device(): before = lax.ppermute(passed, 'seq', onward)  2.23 us
    pallas_call x1, Pallas kernels, per_device(): pl.pallas_call(functools.partial(norm_kernel, width * shards), in_specs=[...  1.56 us
  transfers between devices with their start and end apart: 2, of which 2 were waited for; matrix products, arithmetic and copies ran while one was open for 0% of the time, Pallas kernels for 0%

profile of v10, /device:TPU:0, one launch (start us, length us, event | category | flops | bytes accessed | tf_op | source)
XLA Modules:
  0.0 66.5 jit_solution(30112378843802625)
XLA Ops:
  0.0 8.7 %first_stage.1 = (bf16[4,2,1024,256]{3,2,1,0:T(8,128)(2,1)}, f32[4,2,328,128]{3,2,1,0:T(8,128)}) custom-call(bf16[1024,1024]{1,0:T(8,128)(2,1)} %q_ref.1, bf16[1024,1024]{1,0:T(8,128)(2,1)} %k_hbm.1, bf16[1024,1024]{1,0:T(8,128)(2,1)} %v_ref.1), custom_call_target="tpu_custom_call" | custom-call | tf_op jit(solution)/shard_map/first_stage/pallas_call | solution.py:304
  8.7 24.7 %all_to_all.10.moments_ref = f32[8,328,128]{2,1,0:T(8,128)S(1)} all-to-all(f32[8,328,128]{2,1,0:T(8,128)} %bitcast.3), channel_id=1, replica_groups={{0,2,4,6,8,10,12,14},{16,18,20,22,24,26,28,30},{1,3,5,7,9,11,13,15},{17..., dimensions={0} | all-to-all | bytes 2686976 | tf_op jit(solution)/shard_map/all_to_all | solution.py:284
  33.4 0.0 copy-start.1
  33.4 0.6 owner.1
  34.1 0.0 copy-start
  34.1 0.0 copy-start.2
  34.1 0.0 copy-start.3
  34.1 4.6 %collective-permute-start = (f32[200,128]{1,0:T(8,128)S(1)}, f32[200,128]{1,0:T(8,128)S(1)}, u32[]{:S(2)}, u32[]{:S(2)}) collective-permute-start(f32[200,128]{1,0:T(8,128)S(1)} %get-tuple-element.18), channel_id=1, source_target_pairs={{0,16},{2,18},{4,20},{6,22},{8,24},{10,26},{12,28},{14,30},{1,17},... | collective-permute-start | bytes 307208 | tf_op jit(solution)/shard_map/ppermute | solution.py:328
  38.7 2.2 %collective-permute-done.before_ref = f32[200,128]{1,0:T(8,128)S(1)} collective-permute-done((f32[200,128]{1,0:T(8,128)S(1)}, f32[200,128]{1,0:T(8,128)S(1)}, u32[]{:S(2)}, u32[]{:S(2)}) %collective-permute-start) | collective-permute-done | bytes 102432 | tf_op jit(solution)/shard_map/ppermute | solution.py:328
  41.0 0.5 owner_back.1
  41.4 13.5 %all_to_all.11.back_ref = f32[8,200,128]{2,1,0:T(8,128)S(1)} all-to-all(f32[8,200,128]{2,1,0:T(8,128)S(1)} %owner_back.1), channel_id=1, replica_groups={{0,2,4,6,8,10,12,14},{16,18,20,22,24,26,28,30},{1,3,5,7,9,11,13,15},{17..., dimensions={0} | all-to-all | bytes 1638400 | tf_op jit(solution)/shard_map/all_to_all | solution.py:284
  54.9 0.0 copy-done.1
  54.9 0.0 copy-done
  54.9 0.0 copy-done.2
  54.9 0.0 copy-done.3
  54.9 8.7 %second_stage.1 = (f32[4,256,1024]{2,1,0:T(8,128)S(1)}, f32[8,1024]{1,0:T(8,128)S(1)}) custom-call(bf16[1024,1024]{1,0:T(8,128)(2,1)S(1)} %copy-done, bf16[1024,1024]{1,0:T(8,128)(2,1)S(1)} %copy-done.1, bf16[4,2,1024,256]{3,2,1,0:T(8,128)(2,1)} %get-tuple-element.13.r_hbm, f32[8,200,128]{2,1,0:T(8,128)S(1)} %all_to_all.11.back_ref, ...), custom_call_target="tpu_custom_call" | custom-call | tf_op jit(solution)/shard_map/second_stage/pallas_call | solution.py:338
  63.7 0.1 collective-permute-start.1
  63.7 1.2 %collective-permute-done.1.other_ref = f32[8,1024]{1,0:T(8,128)S(1)} collective-permute-done((f32[8,1024]{1,0:T(8,128)S(1)}, f32[8,1024]{1,0:T(8,128)S(1)}, u32[]{:S(2)}, u32[]{:S(2)}) %collective-permute-start.1) | collective-permute-done | bytes 32800 | tf_op jit(solution)/shard_map/ppermute | solution.py:349
  64.9 1.6 %norm.1 = bf16[1024,1024]{1,0:T(8,128)(2,1)} custom-call(f32[4,256,1024]{2,1,0:T(8,128)S(1)} %get-tuple-element.19.y_ref, f32[8,1024]{1,0:T(8,128)S(1)} %get-tuple-element.20.mine_ref, f32[8,1024]{1,0:T(8,128)S(1)} %collective-permute-done.1.other_ref), custom_call_target="tpu_custom_call" | custom-call | tf_op jit(solution)/shard_map/norm/pallas_call | solution.py:350
Async XLA Ops:
  33.4 21.5 %copy-start.1 = (bf16[1024,1024]{1,0:T(8,128)(2,1)S(1)}, bf16[1024,1024]{1,0:T(8,128)(2,1)}, u32[]{:S(2)}) copy-start(bf16[1024,1024]{1,0:T(8,128)(2,1)} %v_ref.1) | copy-start | bytes 6291460
  34.1 20.8 %copy-start = (bf16[1024,1024]{1,0:T(8,128)(2,1)S(1)}, bf16[1024,1024]{1,0:T(8,128)(2,1)}, u32[]{:S(2)}) copy-start(bf16[1024,1024]{1,0:T(8,128)(2,1)} %q_ref.1) | copy-start | bytes 6291460
  34.1 20.8 %copy-start.2 = (f32[1024]{0:T(1024)S(1)}, f32[1024]{0:T(1024)}, u32[]{:S(2)}) copy-start(f32[1024]{0:T(1024)} %param.9) | copy-start | bytes 12292
  34.1 20.8 %copy-start.3 = (f32[8]{0:T(128)S(1)}, f32[8]{0:T(128)}, u32[]{:S(2)}) copy-start(f32[8]{0:T(128)} %scale_ref.1) | copy-start | bytes 100
  34.1 6.9 %collective-permute-start = (f32[200,128]{1,0:T(8,128)S(1)}, f32[200,128]{1,0:T(8,128)S(1)}, u32[]{:S(2)}, u32[]{:S(2)}) collective-permute-start(f32[200,128]{1,0:T(8,128)S(1)} %get-tuple-element.18), channel_id=1, source_target_pairs={{0,16},{2,18},{4,20},{6,22},{8,24},{10,26},{12,28},{14,30},{1,17},... | collective-permute-start | bytes 307208 | tf_op jit(solution)/shard_map/ppermute | solution.py:328
  63.7 1.3 %collective-permute-start.1 = (f32[8,1024]{1,0:T(8,128)S(1)}, f32[8,1024]{1,0:T(8,128)S(1)}, u32[]{:S(2)}, u32[]{:S(2)}) collective-permute-start(f32[8,1024]{1,0:T(8,128)S(1)} %get-tuple-element.20.mine_ref), channel_id=1, source_target_pairs={{0,1},{1,0},{2,3},{3,2},{4,5},{5,4},{6,7},{7,6},{8,9},{9,8},{10,11... | collective-permute-start | bytes 98312 | tf_op jit(solution)/shard_map/ppermute | solution.py:349

commit v11 on v9

--- a/solution.py
+++ b/solution.py
@@ -16,6 +16,7 @@
 THREE = TWO + BLK
 SMALL = 8 * 1024 * 1024
 LARGE = 60 * 1024 * 1024
+FETCH = 46 * 1024 * 1024
 LATE = 24 * 1024 * 1024
 LAST = 12 * 1024 * 1024
 
@@ -168,16 +169,24 @@
         wait(writes, write_sems, p)
 
 
+def fetch_kernel(r_hbm, gain_ref, owned_hbm, r_ref, gains_ref, sems):
+    pairs = r_ref.shape[0]
+    reads = [(by_pair(r_hbm), by_pair(r_ref))]
+    start(reads, sems, 0, pairs)
+    for h in range(gains_ref.shape[0]):
+        gains_ref[h] = jnp.broadcast_to(gain_ref[h], (BLK, BLK)).T
+    for p in range(pairs):
+        wait(reads, sems, p)
+
+
 def second_stage_kernel(
-    q_ref, v_ref, r_ref, back_ref, gain_ref, scale_ref, y_ref, part_ref, rr_ref, gains_ref, a_ref
+    q_ref, v_ref, r_ref, back_ref, gains_ref, scale_ref, y_ref, part_ref, rr_ref, a_ref
 ):
     pairs, _, tokens, _ = r_ref.shape
     units = chunk_units(tokens)
     steps = tokens // CHUNK
     mask = ordered(CHUNK) <= 0
     part_ref[...] = jnp.zeros_like(part_ref)
-    for h in range(pairs * PAIR):
-        gains_ref[h] = jnp.broadcast_to(gain_ref[h], (BLK, BLK)).T
 
     @pl.loop(0, pairs)
     def _(p):
@@ -233,7 +242,7 @@
     out_ref[PACKED:] = total_ref[PACKED:] + before_ref[PACKED:] + crossed
 
 
-def owner_back_kernel(s_ref, c_ref, base_ref, before_ref, back_ref):
+def owner_back_kernel(s_ref, c_ref, base_ref, before_ref, held_hbm, back_ref):
     packed, d_before = before_ref[:PACKED], before_ref[PACKED:]
     s_before = unpack(packed)
     for m in range(back_ref.shape[0]):
@@ -309,6 +318,15 @@
         compiler_params=params(),
         name="owner",
     )(moments_in)
+    r_held, gain_columns = pl.pallas_call(
+        fetch_kernel,
+        in_specs=[anywhere, in_vmem, anywhere],
+        out_specs=[in_vmem] * 2,
+        out_shape=[twofold, mats(heads)],
+        scratch_shapes=sems(1),
+        compiler_params=params(FETCH),
+        name="fetch",
+    )(r_local, out_gain.reshape(heads, 1, BLK), total)
     before, passed = jnp.zeros_like(total), total
     for turn in range(groups - 1):
         if turn > 0:
@@ -318,10 +336,11 @@
         before = lax.ppermute(passed, "seq", onward)
     back = pl.pallas_call(
         owner_back_kernel,
+        in_specs=[in_vmem] * 4 + [anywhere],
         out_shape=shape((members, TWO, BLK), f32),
         compiler_params=params(),
         name="owner_back",
-    )(s_part, c_part, d_base, before)
+    )(s_part, c_part, d_base, before, r_held)
     back_in = swap(back)
 
     part_shape = shape((8, tokens), f32)
@@ -329,10 +348,10 @@
         second_stage_kernel,
         in_specs=[in_vmem] * 5 + [in_smem],
         out_shape=[turned_f32, part_shape],
-        scratch_shapes=vmem(shape(twofold.shape[1:], bf16), mats(heads), scores),
+        scratch_shapes=vmem(shape(twofold.shape[1:], bf16), scores),
         compiler_params=params(LATE),
         name="second_stage",
-    )(query_rows, value_rows, r_local, back_in, out_gain.reshape(heads, 1, BLK), head_scale)
+    )(query_rows, value_rows, r_held, back_in, gain_columns, head_scale)
     shards = lax.axis_size("head")
     other = jnp.zeros_like(part)
     for turn in range(1, shards):

time: 67.1 us -> 65.2 us (0.972)
  waiting for transfers between devices: 3.42 us -> 1.2 us
  local copies, waits for them, and re-layouts: 2.2 us -> 0.03 us
  Pallas kernels: 18.3 us -> 20.4 us
    ppermute x1, waiting for transfers between devices: 2.23 us -> 0.01 us  [per_device(): before = lax.ppermute(passed, 'seq', onward)]
    pallas_call x1 -> x2, Pallas kernels: 0.47 us -> 2.69 us  [the longest x1 2.21 us: per_device(): pl.pallas_call(fetch_kernel, in_specs=[anywhere, in_vmem, anywhere], out_...]
    unnamed x10 -> x8, local copies, waits for them, and re-layouts: 2.2 us -> 0.03 us
  transfers between devices with their start and end apart: 2 -> 2, of which waited for: 2 -> 1; matrix products, arithmetic and copies ran while one was open for 0% -> 0% of each run, Pallas kernels for 0% -> 3%
where the time goes in v11:
time: 65.2 us; the launch traced here: 65 us
  blocking collectives  38.7 us (59%)
  Pallas kernels  20.4 us (31%)
  starting transfers between devices  4.58 us (7%)
  waiting for transfers between devices  1.2 us (2%)
    all_to_all x2, blocking collectives, swap(): return lax.all_to_all(a, 'seq', 0, 0, axis_index_groups=index_groups)  38.7 us
    pallas_call x1, Pallas kernels, per_device(): pl.pallas_call(first_stage_kernel, in_specs=[anywhere] * 3, out_specs=[an...  7.83 us
    pallas_call x1, Pallas kernels, per_device(): pl.pallas_call(second_stage_kernel, in_specs=[in_vmem] * 5 + [in_smem], o...  7.65 us
    ppermute x1, starting transfers between devices, per_device(): before = lax.ppermute(passed, 'seq', onward)  4.51 us
    pallas_call x1, Pallas kernels, per_device(): pl.pallas_call(fetch_kernel, in_specs=[anywhere, in_vmem, anywhere], out_...  2.21 us
    pallas_call x1, Pallas kernels, per_device(): pl.pallas_call(functools.partial(norm_kernel, width * shards), in_specs=[...  1.57 us
  transfers between devices with their start and end apart: 2, of which 1 were waited for; matrix products, arithmetic and copies ran while one was open for 0% of the time, Pallas kernels for 3%

profile of v11, /device:TPU:0, one launch (start us, length us, event | category | flops | bytes accessed | tf_op | source)
XLA Modules:
  0.0 65.0 jit_solution(10997198041861072716)
XLA Ops:
  0.0 7.8 %first_stage.1 = (bf16[4,2,1024,256]{3,2,1,0:T(8,128)(2,1)}, f32[4,2,328,128]{3,2,1,0:T(8,128)}) custom-call(bf16[1024,1024]{1,0:T(8,128)(2,1)} %q_ref.1, bf16[1024,1024]{1,0:T(8,128)(2,1)} %k_hbm.1, bf16[1024,1024]{1,0:T(8,128)(2,1)} %v_ref.1), custom_call_target="tpu_custom_call" | custom-call | tf_op jit(solution)/shard_map/first_stage/pallas_call | solution.py:303
  7.8 0.0 copy-start.2
  7.8 24.7 %all_to_all.10.moments_ref = f32[8,328,128]{2,1,0:T(8,128)S(1)} all-to-all(f32[8,328,128]{2,1,0:T(8,128)} %bitcast.3), channel_id=1, replica_groups={{0,2,4,6,8,10,12,14},{16,18,20,22,24,26,28,30},{1,3,5,7,9,11,13,15},{17..., dimensions={0} | all-to-all | bytes 2686976 | tf_op jit(solution)/shard_map/all_to_all | solution.py:283
  32.5 0.6 owner.1
  33.2 4.5 %collective-permute-start = (f32[200,128]{1,0:T(8,128)S(1)}, f32[200,128]{1,0:T(8,128)S(1)}, u32[]{:S(2)}, u32[]{:S(2)}) collective-permute-start(f32[200,128]{1,0:T(8,128)S(1)} %get-tuple-element.17.owned_hbm), channel_id=1, source_target_pairs={{0,16},{2,18},{4,20},{6,22},{8,24},{10,26},{12,28},{14,30},{1,17},... | collective-permute-start | bytes 307208 | tf_op jit(solution)/shard_map/ppermute | solution.py:336
  37.7 0.0 copy-done.2
  37.7 2.2 %fetch.1 = (bf16[4,2,1024,256]{3,2,1,0:T(8,128)(2,1)S(1)}, f32[8,128,128]{2,1,0:T(8,128)S(1)}) custom-call(bf16[4,2,1024,256]{3,2,1,0:T(8,128)(2,1)} %get-tuple-element.15.r_hbm, f32[8,1,128]{2,1,0:T(1,128)S(1)} %bitcast.2, f32[200,128]{1,0:T(8,128)S(1)} %get-tuple-element.17.owned_hbm), custom_call_target="tpu_custom_call" | custom-call | tf_op jit(solution)/shard_map/fetch/pallas_call | solution.py:321
  39.9 0.0 collective-permute-done.before_ref
  39.9 0.0 copy-start
  40.0 0.0 copy-start.1
  40.0 0.0 copy-start.3
  40.0 0.5 owner_back.1
  40.5 14.0 %all_to_all.11.back_ref = f32[8,200,128]{2,1,0:T(8,128)S(1)} all-to-all(f32[8,200,128]{2,1,0:T(8,128)S(1)} %owner_back.1), channel_id=1, replica_groups={{0,2,4,6,8,10,12,14},{16,18,20,22,24,26,28,30},{1,3,5,7,9,11,13,15},{17..., dimensions={0} | all-to-all | bytes 1638400 | tf_op jit(solution)/shard_map/all_to_all | solution.py:283
  54.5 0.0 copy-done
  54.5 0.0 copy-done.1
  54.5 0.0 copy-done.3
  54.5 7.7 %second_stage.1 = (f32[4,256,1024]{2,1,0:T(8,128)S(1)}, f32[8,1024]{1,0:T(8,128)S(1)}) custom-call(bf16[1024,1024]{1,0:T(8,128)(2,1)S(1)} %copy-done, bf16[1024,1024]{1,0:T(8,128)(2,1)S(1)} %copy-done.1, bf16[4,2,1024,256]{3,2,1,0:T(8,128)(2,1)S(1)} %get-tuple-element.18.held_hbm.r_ref, f32[8,200,128]{2,1,0:T(8,128)S(1)} %all_to_all.11.back_ref, ...), custom_call_target="tpu_custom_call" | custom-call | tf_op jit(solution)/shard_map/second_stage/pallas_call | solution.py:347
  62.1 0.1 collective-permute-start.1
  62.2 1.2 %collective-permute-done.1.other_ref = f32[8,1024]{1,0:T(8,128)S(1)} collective-permute-done((f32[8,1024]{1,0:T(8,128)S(1)}, f32[8,1024]{1,0:T(8,128)S(1)}, u32[]{:S(2)}, u32[]{:S(2)}) %collective-permute-start.1) | collective-permute-done | bytes 32800 | tf_op jit(solution)/shard_map/ppermute | solution.py:358
  63.4 1.6 %norm.1 = bf16[1024,1024]{1,0:T(8,128)(2,1)} custom-call(f32[4,256,1024]{2,1,0:T(8,128)S(1)} %get-tuple-element.23.y_ref, f32[8,1024]{1,0:T(8,128)S(1)} %get-tuple-element.24.mine_ref, f32[8,1024]{1,0:T(8,128)S(1)} %collective-permute-done.1.other_ref), custom_call_target="tpu_custom_call" | custom-call | tf_op jit(solution)/shard_map/norm/pallas_call | solution.py:359
Async XLA Ops:
  7.8 29.9 %copy-start.2 = (f32[1024]{0:T(1024)S(1)}, f32[1024]{0:T(1024)}, u32[]{:S(2)}) copy-start(f32[1024]{0:T(1024)} %param.9) | copy-start | bytes 12292
  33.2 6.7 %collective-permute-start = (f32[200,128]{1,0:T(8,128)S(1)}, f32[200,128]{1,0:T(8,128)S(1)}, u32[]{:S(2)}, u32[]{:S(2)}) collective-permute-start(f32[200,128]{1,0:T(8,128)S(1)} %get-tuple-element.17.owned_hbm), channel_id=1, source_target_pairs={{0,16},{2,18},{4,20},{6,22},{8,24},{10,26},{12,28},{14,30},{1,17},... | collective-permute-start | bytes 307208 | tf_op jit(solution)/shard_map/ppermute | solution.py:336
  39.9 14.5 %copy-start = (bf16[1024,1024]{1,0:T(8,128)(2,1)S(1)}, bf16[1024,1024]{1,0:T(8,128)(2,1)}, u32[]{:S(2)}) copy-start(bf16[1024,1024]{1,0:T(8,128)(2,1)} %q_ref.1) | copy-start | bytes 6291460
  40.0 14.5 %copy-start.1 = (bf16[1024,1024]{1,0:T(8,128)(2,1)S(1)}, bf16[1024,1024]{1,0:T(8,128)(2,1)}, u32[]{:S(2)}) copy-start(bf16[1024,1024]{1,0:T(8,128)(2,1)} %v_ref.1) | copy-start | bytes 6291460
  40.0 14.5 %copy-start.3 = (f32[8]{0:T(128)S(1)}, f32[8]{0:T(128)}, u32[]{:S(2)}) copy-start(f32[8]{0:T(128)} %scale_ref.1) | copy-start | bytes 100
  62.1 1.3 %collective-permute-start.1 = (f32[8,1024]{1,0:T(8,128)S(1)}, f32[8,1024]{1,0:T(8,128)S(1)}, u32[]{:S(2)}, u32[]{:S(2)}) collective-permute-start(f32[8,1024]{1,0:T(8,128)S(1)} %get-tuple-element.24.mine_ref), channel_id=1, source_target_pairs={{0,1},{1,0},{2,3},{3,2},{4,5},{5,4},{6,7},{7,6},{8,9},{9,8},{10,11... | collective-permute-start | bytes 98312 | tf_op jit(solution)/shard_map/ppermute | solution.py:358

commit v12 on v11

--- a/solution.py
+++ b/solution.py
@@ -188,30 +188,30 @@
     mask = ordered(CHUNK) <= 0
     part_ref[...] = jnp.zeros_like(part_ref)
 
-    @pl.loop(0, pairs)
-    def _(p):
+    for p in range(pairs):
+        turn = p % 2
         backs = [back_ref[p * PAIR + j] for j in range(PAIR)]
         s_both = [rows(*split(unpack(back[:PACKED]))) for back in backs]
-        heads = [pl.ds(pl.multiple_of((p * PAIR + j) * BLK, BLK), BLK) for j in range(PAIR)]
+        heads = [span(p * PAIR + j) for j in range(PAIR)]
         for j in range(PAIR):
             for i in range(steps):
                 at = span(i, CHUNK)
                 q = q_ref[at, heads[j]]
                 r = halves_sum(r_ref[p, j, at].astype(f32)) + dot(lanes(q, q), s_both[j])
-                rr_ref[j, at] = lanes(*split(r))
+                rr_ref[turn, j, at] = lanes(*split(r))
         for i, j, at, cols in units:
             qt = q_ref[at, heads[j]].T
-            a = dot(rr_ref[j, at], rows(qt, qt))
-            a_ref[j, i] = rows(*split(jnp.where(mask, a, 0.0)))
+            a = dot(rr_ref[turn, j, at], rows(qt, qt))
+            a_ref[turn, j, i] = rows(*split(jnp.where(mask, a, 0.0)))
         sums = [[] for _ in range(PAIR)]
         for i, j, at, cols in units:
             if i + 1 < steps:
-                sums[j].append(halves_sum(dot(v_ref[at, heads[j]].T, rr_ref[j, at])))
+                sums[j].append(halves_sum(dot(v_ref[at, heads[j]].T, rr_ref[turn, j, at])))
         states = [running(sums[j], backs[j][PACKED:]) for j in range(PAIR)]
         for i, j, at, cols in units:
             h = p * PAIR + j
             vt, qt = v_ref[at, heads[j]].T, q_ref[at, heads[j]].T
-            num = dot(lanes(vt, vt), a_ref[j, i]) + dot(lanes(*split(states[j][i])), rows(qt, qt))
+            num = dot(lanes(vt, vt), a_ref[turn, j, i]) + dot(lanes(*split(states[j][i])), rows(qt, qt))
             y = num * scale_ref[h]
             part_ref[:, at] += jnp.sum((y * y).reshape(BLK // 8, 8, CHUNK), axis=0)
             y_ref[p, cols, at] = y * lanes(*[gains_ref[h]] * (CHUNK // BLK))
@@ -348,7 +348,7 @@
         second_stage_kernel,
         in_specs=[in_vmem] * 5 + [in_smem],
         out_shape=[turned_f32, part_shape],
-        scratch_shapes=vmem(shape(twofold.shape[1:], bf16), scores),
+        scratch_shapes=vmem(shape((2,) + twofold.shape[1:], bf16), shape((2,) + scores.shape, bf16)),
         compiler_params=params(LATE),
         name="second_stage",
     )(query_rows, value_rows, r_held, back_in, gain_columns, head_scale)

time: 65.2 us -> 64 us (0.982)
  Pallas kernels: 20.4 us -> 19.2 us
    pallas_call x1, Pallas kernels: 7.65 us -> 6.42 us  [per_device(): pl.pallas_call(second_stage_kernel, in_specs=[in_vmem] * 5 + [in_smem], o...]
where the time goes in v12:
time: 64 us; the launch traced here: 63.8 us
  blocking collectives  38.7 us (60%)
  Pallas kernels  19.2 us (30%)
  starting transfers between devices  4.58 us (7%)
  waiting for transfers between devices  1.2 us (2%)
    all_to_all x2, blocking collectives, swap(): return lax.all_to_all(a, 'seq', 0, 0, axis_index_groups=index_groups)  38.7 us
    pallas_call x1, Pallas kernels, per_device(): pl.pallas_call(first_stage_kernel, in_specs=[anywhere] * 3, out_specs=[an...  7.83 us
    pallas_call x1, Pallas kernels, per_device(): pl.pallas_call(second_stage_kernel, in_specs=[in_vmem] * 5 + [in_smem], o...  6.42 us
    ppermute x1, starting transfers between devices, per_device(): before = lax.ppermute(passed, 'seq', onward)  4.51 us
    pallas_call x1, Pallas kernels, per_device(): pl.pallas_call(fetch_kernel, in_specs=[anywhere, in_vmem, anywhere], out_...  2.21 us
    pallas_call x1, Pallas kernels, per_device(): pl.pallas_call(functools.partial(norm_kernel, width * shards), in_specs=[...  1.57 us
  transfers between devices with their start and end apart: 2, of which 1 were waited for; matrix products, arithmetic and copies ran while one was open for 0% of the time, Pallas kernels for 3%

profile of v12, /device:TPU:0, one launch (start us, length us, event | category | flops | bytes accessed | tf_op | source)
XLA Modules:
  0.0 63.8 jit_solution(4587831855444199434)
XLA Ops:
  0.0 7.8 %first_stage.1 = (bf16[4,2,1024,256]{3,2,1,0:T(8,128)(2,1)}, f32[4,2,328,128]{3,2,1,0:T(8,128)}) custom-call(bf16[1024,1024]{1,0:T(8,128)(2,1)} %q_ref.1, bf16[1024,1024]{1,0:T(8,128)(2,1)} %k_hbm.1, bf16[1024,1024]{1,0:T(8,128)(2,1)} %v_ref.1), custom_call_target="tpu_custom_call" | custom-call | tf_op jit(solution)/shard_map/first_stage/pallas_call | solution.py:303
  7.8 0.0 copy-start.2
  7.8 24.7 %all_to_all.10.moments_ref = f32[8,328,128]{2,1,0:T(8,128)S(1)} all-to-all(f32[8,328,128]{2,1,0:T(8,128)} %bitcast.3), channel_id=1, replica_groups={{0,2,4,6,8,10,12,14},{16,18,20,22,24,26,28,30},{1,3,5,7,9,11,13,15},{17..., dimensions={0} | all-to-all | bytes 2686976 | tf_op jit(solution)/shard_map/all_to_all | solution.py:283
  32.5 0.6 %owner.1 = (f32[8,72,128]{2,1,0:T(8,128)S(1)}, f32[9,128,128]{2,1,0:T(8,128)S(1)}, f32[8,128,128]{2,1,0:T(8,128)S(1)}, f32[200,128]{1,0:T(8,128)S(1)}) custom-call(f32[8,328,128]{2,1,0:T(8,128)S(1)} %all_to_all.10.moments_ref), custom_call_target="tpu_custom_call" | custom-call | tf_op jit(solution)/shard_map/owner/pallas_call | solution.py:315
  33.2 4.5 %collective-permute-start = (f32[200,128]{1,0:T(8,128)S(1)}, f32[200,128]{1,0:T(8,128)S(1)}, u32[]{:S(2)}, u32[]{:S(2)}) collective-permute-start(f32[200,128]{1,0:T(8,128)S(1)} %get-tuple-element.17.owned_hbm), channel_id=1, source_target_pairs={{0,16},{2,18},{4,20},{6,22},{8,24},{10,26},{12,28},{14,30},{1,17},... | collective-permute-start | bytes 307208 | tf_op jit(solution)/shard_map/ppermute | solution.py:336
  37.7 0.0 copy-done.2
  37.7 2.2 %fetch.1 = (bf16[4,2,1024,256]{3,2,1,0:T(8,128)(2,1)S(1)}, f32[8,128,128]{2,1,0:T(8,128)S(1)}) custom-call(bf16[4,2,1024,256]{3,2,1,0:T(8,128)(2,1)} %get-tuple-element.15.r_hbm, f32[8,1,128]{2,1,0:T(1,128)S(1)} %bitcast.2, f32[200,128]{1,0:T(8,128)S(1)} %get-tuple-element.17.owned_hbm), custom_call_target="tpu_custom_call" | custom-call | tf_op jit(solution)/shard_map/fetch/pallas_call | solution.py:321
  39.9 0.0 collective-permute-done.before_ref
  39.9 0.0 copy-start
  40.0 0.0 copy-start.1
  40.0 0.0 copy-start.3
  40.0 0.5 owner_back.1
  40.5 14.0 %all_to_all.11.back_ref = f32[8,200,128]{2,1,0:T(8,128)S(1)} all-to-all(f32[8,200,128]{2,1,0:T(8,128)S(1)} %owner_back.1), channel_id=1, replica_groups={{0,2,4,6,8,10,12,14},{16,18,20,22,24,26,28,30},{1,3,5,7,9,11,13,15},{17..., dimensions={0} | all-to-all | bytes 1638400 | tf_op jit(solution)/shard_map/all_to_all | solution.py:283
  54.5 0.0 copy-done
  54.5 0.0 copy-done.1
  54.5 0.0 copy-done.3
  54.5 6.4 %second_stage.1 = (f32[4,256,1024]{2,1,0:T(8,128)S(1)}, f32[8,1024]{1,0:T(8,128)S(1)}) custom-call(bf16[1024,1024]{1,0:T(8,128)(2,1)S(1)} %copy-done, bf16[1024,1024]{1,0:T(8,128)(2,1)S(1)} %copy-done.1, bf16[4,2,1024,256]{3,2,1,0:T(8,128)(2,1)S(1)} %get-tuple-element.18.held_hbm.r_ref, f32[8,200,128]{2,1,0:T(8,128)S(1)} %all_to_all.11.back_ref, ...), custom_call_target="tpu_custom_call" | custom-call | tf_op jit(solution)/shard_map/second_stage/pallas_call | solution.py:347
  60.9 0.1 collective-permute-start.1
  61.0 1.2 %collective-permute-done.1.other_ref = f32[8,1024]{1,0:T(8,128)S(1)} collective-permute-done((f32[8,1024]{1,0:T(8,128)S(1)}, f32[8,1024]{1,0:T(8,128)S(1)}, u32[]{:S(2)}, u32[]{:S(2)}) %collective-permute-start.1) | collective-permute-done | bytes 32800 | tf_op jit(solution)/shard_map/ppermute | solution.py:358
  62.2 1.6 %norm.1 = bf16[1024,1024]{1,0:T(8,128)(2,1)} custom-call(f32[4,256,1024]{2,1,0:T(8,128)S(1)} %get-tuple-element.23.y_ref, f32[8,1024]{1,0:T(8,128)S(1)} %get-tuple-element.24.mine_ref, f32[8,1024]{1,0:T(8,128)S(1)} %collective-permute-done.1.other_ref), custom_call_target="tpu_custom_call" | custom-call | tf_op jit(solution)/shard_map/norm/pallas_call | solution.py:359
Async XLA Ops:
  7.8 29.9 %copy-start.2 = (f32[1024]{0:T(1024)S(1)}, f32[1024]{0:T(1024)}, u32[]{:S(2)}) copy-start(f32[1024]{0:T(1024)} %param.9) | copy-start | bytes 12292
  33.2 6.7 %collective-permute-start = (f32[200,128]{1,0:T(8,128)S(1)}, f32[200,128]{1,0:T(8,128)S(1)}, u32[]{:S(2)}, u32[]{:S(2)}) collective-permute-start(f32[200,128]{1,0:T(8,128)S(1)} %get-tuple-element.17.owned_hbm), channel_id=1, source_target_pairs={{0,16},{2,18},{4,20},{6,22},{8,24},{10,26},{12,28},{14,30},{1,17},... | collective-permute-start | bytes 307208 | tf_op jit(solution)/shard_map/ppermute | solution.py:336
  39.9 14.5 %copy-start = (bf16[1024,1024]{1,0:T(8,128)(2,1)S(1)}, bf16[1024,1024]{1,0:T(8,128)(2,1)}, u32[]{:S(2)}) copy-start(bf16[1024,1024]{1,0:T(8,128)(2,1)} %q_ref.1) | copy-start | bytes 6291460
  40.0 14.5 %copy-start.1 = (bf16[1024,1024]{1,0:T(8,128)(2,1)S(1)}, bf16[1024,1024]{1,0:T(8,128)(2,1)}, u32[]{:S(2)}) copy-start(bf16[1024,1024]{1,0:T(8,128)(2,1)} %v_ref.1) | copy-start | bytes 6291460
  40.0 14.5 %copy-start.3 = (f32[8]{0:T(128)S(1)}, f32[8]{0:T(128)}, u32[]{:S(2)}) copy-start(f32[8]{0:T(128)} %scale_ref.1) | copy-start | bytes 100
  60.9 1.3 %collective-permute-start.1 = (f32[8,1024]{1,0:T(8,128)S(1)}, f32[8,1024]{1,0:T(8,128)S(1)}, u32[]{:S(2)}, u32[]{:S(2)}) collective-permute-start(f32[8,1024]{1,0:T(8,128)S(1)} %get-tuple-element.24.mine_ref), channel_id=1, source_target_pairs={{0,1},{1,0},{2,3},{3,2},{4,5},{5,4},{6,7},{7,6},{8,9},{9,8},{10,11... | collective-permute-start | bytes 98312 | tf_op jit(solution)/shard_map/ppermute | solution.py:358

commit v13 on v12

--- a/solution.py
+++ b/solution.py
@@ -139,12 +139,12 @@
     writes = [(by_pair(m_ref), by_pair(m_hbm)), (by_pair(r_ref), by_pair(r_hbm))]
     start(reads, read_sems, 0, pairs)
 
-    @pl.loop(0, pairs)
-    def _(p):
+    for p in range(pairs):
+        turn = p % 2
         wait(reads, read_sems, p)
         for i, j, at, cols in units:
             a = dot(k_ref[p, at, cols], q_ref[p, at, cols].T)
-            a_ref[j, i] = rows(*split(jnp.where(mask, a, 0.0)))
+            a_ref[turn, j, i] = rows(*split(jnp.where(mask, a, 0.0)))
         states = []
         for j in range(PAIR):
             blocks = [k_ref[p, span(i, CHUNK), span(j)] for i in range(steps)]
@@ -152,7 +152,7 @@
             m_ref[p, j, :PACKED] = pack(states[j][steps])
         for i, j, at, cols in units:
             kt = k_ref[p, at, cols].T
-            r = dot(lanes(kt, kt), a_ref[j, i])
+            r = dot(lanes(kt, kt), a_ref[turn, j, i])
             if i > 0:
                 qt = q_ref[p, at, cols].T
                 r = r + dot(lanes(*split(states[j][i])), rows(qt, qt))
@@ -305,7 +305,7 @@
         in_specs=[anywhere] * 3,
         out_specs=[anywhere] * 2,
         out_shape=[twofold, moment_mats],
-        scratch_shapes=vmem(upright, upright, upright, twofold, moment_mats, scores) + sems(3, 2),
+        scratch_shapes=vmem(upright, upright, upright, twofold, moment_mats, shape((2,) + scores.shape, bf16)) + sems(3, 2),
         compiler_params=params(LARGE),
         name="first_stage",
     )(query_rows, key_rows, value_rows)

time: 64 us -> 64.1 us (level)
  no operation moved by 1% of the time
where the time goes in v13:
time: 64.1 us; the launch traced here: 63.9 us
  blocking collectives  38.7 us (60%)
  Pallas kernels  19.1 us (30%)
  starting transfers between devices  4.56 us (7%)
  waiting for transfers between devices  1.2 us (2%)
    all_to_all x2, blocking collectives, swap(): return lax.all_to_all(a, 'seq', 0, 0, axis_index_groups=index_groups)  38.7 us
    pallas_call x1, Pallas kernels, per_device(): pl.pallas_call(first_stage_kernel, in_specs=[anywhere] * 3, out_specs=[an...  7.81 us
    pallas_call x1, Pallas kernels, per_device(): pl.pallas_call(second_stage_kernel, in_specs=[in_vmem] * 5 + [in_smem], o...  6.42 us
    ppermute x1, starting transfers between devices, per_device(): before = lax.ppermute(passed, 'seq', onward)  4.48 us
    pallas_call x1, Pallas kernels, per_device(): pl.pallas_call(fetch_kernel, in_specs=[anywhere, in_vmem, anywhere], out_...  2.21 us
    pallas_call x1, Pallas kernels, per_device(): pl.pallas_call(functools.partial(norm_kernel, width * shards), in_specs=[...  1.57 us
  transfers between devices with their start and end apart: 2, of which 1 were waited for; matrix products, arithmetic and copies ran while one was open for 0% of the time, Pallas kernels for 3%

profile of v13, /device:TPU:0, one launch (start us, length us, event | category | flops | bytes accessed | tf_op | source)
XLA Modules:
  0.0 63.9 jit_solution(17323403453316463415)
XLA Ops:
  0.0 7.8 %first_stage.1 = (bf16[4,2,1024,256]{3,2,1,0:T(8,128)(2,1)}, f32[4,2,328,128]{3,2,1,0:T(8,128)}) custom-call(bf16[1024,1024]{1,0:T(8,128)(2,1)} %q_ref.1, bf16[1024,1024]{1,0:T(8,128)(2,1)} %k_hbm.1, bf16[1024,1024]{1,0:T(8,128)(2,1)} %v_ref.1), custom_call_target="tpu_custom_call" | custom-call | tf_op jit(solution)/shard_map/first_stage/pallas_call | solution.py:303
  7.8 0.0 copy-start.2
  7.8 24.7 %all_to_all.10.moments_ref = f32[8,328,128]{2,1,0:T(8,128)S(1)} all-to-all(f32[8,328,128]{2,1,0:T(8,128)} %bitcast.3), channel_id=1, replica_groups={{0,2,4,6,8,10,12,14},{16,18,20,22,24,26,28,30},{1,3,5,7,9,11,13,15},{17..., dimensions={0} | all-to-all | bytes 2686976 | tf_op jit(solution)/shard_map/all_to_all | solution.py:283
  32.6 0.6 %owner.1 = (f32[8,72,128]{2,1,0:T(8,128)S(1)}, f32[9,128,128]{2,1,0:T(8,128)S(1)}, f32[8,128,128]{2,1,0:T(8,128)S(1)}, f32[200,128]{1,0:T(8,128)S(1)}) custom-call(f32[8,328,128]{2,1,0:T(8,128)S(1)} %all_to_all.10.moments_ref), custom_call_target="tpu_custom_call" | custom-call | tf_op jit(solution)/shard_map/owner/pallas_call | solution.py:315
  33.2 4.5 %collective-permute-start = (f32[200,128]{1,0:T(8,128)S(1)}, f32[200,128]{1,0:T(8,128)S(1)}, u32[]{:S(2)}, u32[]{:S(2)}) collective-permute-start(f32[200,128]{1,0:T(8,128)S(1)} %get-tuple-element.17.owned_hbm), channel_id=1, source_target_pairs={{0,16},{2,18},{4,20},{6,22},{8,24},{10,26},{12,28},{14,30},{1,17},... | collective-permute-start | bytes 307208 | tf_op jit(solution)/shard_map/ppermute | solution.py:336
  37.7 0.0 copy-done.2
  37.7 2.2 %fetch.1 = (bf16[4,2,1024,256]{3,2,1,0:T(8,128)(2,1)S(1)}, f32[8,128,128]{2,1,0:T(8,128)S(1)}) custom-call(bf16[4,2,1024,256]{3,2,1,0:T(8,128)(2,1)} %get-tuple-element.15.r_hbm, f32[8,1,128]{2,1,0:T(1,128)S(1)} %bitcast.2, f32[200,128]{1,0:T(8,128)S(1)} %get-tuple-element.17.owned_hbm), custom_call_target="tpu_custom_call" | custom-call | tf_op jit(solution)/shard_map/fetch/pallas_call | solution.py:321
  39.9 0.0 collective-permute-done.before_ref
  39.9 0.0 copy-start
  39.9 0.0 copy-start.1
  40.0 0.0 copy-start.3
  40.0 0.5 owner_back.1
  40.5 14.0 %all_to_all.11.back_ref = f32[8,200,128]{2,1,0:T(8,128)S(1)} all-to-all(f32[8,200,128]{2,1,0:T(8,128)S(1)} %owner_back.1), channel_id=1, replica_groups={{0,2,4,6,8,10,12,14},{16,18,20,22,24,26,28,30},{1,3,5,7,9,11,13,15},{17..., dimensions={0} | all-to-all | bytes 1638400 | tf_op jit(solution)/shard_map/all_to_all | solution.py:283
  54.5 0.0 copy-done
  54.5 0.0 copy-done.1
  54.5 0.0 copy-done.3
  54.5 6.4 %second_stage.1 = (f32[4,256,1024]{2,1,0:T(8,128)S(1)}, f32[8,1024]{1,0:T(8,128)S(1)}) custom-call(bf16[1024,1024]{1,0:T(8,128)(2,1)S(1)} %copy-done, bf16[1024,1024]{1,0:T(8,128)(2,1)S(1)} %copy-done.1, bf16[4,2,1024,256]{3,2,1,0:T(8,128)(2,1)S(1)} %get-tuple-element.18.held_hbm.r_ref, f32[8,200,128]{2,1,0:T(8,128)S(1)} %all_to_all.11.back_ref, ...), custom_call_target="tpu_custom_call" | custom-call | tf_op jit(solution)/shard_map/second_stage/pallas_call | solution.py:347
  60.9 0.1 collective-permute-start.1
  61.0 1.2 %collective-permute-done.1.other_ref = f32[8,1024]{1,0:T(8,128)S(1)} collective-permute-done((f32[8,1024]{1,0:T(8,128)S(1)}, f32[8,1024]{1,0:T(8,128)S(1)}, u32[]{:S(2)}, u32[]{:S(2)}) %collective-permute-start.1) | collective-permute-done | bytes 32800 | tf_op jit(solution)/shard_map/ppermute | solution.py:358
  62.2 1.6 %norm.1 = bf16[1024,1024]{1,0:T(8,128)(2,1)} custom-call(f32[4,256,1024]{2,1,0:T(8,128)S(1)} %get-tuple-element.23.y_ref, f32[8,1024]{1,0:T(8,128)S(1)} %get-tuple-element.24.mine_ref, f32[8,1024]{1,0:T(8,128)S(1)} %collective-permute-done.1.other_ref), custom_call_target="tpu_custom_call" | custom-call | tf_op jit(solution)/shard_map/norm/pallas_call | solution.py:359
Async XLA Ops:
  7.8 29.9 %copy-start.2 = (f32[1024]{0:T(1024)S(1)}, f32[1024]{0:T(1024)}, u32[]{:S(2)}) copy-start(f32[1024]{0:T(1024)} %param.9) | copy-start | bytes 12292
  33.2 6.7 %collective-permute-start = (f32[200,128]{1,0:T(8,128)S(1)}, f32[200,128]{1,0:T(8,128)S(1)}, u32[]{:S(2)}, u32[]{:S(2)}) collective-permute-start(f32[200,128]{1,0:T(8,128)S(1)} %get-tuple-element.17.owned_hbm), channel_id=1, source_target_pairs={{0,16},{2,18},{4,20},{6,22},{8,24},{10,26},{12,28},{14,30},{1,17},... | collective-permute-start | bytes 307208 | tf_op jit(solution)/shard_map/ppermute | solution.py:336
  39.9 14.5 %copy-start = (bf16[1024,1024]{1,0:T(8,128)(2,1)S(1)}, bf16[1024,1024]{1,0:T(8,128)(2,1)}, u32[]{:S(2)}) copy-start(bf16[1024,1024]{1,0:T(8,128)(2,1)} %q_ref.1) | copy-start | bytes 6291460
  39.9 14.5 %copy-start.1 = (bf16[1024,1024]{1,0:T(8,128)(2,1)S(1)}, bf16[1024,1024]{1,0:T(8,128)(2,1)}, u32[]{:S(2)}) copy-start(bf16[1024,1024]{1,0:T(8,128)(2,1)} %v_ref.1) | copy-start | bytes 6291460
  40.0 14.5 %copy-start.3 = (f32[8]{0:T(128)S(1)}, f32[8]{0:T(128)}, u32[]{:S(2)}) copy-start(f32[8]{0:T(128)} %scale_ref.1) | copy-start | bytes 100
  60.9 1.3 %collective-permute-start.1 = (f32[8,1024]{1,0:T(8,128)S(1)}, f32[8,1024]{1,0:T(8,128)S(1)}, u32[]{:S(2)}, u32[]{:S(2)}) collective-permute-start(f32[8,1024]{1,0:T(8,128)S(1)} %get-tuple-element.24.mine_ref), channel_id=1, source_target_pairs={{0,1},{1,0},{2,3},{3,2},{4,5},{5,4},{6,7},{7,6},{8,9},{9,8},{10,11... | collective-permute-start | bytes 98312 | tf_op jit(solution)/shard_map/ppermute | solution.py:358
